TPU v7x, 32 devices: a whole 2x2x4 slice. The times are simulated.
32 devices in a mesh: fsdp: 32 (over z, y, x, core).
Axes of the slice: x: 2, y: 2, z: 4, core: 2. Of those that a mesh axis runs over, the one named last changes fastest.
Arguments:
- tokens: bfloat16 [64, 64, 768], P('fsdp'), may hold values from -6 to 6
- segments: int32 [64, 64], P('fsdp'), may hold values from -1 to 3, as said below
- norm_gain: bfloat16 [2, 768], P(None, 'fsdp'), may hold values from 0.5 to 1.5
- in_weight: bfloat16 [2, 768, 3352], P(None, 'fsdp'), may hold values from -0.21875 to 0.21875
- conv_weight: bfloat16 [2, 4, 1792], P(None, None, 'fsdp'), may hold values from -3 to 3
- conv_bias: bfloat16 [2, 1792], P(None, 'fsdp'), may hold values from -3 to 3
- log_decay: float32 [2, 24], replicated, may hold values from 0 to 2.77
- skip_gain: float32 [2, 24], replicated, may hold values from 0.5 to 2
- step_bias: float32 [2, 24], replicated, may hold values from -6 to -1
- gate_gain: bfloat16 [2, 1536], P(None, 'fsdp'), may hold values from 0.5 to 1.5
- out_weight: bfloat16 [2, 1536, 768], P(None, 'fsdp'), may hold values from -0.15625 to 0.15625
- cotangent: bfloat16 [64, 64, 768], P('fsdp'), may hold values from -6 to 6
Outputs:
- mixed: bfloat16 [64, 64, 768], P('fsdp')
- token_grad: float32 [64, 64, 768], P('fsdp')
- norm_gain_grad: float32 [2, 768], P(None, 'fsdp')
- in_weight_grad: float32 [2, 768, 3352], P(None, 'fsdp')
- conv_weight_grad: float32 [2, 4, 1792], P(None, None, 'fsdp')
- conv_bias_grad: float32 [2, 1792], P(None, 'fsdp')
- log_decay_grad: float32 [2, 24], replicated
- skip_gain_grad: float32 [2, 24], replicated
- step_bias_grad: float32 [2, 24], replicated
- gate_gain_grad: float32 [2, 1536], P(None, 'fsdp')
- out_weight_grad: float32 [2, 1536, 768], P(None, 'fsdp')
Inputs may be any that keep to these rules, and one draw needn't show every extreme that they name: `segments`: in each block the segment numbers start at 0 at the first position and never fall over the live positions; the positions after a block's live positions hold -1; each block has at least one live position.
All inputs are finite; a program needn't handle non-finite values.
Results may differ from a plain program's by a relative error of at most 0.012.
Values may be sent and summed in bfloat16 or wider, within the bound.
No kernel may reach another device: no remote copies, remote signals or barrier semaphores. Data moves between devices by JAX's collectives and lax.ppermute only.
A program may use at most 192 MiB of HBM per device.

v0:
```python
from functools import partial

import jax
import jax.numpy as jnp
from jax import lax
from jax.sharding import PartitionSpec as P

HEADS = 24
HEADDIM = 64
STATE = 128
CONV = 4


EPSILON = 1e-05
EXACT = lax.Precision.HIGHEST
ROWS_DIMS = (((0,), (0,)), ((), ()))
COLS_DIMS = (((1,), (1,)), ((), ()))


def rms_norm(values, gain):
    return values * lax.rsqrt(jnp.mean(values * values, axis=-1, keepdims=True) + EPSILON) * gain


def segment_mixer(
    segment_ids, hidden, conv_weight, conv_bias, log_decay, skip_gain, step_bias, gate_gain
):
    length = hidden.shape[0]
    inner = HEADS * HEADDIM
    gate_part = hidden[:, :inner]
    signal = hidden[:, inner : 2 * inner + 2 * STATE]
    step_raw = hidden[:, 2 * inner + 2 * STATE :]
    mixed_conv = conv_bias + signal * conv_weight[CONV - 1]
    for offset in range(1, CONV):
        shifted = jnp.pad(signal, ((offset, 0), (0, 0)))[:length]
        earlier = jnp.pad(segment_ids, (offset, 0), constant_values=-2)[:length]
        mixed_conv = (
            mixed_conv
            + jnp.where((earlier == segment_ids)[:, None], shifted, 0.0)
            * conv_weight[CONV - 1 - offset]
        )
    mixed_conv = jax.nn.silu(mixed_conv)
    values = mixed_conv[:, :inner].reshape(length, HEADS, HEADDIM)
    inputs_b = mixed_conv[:, inner : inner + STATE]
    outputs_c = mixed_conv[:, inner + STATE :]
    step_size = jax.nn.softplus(step_raw + step_bias)
    rates = step_size * -jnp.exp(log_decay)
    totals = jnp.cumsum(rates, axis=0).T
    position = jnp.arange(length)
    allowed = (position[:, None] >= position[None, :]) & (
        segment_ids[:, None] == segment_ids[None, :]
    )
    gaps = jnp.where(allowed[None], totals[:, :, None] - totals[:, None, :], 0.0)
    decays = jnp.where(allowed[None], jnp.exp(gaps), 0.0)
    scores = jnp.dot(outputs_c, inputs_b.T, precision=EXACT)
    weights = scores[None] * decays
    scaled = values * step_size[:, :, None]
    states = jnp.einsum("hts,shp->thp", weights, scaled, precision=EXACT)
    states = states + values * skip_gain[None, :, None]
    gated = states.reshape(length, inner) * jax.nn.silu(gate_part)
    return rms_norm(gated, gate_gain)


def body(
    tokens,
    segments,
    norm_gain,
    in_weight,
    conv_weight,
    conv_bias,
    log_decay,
    skip_gain,
    step_bias,
    gate_gain,
    out_weight,
    cotangent,
):
    layers = in_weight.shape[0]
    conv_turned = jnp.transpose(conv_weight, (0, 2, 1))
    shards = (norm_gain, in_weight, conv_turned, conv_bias, gate_gain, out_weight)
    mixed_blocks = []
    token_grads = []
    kept_rows = [[] for layer_index in range(layers)]
    small_sums = None
    for batch in range(tokens.shape[0]):
        forward_set = (
            lax.all_gather(shards[0], "fsdp", axis=1, tiled=True),
            lax.all_gather(shards[1], "fsdp", axis=1, tiled=True),
            lax.all_gather(shards[2], "fsdp", axis=1, tiled=True),
            lax.all_gather(shards[3], "fsdp", axis=1, tiled=True),
            lax.all_gather(shards[4], "fsdp", axis=1, tiled=True),
            lax.all_gather(shards[5], "fsdp", axis=1, tiled=True),
        )
        segment_ids = segments[batch]
        resid = tokens[batch].astype(jnp.float32)
        saved = []
        for layer_index in range(layers):
            norm_full = forward_set[0][layer_index].astype(jnp.float32)
            in_full = forward_set[1][layer_index]
            conv_full = forward_set[2][layer_index].astype(jnp.float32).T
            bias_full = forward_set[3][layer_index].astype(jnp.float32)
            gain_full = forward_set[4][layer_index].astype(jnp.float32)
            out_full = forward_set[5][layer_index]
            normed, pull_norm = jax.vjp(rms_norm, resid, norm_full)
            normed_low = normed.astype(jnp.bfloat16)
            hidden = jnp.dot(normed_low, in_full, preferred_element_type=jnp.float32)
            gated, pull_mix = jax.vjp(
                partial(segment_mixer, segment_ids),
                hidden,
                conv_full,
                bias_full,
                log_decay[layer_index],
                skip_gain[layer_index],
                step_bias[layer_index],
                gain_full,
            )
            gated_low = gated.astype(jnp.bfloat16)
            resid = resid + jnp.dot(gated_low, out_full, preferred_element_type=jnp.float32)
            saved.append((pull_norm, normed_low, pull_mix, gated_low))
        valid = (segment_ids >= 0).astype(jnp.float32)[:, None]
        mixed_blocks.append((resid * valid).astype(jnp.bfloat16))
        grad = cotangent[batch].astype(jnp.float32) * valid
        layer_small = [None] * layers
        for layer_index in reversed(range(layers)):
            pull_norm, normed_low, pull_mix, gated_low = saved[layer_index]
            in_full = forward_set[1][layer_index]
            out_full = forward_set[5][layer_index]
            grad_low = grad.astype(jnp.bfloat16)
            gated_grad = lax.dot_general(
                grad_low, out_full, COLS_DIMS, preferred_element_type=jnp.float32
            )
            hidden_grad, conv_grad, bias_grad, decay_grad, skip_grad, step_grad, gain_grad = (
                pull_mix(gated_grad)
            )
            hidden_low = hidden_grad.astype(jnp.bfloat16)
            normed_grad = lax.dot_general(
                hidden_low, in_full, COLS_DIMS, preferred_element_type=jnp.float32
            )
            resid_grad, norm_grad = pull_norm(normed_grad)
            grad = grad + resid_grad
            kept_rows[layer_index].append((normed_low, hidden_low, gated_low, grad_low))
            layer_small[layer_index] = (
                norm_grad,
                conv_grad.T,
                bias_grad,
                gain_grad,
                decay_grad,
                skip_grad,
                step_grad,
            )
        token_grads.append(grad)
        stacked = tuple(
            (jnp.stack([entry[member] for entry in layer_small]) for member in range(7))
        )
        if small_sums is None:
            small_sums = stacked
        else:
            small_sums = tuple((first + second for first, second in zip(small_sums, stacked)))
    in_sums = []
    out_sums = []
    for layer_index in range(layers):
        normed_all = jnp.concatenate([entry[0] for entry in kept_rows[layer_index]], axis=0)
        hidden_all = jnp.concatenate([entry[1] for entry in kept_rows[layer_index]], axis=0)
        gated_all = jnp.concatenate([entry[2] for entry in kept_rows[layer_index]], axis=0)
        grad_all = jnp.concatenate([entry[3] for entry in kept_rows[layer_index]], axis=0)
        in_sums.append(
            lax.dot_general(normed_all, hidden_all, ROWS_DIMS, preferred_element_type=jnp.float32)
        )
        out_sums.append(
            lax.dot_general(gated_all, grad_all, ROWS_DIMS, preferred_element_type=jnp.float32)
        )
    weight_sums = (
        lax.psum_scatter(small_sums[0], "fsdp", scatter_dimension=1, tiled=True),
        lax.psum_scatter(jnp.stack(in_sums), "fsdp", scatter_dimension=1, tiled=True),
        lax.psum_scatter(small_sums[1], "fsdp", scatter_dimension=1, tiled=True),
        lax.psum_scatter(small_sums[2], "fsdp", scatter_dimension=1, tiled=True),
        lax.psum_scatter(small_sums[3], "fsdp", scatter_dimension=1, tiled=True),
        lax.psum_scatter(jnp.stack(out_sums), "fsdp", scatter_dimension=1, tiled=True),
    )
    head_sums = lax.psum((small_sums[4], small_sums[5], small_sums[6]), "fsdp")
    conv_result = jnp.transpose(weight_sums[2], (0, 2, 1))
    return (
        jnp.stack(mixed_blocks),
        jnp.stack(token_grads),
        weight_sums[0],
        weight_sums[1],
        conv_result,
        weight_sums[3],
        head_sums[0],
        head_sums[1],
        head_sums[2],
        weight_sums[4],
        weight_sums[5],
    )


def solution(mesh):
    in_specs = (
        P("fsdp", None, None),
        P("fsdp", None),
        P(None, "fsdp"),
        P(None, "fsdp", None),
        P(None, None, "fsdp"),
        P(None, "fsdp"),
        P(),
        P(),
        P(),
        P(None, "fsdp"),
        P(None, "fsdp", None),
        P("fsdp", None, None),
    )
    out_specs = (
        P("fsdp", None, None),
        P("fsdp", None, None),
        P(None, "fsdp"),
        P(None, "fsdp", None),
        P(None, None, "fsdp"),
        P(None, "fsdp"),
        P(),
        P(),
        P(),
        P(None, "fsdp"),
        P(None, "fsdp", None),
    )
    return jax.shard_map(body, mesh=mesh, in_specs=in_specs, out_specs=out_specs, check_vma=False)
```

profile of v0, /device:TPU:0, one launch (start us, length us, event | category | flops | bytes accessed | tf_op | source)
XLA Modules:
  0.0 1093.9 jit_solution(6118390443331828669)
XLA Ops:
  8.7 43.3 %all-gather.1 = bf16[32,24,2]{1,2,0:T(2,128)(2,1)S(1)} all-gather(bf16[1,24,2]{1,2,0:T(2,128)(2,1)} %bitcast.397), channel_id=1, replica_groups=mesh['fsdp'=32] {'fsdp'}, dimensions={0}, use_global_device_ids=true | all-gather | bytes 3168 | tf_op jit(solution)/shard_map/all_gather | solution.py:86
  52.1 36.6 %all-gather = bf16[32,56,2]{1,2,0:T(2,128)(2,1)S(1)} all-gather(bf16[1,56,2]{1,2,0:T(2,128)(2,1)} %bitcast.398), channel_id=1, replica_groups=mesh['fsdp'=32] {'fsdp'}, dimensions={0}, use_global_device_ids=true | all-gather | bytes 7392 | tf_op jit(solution)/shard_map/all_gather | solution.py:89
  88.8 38.1 %all-gather.2 = bf16[32,48,2]{1,2,0:T(2,128)(2,1)S(1)} all-gather(bf16[1,48,2]{1,2,0:T(2,128)(2,1)} %bitcast.399), channel_id=1, replica_groups=mesh['fsdp'=32] {'fsdp'}, dimensions={0}, use_global_device_ids=true | all-gather | bytes 6336 | tf_op jit(solution)/shard_map/all_gather | solution.py:90
  127.8 42.0 %all_gather.27 = bf16[2,1792,4]{2,0,1:T(2,128)(2,1)S(1)} all-gather(bf16[2,56,4]{2,0,1:T(2,128)(2,1)S(1)} %bitcast.384), channel_id=1, replica_groups=mesh['fsdp'=32] {'fsdp'}, dimensions={1}, use_global_device_ids=true | all-gather | bytes 29568 | tf_op jit(solution)/shard_map/all_gather | solution.py:88
  172.9 1.8 slice_convert_fusion
  174.7 2.3 slice_reduce_fusion.3
  177.1 1.7 slice_reduce_fusion.7
  182.0 3.2 fusion.12
  185.3 3.6 fusion.2
  188.9 4.0 fusion.3
  193.9 1.8 fusion.119
  199.9 2.5 fusion.18
  202.4 2.3 copy.320
  206.4 3.9 fusion.16
  213.3 2.7 multiply_reduce_fusion.45
  216.0 2.4 multiply_reduce_fusion.44
  219.0 4.1 fusion.7
  224.7 1.8 fusion.118
  229.1 2.2 copy.343
  231.3 2.2 copy.345
  233.5 4.0 fusion.19
  237.5 2.1 copy.321
  239.6 2.0 multiply_reduce_fusion.36
  241.6 3.8 fusion.17
  245.5 2.2 copy.319
  249.1 3.3 multiply_reduce_fusion.26
  252.4 3.5 multiply_reduce_fusion.30
  257.1 3.2 fusion.77
  260.3 1.6 fusion.290
  263.4 2.1 reshape.650
  265.4 3.4 fusion.81
  268.9 1.6 fusion.276
  272.0 2.3 copy.298
  278.3 2.0 reduce_window_sum.51
  283.0 1.6 reduce_window_sum.64
  284.7 4.8 multiply_reduce_fusion.3
  289.5 2.2 copy.330
  293.1 4.6 multiply_reduce_fusion.7
  297.7 2.1 copy.324
  301.2 2.5 fusion.329
  303.7 3.0 fusion.331
  310.2 4.6 fusion.4
  314.9 2.3 multiply_reduce_fusion.41
  319.3 1.6 multiply_reduce_fusion.27
  321.0 3.2 multiply_reduce_fusion.31
  325.4 3.4 fusion.79
  331.6 3.2 fusion.83
  338.8 6.4 convolution_bitcast_fusion
  373.2 4.1 multiply_reduce_fusion.1
  378.7 1.6 fusion.328
  384.0 4.7 multiply_reduce_fusion.5
  388.7 2.1 copy.327
  390.9 2.4 fusion.330
  399.4 4.2 fusion
  403.9 1.8 fusion.200
  409.0 5.5 convolution_bitcast_fusion.1
  414.6 15.8 %pad_maximum_fusion = f32[2,768,3352]{1,2,0:T(8,128)} fusion(f32[1,768,3352]{1,2,0:T(8,128)} %convolution_bitcast_fusion, f32[1,768,3352]{1,2,0:T(8,128)} %convolution_bitcast_fusion.1), kind=kLoop, calls=%fused_computation | loop fusion | flops 5148672 | bytes 41189376 | tf_op jit(solution)/shard_map/stack | solution.py:173
  430.3 32.5 %copy.308 = f32[2,768,3352]{2,0,1:T(2,128)} copy(f32[2,768,3352]{1,2,0:T(8,128)} %pad_maximum_fusion) | data formatting | bytes 41189376 | tf_op jit(solution)/shard_map/stack | solution.py:173
  465.6 4.2 pad_maximum_fusion.1
  470.7 2.2 fusion.28
  473.0 2.2 fusion.29
  478.2 113.4 %all-reduce.80.cloned.1.call-done = (f32[2,768]{1,0:T(2,128)}, f32[2,1792,4]{1,2,0:T(4,128)}, f32[2,1792]{1,0:T(2,128)}, f32[2,24]{1,0:T(2,128)}, f32[2,24]{1,0:T(2,128)}, /*index=5*/f32[2,24]{1,0:T(2,128)}) async-done(((f32[2,768]{1,0:T(2,128)}, f32[2,1792,4]{1,2,0:T(4,128)}, f32[2,1792]{1,0:T(2,128)}, f32[2,24]{1,0:T(2,128)}, f32[2,24]{1,0:T(2,128)}, /*index=5*/f32[2,24]{1,0:T(2,128)}), ...) | async-done | bytes 78416
  595.6 346.7 %all-reduce.78.cloned.1.call-done = f32[2,768,3352]{2,0,1:T(2,128)} async-done(((f32[2,768,3352]{2,0,1:T(2,128)}), f32[2,768,3352]{2,0,1:T(2,128)}) %all-reduce.78.cloned.1.call-update) | async-done | bytes 20594704
  944.3 138.9 %reduce-scatter.8.cloned.1.call-done = f32[2,48,768]{2,1,0:T(8,128)} async-done(((f32[2,1536,768]{2,1,0:T(8,128)}), f32[2,48,768]{2,1,0:T(8,128)}) %reduce-scatter.8.cloned.1.call-update) | async-done | bytes 294928 | tf_op jit(solution)/shard_map/reduce_scatter | solution.py:177
  (572 shorter events, 109.5 us)
Async XLA Ops:
  7.2 174.8 %all-gather.8.cloned.1.call-start = ((), (), s32[]{:S(2)}) async-start(), calls=%async_computation.3 | async-start | bytes 4866048 | tf_op jit(solution)/shard_map/all_gather | solution.py:91
  7.9 177.4 %all-gather.6.cloned.1.call-start = ((), (), s32[]{:S(2)}) async-start(), calls=%async_computation.2 | async-start | bytes 10948608 | tf_op jit(solution)/shard_map/all_gather | solution.py:87
  8.7 468.2 %reduce-scatter.10.cloned.1.call-start = ((), (), s32[]{:S(2)}) async-start(), calls=%async_computation.5 | async-start | bytes 811008
  170.5 18.4 %copy-start.128 = (f32[768]{0:T(1024)}, f32[768]{0:T(1024)S(1)}, u32[]{:S(2)}) copy-start(f32[768]{0:T(1024)S(1)} %get-tuple-element.159) | copy-start | bytes 9220
  172.9 9.1 copy-start.53
  174.7 10.5 copy-start.39
  178.8 14.2 %copy-start.76 = (f32[1792]{0:T(1024)}, f32[1792]{0:T(1024)S(1)}, u32[]{:S(2)}) copy-start(f32[1792]{0:T(1024)S(1)} %get-tuple-element.98) | copy-start | bytes 21508
  178.9 14.2 %copy-start.78 = (f32[1792]{0:T(1024)}, f32[1792]{0:T(1024)S(1)}, u32[]{:S(2)}) copy-start(f32[1792]{0:T(1024)S(1)} %get-tuple-element.99) | copy-start | bytes 21508
  178.9 14.2 %copy-start.79 = (f32[1792]{0:T(1024)}, f32[1792]{0:T(1024)S(1)}, u32[]{:S(2)}) copy-start(f32[1792]{0:T(1024)S(1)} %get-tuple-element.100) | copy-start | bytes 21508
  178.9 14.2 %copy-start.80 = (f32[1792]{0:T(1024)}, f32[1792]{0:T(1024)S(1)}, u32[]{:S(2)}) copy-start(f32[1792]{0:T(1024)S(1)} %get-tuple-element.101) | copy-start | bytes 21508
  178.9 14.0 %copy-start.169 = (f32[64]{0:T(128)}, f32[64]{0:T(128)S(1)}, u32[]{:S(2)}) copy-start(f32[64]{0:T(128)S(1)} %fusion.308) | copy-start | bytes 772
  178.9 14.0 %copy-start.171 = (f32[64]{0:T(128)}, f32[64]{0:T(128)S(1)}, u32[]{:S(2)}) copy-start(f32[64]{0:T(128)S(1)} %fusion.312) | copy-start | bytes 772
  179.5 13.5 %copy-start.164 = (f32[64]{0:T(128)}, f32[64]{0:T(128)S(1)}, u32[]{:S(2)}) copy-start(f32[64]{0:T(128)S(1)} %get-tuple-element.296) | copy-start | bytes 772
  180.0 19.8 %copy-start.140 = (f32[24]{0:T(128)}, f32[24]{0:T(128)S(1)}, u32[]{:S(2)}) copy-start(f32[24]{0:T(128)S(1)} %get-tuple-element.304) | copy-start | bytes 292
  180.5 16.1 %copy-start.136 = (f32[24]{0:T(128)}, f32[24]{0:T(128)S(1)}, u32[]{:S(2)}) copy-start(f32[24]{0:T(128)S(1)} %get-tuple-element.306) | copy-start | bytes 292
  181.1 15.5 %copy-start.137 = (f32[24]{0:T(128)}, f32[24]{0:T(128)S(1)}, u32[]{:S(2)}) copy-start(f32[24]{0:T(128)S(1)} %get-tuple-element.308) | copy-start | bytes 292
  181.2 11.9 %copy-start.112 = (pred[64]{0:T(512)(128)(4,1)}, pred[64]{0:T(512)(128)(4,1)S(1)}, u32[]{:S(2)}) copy-start(pred[64]{0:T(512)(128)(4,1)S(1)} %get-tuple-element.309) | copy-start | bytes 196
  181.2 11.9 %copy-start.115 = (pred[64]{0:T(512)(128)(4,1)}, pred[64]{0:T(512)(128)(4,1)S(1)}, u32[]{:S(2)}) copy-start(pred[64]{0:T(512)(128)(4,1)S(1)} %get-tuple-element.310) | copy-start | bytes 196
  181.2 11.9 %copy-start.117 = (pred[64]{0:T(512)(128)(4,1)}, pred[64]{0:T(512)(128)(4,1)S(1)}, u32[]{:S(2)}) copy-start(pred[64]{0:T(512)(128)(4,1)S(1)} %get-tuple-element.311) | copy-start | bytes 196
  181.2 11.9 %copy-start.119 = (pred[64]{0:T(512)(128)(4,1)}, pred[64]{0:T(512)(128)(4,1)S(1)}, u32[]{:S(2)}) copy-start(pred[64]{0:T(512)(128)(4,1)S(1)} %get-tuple-element.312) | copy-start | bytes 196
  181.2 11.9 %copy-start.122 = (pred[64]{0:T(512)(128)(4,1)}, pred[64]{0:T(512)(128)(4,1)S(1)}, u32[]{:S(2)}) copy-start(pred[64]{0:T(512)(128)(4,1)S(1)} %get-tuple-element.313) | copy-start | bytes 196
  181.2 11.9 %copy-start.125 = (pred[64]{0:T(512)(128)(4,1)}, pred[64]{0:T(512)(128)(4,1)S(1)}, u32[]{:S(2)}) copy-start(pred[64]{0:T(512)(128)(4,1)S(1)} %get-tuple-element.314) | copy-start | bytes 196
  181.3 18.5 %copy-start.87 = (pred[64,64]{1,0:T(8,128)(4,1)}, pred[64,64]{1,0:T(8,128)(4,1)S(1)}, u32[]{:S(2)}) copy-start(pred[64,64]{1,0:T(8,128)(4,1)S(1)} %fusion.270) | copy-start | bytes 12292
  188.9 15.8 %copy-start.14 = (f32[64,3352]{1,0:T(8,128)}, f32[64,3352]{1,0:T(8,128)S(1)}, u32[]{:S(2)}) copy-start(f32[64,3352]{1,0:T(8,128)S(1)} %fusion.2) | copy-start | bytes 2574340
  195.9 14.4 %copy-start.62 = (f32[64,64]{1,0:T(8,128)}, f32[64,64]{1,0:T(8,128)S(1)}, u32[]{:S(2)}) copy-start(f32[64,64]{1,0:T(8,128)S(1)} %fusion.295) | copy-start | bytes 49156
  202.3 21.0 %slice-start = ((s8[10616832]{0:T(1024)(128)(4,1)}), s8[2228224]{0:T(1024)(128)(4,1)S(1)}, s32[]{:S(2)}) async-start(s8[10616832]{0:T(1024)(128)(4,1)} %bitcast.347), calls=%async_computation.8 | async-start | bytes 4456448
  206.4 12.0 %copy-start.132 = (f32[64]{0:T(128)}, f32[64]{0:T(128)S(1)}, u32[]{:S(2)}) copy-start(f32[64]{0:T(128)S(1)} %fusion.313) | copy-start | bytes 772
  210.3 8.2 copy-start.93
  213.1 10.2 slice-start.1
  224.5 9.0 copy-start.88
  224.5 9.0 copy-start.141
  224.7 17.0 %copy-start.85 = (pred[64,64]{1,0:T(8,128)(4,1)S(1)}, pred[64,64]{1,0:T(8,128)(4,1)}, u32[]{:S(2)}) copy-start(pred[64,64]{1,0:T(8,128)(4,1)} %fusion.271) | copy-start | bytes 12292
  226.5 25.9 %copy-start.12 = (f32[64,1792]{1,0:T(8,128)}, f32[64,1792]{1,0:T(8,128)S(1)}, u32[]{:S(2)}) copy-start(f32[64,1792]{1,0:T(8,128)S(1)} %get-tuple-element.254) | copy-start | bytes 1376260
  228.6 11.0 %copy-start.1 = (f32[64,3352]{1,0:T(8,128)S(1)}, f32[64,3352]{1,0:T(8,128)}, u32[]{:S(2)}) copy-start(f32[64,3352]{1,0:T(8,128)} %copy-done) | copy-start | bytes 2574340
  228.8 20.2 %copy-start.74 = (f32[24,64]{1,0:T(8,128)}, f32[24,64]{1,0:T(8,128)S(1)}, u32[]{:S(2)}) copy-start(f32[24,64]{1,0:T(8,128)S(1)} %copy.260) | copy-start | bytes 18436
  228.9 20.2 %copy-start.91 = (f32[64,24]{0,1:T(8,128)}, f32[64,24]{0,1:T(8,128)S(1)}, u32[]{:S(2)}) copy-start(f32[64,24]{0,1:T(8,128)S(1)} %copy.258) | copy-start | bytes 18436
  228.9 20.1 %copy-start.92 = (f32[64,24]{0,1:T(8,128)}, f32[64,24]{0,1:T(8,128)S(1)}, u32[]{:S(2)}) copy-start(f32[64,24]{0,1:T(8,128)S(1)} %copy.270) | copy-start | bytes 18436
  229.1 19.9 %copy-start.75 = (f32[24,64]{1,0:T(8,128)}, f32[24,64]{1,0:T(8,128)S(1)}, u32[]{:S(2)}) copy-start(f32[24,64]{1,0:T(8,128)S(1)} %copy.272) | copy-start | bytes 18436
  231.3 17.8 %copy-start.54 = (bf16[2,64,768]{2,1,0:T(8,128)(2,1)S(1)}, bf16[2,64,768]{2,1,0:T(8,128)(2,1)}, u32[]{:S(2)}) copy-start(bf16[2,64,768]{2,1,0:T(8,128)(2,1)} %param.24) | copy-start | bytes 589828
  231.3 17.8 %copy-start.84 = (f32[1536]{0:T(1024)S(1)}, f32[1536]{0:T(1024)}, u32[]{:S(2)}) copy-start(f32[1536]{0:T(1024)} %get-tuple-element.156) | copy-start | bytes 18436
  231.3 17.8 %copy-start.142 = (f32[64]{0:T(128)S(1)}, f32[64]{0:T(128)}, u32[]{:S(2)}) copy-start(f32[64]{0:T(128)} %get-tuple-element.295) | copy-start | bytes 772
  289.5 14.2 %copy-start.67 = (f32[64,128]{1,0:T(8,128)S(1)}, f32[64,128]{1,0:T(8,128)}, u32[]{:S(2)}) copy-start(f32[64,128]{1,0:T(8,128)} %fusion.290) | copy-start | bytes 98308
  297.7 10.3 copy-start.68
  301.2 13.6 %slice-start.3 = ((s8[10616832]{0:T(1024)(128)(4,1)}), s8[4194304]{0:T(1024)(128)(4,1)S(1)}, s32[]{:S(2)}) async-start(s8[10616832]{0:T(1024)(128)(4,1)} %bitcast.349), calls=%async_computation.11 | async-start | bytes 8388608
  306.7 8.1 slice-start.4
  310.2 8.2 slice-start.9
  325.4 13.4 %copy-start.25 = (bf16[64,3352]{1,0:T(8,128)(2,1)S(1)}, bf16[64,3352]{1,0:T(8,128)(2,1)}, u32[]{:S(2)}) copy-start(bf16[64,3352]{1,0:T(8,128)(2,1)} %copy-done.24) | copy-start | bytes 1287172
  325.4 13.4 %copy-start.30 = (bf16[64,768]{1,0:T(8,128)(2,1)S(1)}, bf16[64,768]{1,0:T(8,128)(2,1)}, u32[]{:S(2)}) copy-start(bf16[64,768]{1,0:T(8,128)(2,1)} %copy-done.29) | copy-start | bytes 294916
  325.4 13.4 %copy-start.32 = (bf16[64,768]{1,0:T(8,128)(2,1)S(1)}, bf16[64,768]{1,0:T(8,128)(2,1)}, u32[]{:S(2)}) copy-start(bf16[64,768]{1,0:T(8,128)(2,1)} %copy-done.31) | copy-start | bytes 294916
  345.1 33.5 %copy-start.6 = (f32[64,1792]{1,0:T(8,128)S(1)}, f32[64,1792]{1,0:T(8,128)}, u32[]{:S(2)}) copy-start(f32[64,1792]{1,0:T(8,128)} %copy-done.5) | copy-start | bytes 1376260
  345.1 33.5 %copy-start.65 = (f32[64,128]{1,0:T(8,128)S(1)}, f32[64,128]{1,0:T(8,128)}, u32[]{:S(2)}) copy-start(f32[64,128]{1,0:T(8,128)} %fusion.283) | copy-start | bytes 98308
  345.1 33.5 %copy-start.66 = (f32[64,128]{1,0:T(8,128)S(1)}, f32[64,128]{1,0:T(8,128)}, u32[]{:S(2)}) copy-start(f32[64,128]{1,0:T(8,128)} %fusion.279) | copy-start | bytes 98308
  345.1 33.6 %copy-start.121 = (pred[64]{0:T(512)(128)(4,1)S(1)}, pred[64]{0:T(512)(128)(4,1)}, u32[]{:S(2)}) copy-start(pred[64]{0:T(512)(128)(4,1)} %copy-done.119) | copy-start | bytes 196
  345.1 33.6 %copy-start.124 = (pred[64]{0:T(512)(128)(4,1)S(1)}, pred[64]{0:T(512)(128)(4,1)}, u32[]{:S(2)}) copy-start(pred[64]{0:T(512)(128)(4,1)} %copy-done.122) | copy-start | bytes 196
  345.2 33.6 %copy-start.127 = (pred[64]{0:T(512)(128)(4,1)S(1)}, pred[64]{0:T(512)(128)(4,1)}, u32[]{:S(2)}) copy-start(pred[64]{0:T(512)(128)(4,1)} %copy-done.125) | copy-start | bytes 196
  345.2 38.8 %copy-start.72 = (f32[24,64]{1,0:T(8,128)S(1)}, f32[24,64]{1,0:T(8,128)}, u32[]{:S(2)}) copy-start(f32[24,64]{1,0:T(8,128)} %copy.253) | copy-start | bytes 18436
  369.7 221.9 %all-reduce.80.cloned.1.call-start = ((), (), s32[]{:S(2)}) async-start(), calls=%async_computation.7 | async-start | bytes 161792
  373.2 17.7 %copy-start.114 = (pred[64]{0:T(512)(128)(4,1)S(1)}, pred[64]{0:T(512)(128)(4,1)}, u32[]{:S(2)}) copy-start(pred[64]{0:T(512)(128)(4,1)} %copy-done.112) | copy-start | bytes 196
  384.0 11.5 %copy-start.59 = (f32[64,24]{1,0:T(8,128)S(1)}, f32[64,24]{1,0:T(8,128)}, u32[]{:S(2)}) copy-start(f32[64,24]{1,0:T(8,128)} %copy-done.58) | copy-start | bytes 18436
  384.0 11.5 %copy-start.61 = (f32[64,24]{1,0:T(8,128)S(1)}, f32[64,24]{1,0:T(8,128)}, u32[]{:S(2)}) copy-start(f32[64,24]{1,0:T(8,128)} %copy-done.60) | copy-start | bytes 18436
  384.0 19.7 %slice-start.6 = ((s8[10616832]{0:T(1024)(128)(4,1)}), s8[2228224]{0:T(1024)(128)(4,1)S(1)}, s32[]{:S(2)}) async-start(s8[10616832]{0:T(1024)(128)(4,1)} %bitcast.351), calls=%async_computation.14 | async-start | bytes 4456448
  394.1 9.5 slice-start.7
  414.5 527.8 %all-reduce.78.cloned.1.call-start = ((), (), s32[]{:S(2)}) async-start(), calls=%async_computation.6 | async-start | bytes 42467328
  462.9 620.3 %reduce-scatter.8.cloned.1.call-start = ((), (), s32[]{:S(2)}) async-start(), calls=%async_computation.4 | async-start | bytes 9732096 | tf_op jit(solution)/shard_map/reduce_scatter | solution.py:177
  (134 other events, 589.6 us)
Sparse Core Ops, SparseCore 0:
  11.0 66.4 all-gather.7
  80.3 91.1 all-gather.5
  369.8 92.5 reduce-scatter.9
  469.9 121.6 all-reduce.79
  597.9 344.3 all-reduce.77
  948.6 134.5 reduce-scatter.7
where the time goes:
time: 1100 us; the launch traced here: 1090 us
  waiting for transfers between devices  600 us (55%)
  blocking collectives  160 us (15%)
  local copies, waits for them, and re-layouts  123 us (11%)
  matrix products  113 us (10%)
  other arithmetic  79.4 us (7%)
  between operations  17.1 us (2%)
    unnamed x9, waiting for transfers between devices  462 us
    reduce_scatter x1, waiting for transfers between devices, body(): lax.psum_scatter(jnp.stack(out_sums), 'fsdp', scatter_dimension=1, tiled=...  139 us
    dot_general x12, matrix products, segment_mixer(): states = jnp.einsum('hts,shp->thp', weights, scaled, precision=EXACT)  45.6 us
    all_gather x1, blocking collectives, body(): lax.all_gather(shards[0], 'fsdp', axis=1, tiled=True)  43.3 us
    all_gather x1, blocking collectives, body(): lax.all_gather(shards[2], 'fsdp', axis=1, tiled=True)  42 us
    all_gather x1, blocking collectives, body(): lax.all_gather(shards[4], 'fsdp', axis=1, tiled=True)  38.1 us
    all_gather x1, blocking collectives, body(): lax.all_gather(shards[3], 'fsdp', axis=1, tiled=True)  36.6 us
    another operation x1, local copies, waits for them, and re-layouts, body(): jnp.stack(in_sums)  32.5 us
  transfers between devices with their start and end apart: 6, of which 3 were waited for; matrix products, arithmetic and copies ran while one was open for 12% of the time, Pallas kernels for 0%

commit v1 on v0

v1 whole, which is shorter than its diff:
```python
from functools import partial

import jax
import jax.numpy as jnp
from jax import lax
from jax.experimental import pallas as pl
from jax.experimental.pallas import tpu as pltpu
from jax.sharding import PartitionSpec as P

HEADS = 24
HEADDIM = 64
STATE = 128
CONV = 4
BLOCK = 64
WIDTH = 768
INNER = HEADS * HEADDIM
CONVCH = INNER + 2 * STATE
PROJ = INNER + CONVCH + HEADS
LANES = 128
PADDED = INNER + CONVCH + LANES
PAIRS = INNER // LANES
STEP_AT = INNER + CONVCH
SMALL_ROWS = 8
PARTS = 32
EPSILON = 1e-05
EXACT = lax.Precision.HIGHEST
F32 = jnp.float32
LOW = jnp.bfloat16
NT = (((1,), (1,)), ((), ()))
TN = (((0,), (0,)), ((), ()))
VMEM_LIMIT = 56 * 1024 * 1024


def tile(index):
    return pl.ds(pl.multiple_of(index * LANES, LANES), LANES)


def iota(shape, dim):
    return lax.broadcasted_iota(jnp.int32, shape, dim)


def split(values):
    high = values.astype(LOW)
    return high, (values - high.astype(F32)).astype(LOW)


def low_half():
    return iota((1, LANES), 1) < HEADDIM


def set_masks(seg_col, seg_row, allowed_ref, taps_ref):
    rows = seg_col.shape[0]
    t, s = iota((rows, rows), 0), iota((rows, rows), 1)
    tri = (t >= s) & (t // BLOCK == s // BLOCK)
    allowed_ref[...] = jnp.where(tri & (seg_col == seg_row), 1.0, 0.0)
    wide = jnp.broadcast_to(seg_col, (rows, LANES))
    place = iota((rows, LANES), 0) % BLOCK
    for tap in range(1, CONV):
        earlier = pltpu.roll(wide, tap, axis=0)
        taps_ref[tap - 1] = jnp.where((earlier == wide) & (place >= tap), 1.0, 0.0)
    return jnp.where(tri, 1.0, 0.0)


def conv_tile(signal, weight_ref, bias_ref, taps_ref, at):
    total = bias_ref[:, at] + signal * weight_ref[CONV - 1 : CONV, at]
    for tap in range(1, CONV):
        shifted = pltpu.roll(signal, tap, axis=0) * taps_ref[tap - 1]
        total = total + shifted * weight_ref[CONV - 1 - tap : CONV - tap, at]
    return total


def steps(raw, heads_ref):
    raw = raw + heads_ref[2:3]
    step = jnp.maximum(raw, 0.0) + jnp.log1p(jnp.exp(-jnp.abs(raw)))
    return raw, step, step * -jnp.exp(heads_ref[0:1])


def spread_heads(high, low, index):
    head = iota((LANES, LANES), 0)
    lane = iota((LANES, LANES), 1)
    pick = jnp.where(head == 2 * index + lane // HEADDIM, 1.0, 0.0).astype(LOW)
    return jnp.dot(high, pick, preferred_element_type=F32) + jnp.dot(
        low, pick, preferred_element_type=F32
    )


def decays(turned_ref, allowed, head):
    rows = allowed.shape[0]
    across = jnp.broadcast_to(turned_ref[pl.ds(head, 1), :], (rows, rows))
    gaps = jnp.where(allowed > 0.0, across.T - across, -1e30)
    return jnp.exp(gaps)


def forward_kernel(
    resid_ref, in_ref, out_ref, norm_ref, conv_ref, bias_ref, gate_ref, heads_ref, skip_ref, col_ref, row_ref,
    next_ref, hidden_ref, mixed_ref, normed_ref, gated_ref,
    allowed_ref, taps_ref, turned_ref, scores_ref, product_ref,
):
    tri = set_masks(col_ref[...], row_ref[...], allowed_ref, taps_ref)
    resid = resid_ref[...]
    scale = lax.rsqrt(jnp.mean(resid * resid, axis=-1, keepdims=True) + EPSILON)
    normed_ref[...] = (resid * scale * norm_ref[...]).astype(LOW)

    def project(index, carry):
        at = pl.ds(pl.multiple_of(index * 3 * LANES, LANES), 3 * LANES)
        hidden_ref[:, at] = jnp.dot(normed_ref[...], in_ref[:, at], preferred_element_type=F32)
        return carry

    lax.fori_loop(0, PADDED // (3 * LANES), project, 0)
    raw, step, rate = steps(hidden_ref[:, STEP_AT:], heads_ref)
    turned_ref[...] = jnp.dot(tri, rate, precision=EXACT, preferred_element_type=F32).T
    high, low = split(step)
    pair = []
    for index in (0, 1):
        at = pl.ds(INNER + index * STATE, STATE)
        total = conv_tile(hidden_ref[:, pl.ds(2 * INNER + index * STATE, STATE)], conv_ref, bias_ref, taps_ref, at)
        pair.append(total * jax.nn.sigmoid(total))
    scores_ref[...] = lax.dot_general(pair[1], pair[0], NT, precision=EXACT, preferred_element_type=F32)
    first = low_half()

    def heads(index, squares):
        at = tile(index)
        total = conv_tile(hidden_ref[:, tile(index + PAIRS)], conv_ref, bias_ref, taps_ref, at)
        values = total * jax.nn.sigmoid(total)
        scaled = values * spread_heads(high, low, index)
        allowed = allowed_ref[...]
        scores = scores_ref[...]
        weights = jnp.concatenate(
            [(scores * decays(turned_ref, allowed, 2 * index + head)).astype(LOW) for head in (0, 1)], axis=1
        )
        both = jnp.concatenate([jnp.where(first, scaled, 0.0), jnp.where(first, 0.0, scaled)], axis=0).astype(LOW)
        mixed = jnp.dot(weights, both, preferred_element_type=F32)
        mixed_ref[:, at] = mixed
        gate = hidden_ref[:, at]
        product = (mixed + values * skip_ref[:, at]) * (gate * jax.nn.sigmoid(gate))
        product_ref[:, at] = product
        return squares + product * product

    squares = lax.fori_loop(0, PAIRS, heads, jnp.zeros((resid.shape[0], LANES), F32))
    scale = lax.rsqrt(jnp.sum(squares, axis=-1, keepdims=True) / INNER + EPSILON)
    gated_ref[...] = (product_ref[...] * scale * gate_ref[...]).astype(LOW)
    next_ref[...] = resid + jnp.dot(gated_ref[...], out_ref[...], preferred_element_type=F32)


def backward_kernel(
    me_ref, grad_ref, resid_ref, hidden_ref, mixed_ref, normed_ref, gated_ref,
    in_ref, out_ref, norm_ref, conv_ref, bias_ref, gate_ref, heads_ref, skip_ref, col_ref, row_ref,
    back_ref, in_keep_ref, in_send_ref, out_keep_ref, out_send_ref, small_ref,
    allowed_ref, taps_ref, turned_ref, scores_ref, dscores_ref, gated_grad_ref, values_ref, slope_ref,
    dhidden_ref, gathered_ref, turned_norm_ref, dnorm_ref,
):
    me = me_ref[0]
    core = me % 2
    chip = me // 2
    tri = set_masks(col_ref[...], row_ref[...], allowed_ref, taps_ref)
    rows = grad_ref.shape[0]
    grad_low = grad_ref[...].astype(LOW)
    small_ref[...] = jnp.zeros_like(small_ref)

    def out_back(index, carry):
        at = pl.ds(pl.multiple_of(index * 3 * LANES, LANES), 3 * LANES)
        gated_grad_ref[:, at] = lax.dot_general(grad_low, out_ref[at, :], NT, preferred_element_type=F32)
        part = lax.dot_general(gated_ref[:, at], grad_low, TN, preferred_element_type=F32)
        depth = INNER // PARTS
        for pair in range(3 * LANES // (2 * depth)):
            even = part[2 * pair * depth : (2 * pair + 1) * depth]
            odd = part[(2 * pair + 1) * depth : (2 * pair + 2) * depth]
            other = (index * (3 * LANES // (2 * depth)) + pair) ^ chip
            out_keep_ref[other % 4, other // 4] = jnp.where(core == 0, even, odd).astype(LOW)
            out_send_ref[other % 4, other // 4] = jnp.where(core == 0, odd, even).astype(LOW)
        return carry

    lax.fori_loop(0, INNER // (3 * LANES), out_back, 0)

    raw, step, rate = steps(hidden_ref[:, STEP_AT:], heads_ref)
    turned_ref[...] = jnp.dot(tri, rate, precision=EXACT, preferred_element_type=F32).T
    high, low = split(step)

    def again(index, carry):
        at = tile(index)
        total = conv_tile(hidden_ref[:, tile(index + PAIRS)], conv_ref, bias_ref, taps_ref, at)
        sigmoid = jax.nn.sigmoid(total)
        values_ref[:, at] = total * sigmoid
        slope_ref[:, at] = sigmoid * (1.0 + total * (1.0 - sigmoid))
        return carry

    lax.fori_loop(0, PAIRS + 2, again, 0)
    inputs_b = values_ref[:, INNER : INNER + STATE]
    outputs_c = values_ref[:, INNER + STATE :]
    scores_ref[...] = lax.dot_general(outputs_c, inputs_b, NT, precision=EXACT, preferred_element_type=F32)
    dscores_ref[...] = jnp.zeros_like(dscores_ref)

    def measure(index, carry):
        squares, dots = carry
        at = tile(index)
        gate = hidden_ref[:, at]
        product = (mixed_ref[:, at] + values_ref[:, at] * skip_ref[:, at]) * (gate * jax.nn.sigmoid(gate))
        return squares + product * product, dots + product * gated_grad_ref[:, at] * gate_ref[:, at]

    zero = jnp.zeros((rows, LANES), F32)
    squares, dots = lax.fori_loop(0, PAIRS, measure, (zero, zero))
    scale = lax.rsqrt(jnp.sum(squares, axis=-1, keepdims=True) / INNER + EPSILON)
    pull = scale * scale * scale * (jnp.sum(dots, axis=-1, keepdims=True) / INNER)
    first = low_half()

    def conv_back(index, du):
        at = tile(index)
        signal = hidden_ref[:, tile(index + PAIRS)]
        small_ref[5:6, at] = jnp.sum(du, axis=0, keepdims=True)
        small_ref[CONV : CONV + 1, at] = jnp.sum(du * signal, axis=0, keepdims=True)
        total = du * conv_ref[CONV - 1 : CONV, at]
        for tap in range(1, CONV):
            masked = du * taps_ref[tap - 1]
            shifted = pltpu.roll(signal, tap, axis=0)
            small_ref[CONV - tap : CONV - tap + 1, at] = jnp.sum(masked * shifted, axis=0, keepdims=True)
            total = total + pltpu.roll(masked, rows - tap, axis=0) * conv_ref[CONV - 1 - tap : CONV - tap, at]
        dhidden_ref[:, tile(index + PAIRS)] = total.astype(LOW)

    def heads(index, carry):
        dcum, dstep = carry
        at = tile(index)
        gate = hidden_ref[:, at]
        sigmoid = jax.nn.sigmoid(gate)
        silu = gate * sigmoid
        values = values_ref[:, at]
        mixed = mixed_ref[:, at]
        skip = skip_ref[:, at]
        states = mixed + values * skip
        product = states * silu
        gated_grad = gated_grad_ref[:, at]
        small_ref[6:7, at] = jnp.sum(gated_grad * product * scale, axis=0, keepdims=True)
        dproduct = scale * (gated_grad * gate_ref[:, at]) - product * pull
        dhidden_ref[:, at] = (dproduct * states * (sigmoid * (1.0 + gate * (1.0 - sigmoid)))).astype(LOW)
        dstates = dproduct * silu
        small_ref[7:8, at] = jnp.sum(dstates * values, axis=0, keepdims=True)
        step_wide = spread_heads(high, low, index)
        scaled = (values * step_wide).astype(LOW)
        dlow = dstates.astype(LOW)
        none = jnp.zeros_like(dlow)
        stacked = jnp.concatenate([jnp.where(first, dlow, none), jnp.where(first, none, dlow)], axis=0)
        allowed = allowed_ref[...]
        scores = scores_ref[...]
        factors = [decays(turned_ref, allowed, 2 * index + head) for head in (0, 1)]
        weights = jnp.concatenate([(scores * factor).astype(LOW) for factor in factors], axis=0)
        dweights = lax.dot_general(stacked, scaled, NT, preferred_element_type=F32)
        dscores_ref[...] += dweights[:rows] * factors[0] + dweights[rows:] * factors[1]
        dscaled = lax.dot_general(weights, stacked, TN, preferred_element_type=F32)
        head = iota((LANES, LANES), 1)
        lane = iota((LANES, LANES), 0)
        pick = jnp.where(head == 2 * index + lane // HEADDIM, 1.0, 0.0).astype(LOW)
        gained = split(dlow.astype(F32) * mixed - scaled.astype(F32) * dscaled)
        dcum = dcum + sum(jnp.dot(item, pick, preferred_element_type=F32) for item in gained)
        gained = split(values * dscaled)
        dstep = dstep + sum(jnp.dot(item, pick, preferred_element_type=F32) for item in gained)
        dvalues = step_wide * dscaled + skip * dstates
        conv_back(index, dvalues * slope_ref[:, at])
        return dcum, dstep

    dcum, dstep = lax.fori_loop(0, PAIRS, heads, (zero, zero))
    dscores = dscores_ref[...]
    dinputs = lax.dot_general(dscores, outputs_c, TN, precision=EXACT, preferred_element_type=F32)
    doutputs = jnp.dot(dscores, inputs_b, precision=EXACT, preferred_element_type=F32)
    conv_back(PAIRS, dinputs * slope_ref[:, INNER : INNER + STATE])
    conv_back(PAIRS + 1, doutputs * slope_ref[:, INNER + STATE :])
    drate = lax.dot_general(tri, dcum, TN, precision=EXACT, preferred_element_type=F32)
    small_ref[0:1, WIDTH : WIDTH + LANES] = jnp.sum(drate * rate, axis=0, keepdims=True)
    draw = (dstep - drate * jnp.exp(heads_ref[0:1])) * jax.nn.sigmoid(raw)
    small_ref[0:1, WIDTH + LANES : WIDTH + 2 * LANES] = jnp.sum(draw, axis=0, keepdims=True)
    dhidden_ref[:, STEP_AT:] = draw.astype(LOW)

    turned_norm_ref[...] = normed_ref[...].T
    dnorm_ref[...] = jnp.zeros_like(dnorm_ref)

    def in_back(index, carry):
        at = pl.ds(pl.multiple_of(index * 3 * LANES, LANES), 3 * LANES)
        dhidden = dhidden_ref[:, at]
        dnorm_ref[...] += lax.dot_general(dhidden, in_ref[:, at], NT, preferred_element_type=F32)
        gathered_ref[...] = jnp.dot(turned_norm_ref[...], dhidden, preferred_element_type=F32)
        depth = WIDTH // PARTS
        for pair in range(PARTS // 2):
            even = gathered_ref[2 * pair * depth : (2 * pair + 1) * depth]
            odd = gathered_ref[(2 * pair + 1) * depth : (2 * pair + 2) * depth]
            other = pair ^ chip
            in_keep_ref[other % 4, other // 4, :, at] = jnp.where(core == 0, even, odd).astype(LOW)
            in_send_ref[other % 4, other // 4, :, at] = jnp.where(core == 0, odd, even).astype(LOW)
        return carry

    lax.fori_loop(0, PADDED // (3 * LANES), in_back, 0)
    resid = resid_ref[...]
    scale = lax.rsqrt(jnp.mean(resid * resid, axis=-1, keepdims=True) + EPSILON)
    dnorm = dnorm_ref[...]
    small_ref[0:1, :WIDTH] = jnp.sum(dnorm * resid * scale, axis=0, keepdims=True)
    gained = dnorm * norm_ref[...]
    pull = scale * scale * scale * jnp.mean(gained * resid, axis=-1, keepdims=True)
    back_ref[...] = grad_ref[...] + scale * gained - resid * pull


def shape(*dims, dtype=F32):
    return jax.ShapeDtypeStruct(dims, dtype)


def mixer_scratch(rows):
    return [
        pltpu.VMEM((rows, rows), F32),
        pltpu.VMEM((CONV - 1, rows, LANES), F32),
        pltpu.VMEM((LANES, rows), F32),
        pltpu.VMEM((rows, rows), F32),
    ]


VMEM = pl.BlockSpec(memory_space=pltpu.VMEM)
SMEM = pl.BlockSpec(memory_space=pltpu.SMEM)


def forward(resid, weights, small, segs):
    rows = resid.shape[0]
    return pl.pallas_call(
        forward_kernel,
        out_shape=(
            shape(rows, WIDTH),
            shape(rows, PADDED),
            shape(rows, INNER),
            shape(rows, WIDTH, dtype=LOW),
            shape(rows, INNER, dtype=LOW),
        ),
        in_specs=[VMEM] * 11,
        out_specs=(VMEM,) * 5,
        scratch_shapes=mixer_scratch(rows) + [pltpu.VMEM((rows, INNER), F32)],
        compiler_params=pltpu.CompilerParams(vmem_limit_bytes=VMEM_LIMIT),
        cost_estimate=pl.CostEstimate(flops=40_000_000_000, bytes_accessed=12_000_000, transcendentals=0),
        name="block_forward",
    )(resid, *weights, *small, *segs)


def backward(me, grad, resid, kept, weights, small, segs):
    rows = resid.shape[0]
    in_part = shape(4, 4, WIDTH // PARTS, PADDED, dtype=LOW)
    out_part = shape(4, 4, INNER // PARTS, WIDTH, dtype=LOW)
    return pl.pallas_call(
        backward_kernel,
        out_shape=(shape(rows, WIDTH), in_part, in_part, out_part, out_part, shape(SMALL_ROWS, CONVCH)),
        in_specs=[SMEM] + [VMEM] * 16,
        out_specs=(VMEM,) * 6,
        scratch_shapes=mixer_scratch(rows)
        + [
            pltpu.VMEM((rows, rows), F32),
            pltpu.VMEM((rows, INNER), F32),
            pltpu.VMEM((rows, CONVCH), F32),
            pltpu.VMEM((rows, CONVCH), F32),
            pltpu.VMEM((rows, PADDED), LOW),
            pltpu.VMEM((WIDTH, 3 * LANES), F32),
            pltpu.VMEM((WIDTH, rows), LOW),
            pltpu.VMEM((rows, WIDTH), F32),
        ],
        compiler_params=pltpu.CompilerParams(vmem_limit_bytes=VMEM_LIMIT),
        cost_estimate=pl.CostEstimate(flops=60_000_000_000, bytes_accessed=24_000_000, transcendentals=0),
        name="block_backward",
    )(me, grad, resid, *kept, *weights, *small, *segs)


def swap(values, bit, count):
    return lax.ppermute(values, "fsdp", [(index, index ^ bit) for index in range(count)])


def place_kernel(me_ref, *refs):
    *pieces, whole_ref = refs
    me = me_ref[0]
    for core in (0, 1):
        cur, right, up, far_a, far_b = pieces[5 * core : 5 * core + 5]
        half = far_a.shape[0]
        for group, (ref, start) in enumerate(((cur, 0), (right, 0), (up, 0), (far_a, 0), (far_b, half))):
            for item in range(ref.shape[0]):
                away = 2 * (4 * (start + item) + min(group, 3)) + core
                whole_ref[me ^ away] = ref[item]


def gather(shard, me, count):
    if count != PARTS:
        return lax.all_gather(shard, "fsdp", axis=0, tiled=True)
    cur = shard[None]
    cur = jnp.concatenate([cur, swap(cur, 8, count)], axis=0)
    cur = jnp.concatenate([cur, swap(cur, 16, count)], axis=0)
    right, up = swap(cur, 2, count), swap(cur, 4, count)
    pieces = [cur, right, up, swap(right[:2], 4, count), swap(up[2:], 2, count)]
    pieces = pieces + [swap(piece, 1, count) for piece in pieces]
    whole = pl.pallas_call(
        place_kernel,
        out_shape=jax.ShapeDtypeStruct((PARTS,) + shard.shape, shard.dtype),
        in_specs=[SMEM] + [VMEM] * 10,
        out_specs=VMEM,
        compiler_params=pltpu.CompilerParams(vmem_limit_bytes=VMEM_LIMIT),
        cost_estimate=pl.CostEstimate(flops=0, bytes_accessed=10_000_000, transcendentals=0),
        name="place",
    )(me, *pieces)
    return whole.reshape(PARTS * shard.shape[0], shard.shape[1])


def scatter(keep, send, count):
    if count != PARTS:
        both = jnp.stack([jnp.swapaxes(keep, 0, 1), jnp.swapaxes(send, 0, 1)], axis=2)
        whole = both.reshape(-1, keep.shape[-1]).astype(F32)
        return lax.psum_scatter(whole, "fsdp", scatter_dimension=0, tiled=True)
    other = swap(send, 1, count)

    def local(group, low, high):
        return keep[group, low:high].astype(F32) + other[group, low:high].astype(F32)

    far_a = swap(local(3, 0, 2).astype(LOW), 4, count)
    far_b = swap(local(3, 2, 4).astype(LOW), 2, count)
    to_right = jnp.concatenate([local(1, 0, 2) + far_a.astype(F32), local(1, 2, 4)]).astype(LOW)
    to_up = jnp.concatenate([local(2, 0, 2), local(2, 2, 4) + far_b.astype(F32)]).astype(LOW)
    right, up = swap(to_right, 2, count), swap(to_up, 4, count)

    def mine(low, high):
        return local(0, low, high) + right[low:high].astype(F32) + up[low:high].astype(F32)

    deep = swap(mine(2, 4).astype(LOW), 16, count)
    near = swap((mine(1, 2) + deep[1:2].astype(F32)).astype(LOW), 8, count)
    return (mine(0, 1) + deep[0:1].astype(F32) + near.astype(F32))[0]


def gather_small(values, me, count):
    bit = 1
    while bit < count:
        other = swap(values, bit, count)
        upper = (me & bit) > 0
        values = jnp.where(
            upper, jnp.concatenate([other, values], axis=0), jnp.concatenate([values, other], axis=0)
        )
        bit *= 2
    return values


def sum_small(values, count):
    bit = 1
    while bit < count:
        values = values + swap(values, bit, count)
        bit *= 2
    return values


def body(
    count, tokens, segments, norm_gain, in_weight, conv_weight, conv_bias,
    log_decay, skip_gain, step_bias, gate_gain, out_weight, cotangent,
):
    layers, in_rows = in_weight.shape[:2]
    blocks = tokens.shape[0]
    rows = blocks * BLOCK
    me = lax.axis_index("fsdp")
    place = me if count == PARTS else me * 0
    place = place.astype(jnp.int32).reshape(1)
    chans = conv_bias.shape[1]
    widths = (in_rows, CONV * chans, chans, gate_gain.shape[1])
    packed = jnp.concatenate(
        [norm_gain, conv_weight.reshape(layers, -1), conv_bias, gate_gain], axis=1
    )
    packed = gather_small(packed[None], me, count)
    padded = jnp.pad(in_weight, ((0, 0), (0, 0), (0, PADDED - PROJ)))
    weights = [
        (gather(padded[layer], place, count), gather(out_weight[layer], place, count)) for layer in range(layers)
    ]
    small = []
    for layer in range(layers):
        ends = [sum(widths[: item + 1]) for item in range(4)]
        held = packed[:, layer].astype(F32)
        norm = held[:, : ends[0]].reshape(1, WIDTH)
        conv = held[:, ends[0] : ends[1]].reshape(count, CONV, chans)
        conv = jnp.swapaxes(conv, 0, 1).reshape(CONV, CONVCH)
        bias = held[:, ends[1] : ends[2]].reshape(1, CONVCH)
        gate = held[:, ends[2] :].reshape(1, INNER)
        heads = jnp.pad(
            jnp.stack([log_decay[layer], skip_gain[layer], step_bias[layer]]), ((0, 0), (0, LANES - HEADS))
        )
        skip = jnp.repeat(skip_gain[layer], HEADDIM).reshape(1, INNER)
        small.append((norm, conv, bias, gate, heads, skip))
    segs = (segments.reshape(rows, 1), segments.reshape(1, rows))
    resid = tokens.reshape(rows, WIDTH).astype(F32)
    kept = []
    for layer in range(layers):
        after, *saved = forward(resid, weights[layer], small[layer], segs)
        kept.append((resid, saved))
        resid = after
    valid = (segs[0] >= 0).astype(F32)
    mixed = (resid * valid).astype(LOW).reshape(tokens.shape)
    grad = cotangent.reshape(rows, WIDTH).astype(F32) * valid
    in_grads, out_grads, sums = [None] * layers, [None] * layers, [None] * layers
    for layer in reversed(range(layers)):
        resid, saved = kept[layer]
        grad, in_keep, in_send, out_keep, out_send, sums[layer] = backward(
            place, grad, resid, saved, weights[layer], small[layer], segs
        )
        out_grads[layer] = scatter(out_keep, out_send, count)
        in_grads[layer] = scatter(in_keep, in_send, count)[:, :PROJ]
    total = sum_small(jnp.stack(sums), count)

    def own(values, size):
        return lax.dynamic_slice_in_dim(values, me * size, size, axis=values.ndim - 1)

    by_head = total[:, 7, :INNER].reshape(layers, HEADS, HEADDIM).sum(axis=-1)
    return (
        mixed,
        grad.reshape(tokens.shape),
        own(total[:, 0, :WIDTH], in_rows),
        jnp.stack(in_grads),
        own(total[:, 1 : 1 + CONV], chans),
        own(total[:, 5], chans),
        total[:, 0, WIDTH : WIDTH + HEADS],
        by_head,
        total[:, 0, WIDTH + LANES : WIDTH + LANES + HEADS],
        own(total[:, 6, :INNER], gate_gain.shape[1]),
        jnp.stack(out_grads),
    )


def solution(mesh):
    split0 = P("fsdp", None, None)
    split1 = P(None, "fsdp", None)
    in_specs = (
        split0, P("fsdp", None), P(None, "fsdp"), split1, P(None, None, "fsdp"), P(None, "fsdp"),
        P(), P(), P(), P(None, "fsdp"), split1, split0,
    )
    out_specs = (
        split0, split0, P(None, "fsdp"), split1, P(None, None, "fsdp"), P(None, "fsdp"),
        P(), P(), P(), P(None, "fsdp"), split1,
    )
    return jax.shard_map(
        partial(body, mesh.shape["fsdp"]), mesh=mesh, in_specs=in_specs, out_specs=out_specs, check_vma=False
    )
```

time: 1100 us -> 361 us (0.33)
  waiting for transfers between devices: 600 us -> 153 us
  blocking collectives: 160 us -> 0 us
  matrix products: 113 us -> 0 us
  local copies, waits for them, and re-layouts: 123 us -> 23 us
  Pallas kernels: 0 us -> 86.3 us
  starting transfers between devices: 0.45 us -> 56.1 us
  other arithmetic: 79.4 us -> 39.4 us
  between operations: 17.1 us -> 1.48 us
    unnamed x9 -> x0, waiting for transfers between devices: 462 us -> none
    all_gather x4 -> x0, blocking collectives: 160 us -> none  [the longest x1 43.3 us: body(): lax.all_gather(shards[0], 'fsdp', axis=1, tiled=True)]
    ppermute x0 -> x82, waiting for transfers between devices: none -> 153 us  [swap(): lax.ppermute(values, 'fsdp', [(index, index ^ bit) for index in range(cou...]
    reduce_scatter x1 -> x0, waiting for transfers between devices: 139 us -> none  [body(): lax.psum_scatter(jnp.stack(out_sums), 'fsdp', scatter_dimension=1, tiled=...]
    dot_general x44 -> x0, matrix products: 113 us -> none  [the longest x12 45.6 us: segment_mixer(): states = jnp.einsum('hts,shp->thp', weights, scaled, precision=EXACT)]
    pallas_call x0 -> x8, Pallas kernels: none -> 86.3 us  [the longest x2 45.7 us: backward(): pl.pallas_call(backward_kernel, out_shape=(shape(rows, WIDTH), in_part, i...]
    ppermute x0 -> x82, starting transfers between devices: none -> 56.1 us  [swap(): lax.ppermute(values, 'fsdp', [(index, index ^ bit) for index in range(cou...]
    reshape x48 -> x15, local copies, waits for them, and re-layouts: 53.8 us -> 8.53 us  [the longest x2 2.06 us: body(): norm = held[:, :ends[0]].reshape(1, WIDTH)]
  transfers between devices with their start and end apart: 6 -> 82, of which waited for: 3 -> 43; matrix products, arithmetic and copies ran while one was open for 12% -> 15% of each run, Pallas kernels for 0% -> 7%
where the time goes in v1:
time: 361 us; the launch traced here: 359 us
  waiting for transfers between devices  153 us (42%)
  Pallas kernels  86.3 us (24%)
  starting transfers between devices  56.1 us (16%)
  other arithmetic  39.4 us (11%)
  local copies, waits for them, and re-layouts  23 us (6%)
    ppermute x82, waiting for transfers between devices, swap(): lax.ppermute(values, 'fsdp', [(index, index ^ bit) for index in range(cou...  153 us
    ppermute x82, starting transfers between devices, swap(): lax.ppermute(values, 'fsdp', [(index, index ^ bit) for index in range(cou...  56.1 us
    pallas_call x2, Pallas kernels, backward(): pl.pallas_call(backward_kernel, out_shape=(shape(rows, WIDTH), in_part, i...  45.7 us
    pallas_call x2, Pallas kernels, forward(): pl.pallas_call(forward_kernel, out_shape=(shape(rows, WIDTH), shape(rows,...  23.9 us
    pallas_call x4, Pallas kernels, gather(): pl.pallas_call(place_kernel, out_shape=jax.ShapeDtypeStruct((PARTS,) + sh...  16.7 us
  transfers between devices with their start and end apart: 82, of which 43 were waited for; matrix products, arithmetic and copies ran while one was open for 15% of the time, Pallas kernels for 7%

profile of v1, /device:TPU:0, one launch (start us, length us, event | category | flops | bytes accessed | tf_op | source)
XLA Modules:
  0.0 359.3 jit_solution(17885110757181207767)
XLA Ops:
  3.5 2.9 collective-permute-start.23
  7.4 1.6 collective-permute-start
  9.0 1.6 collective-permute-start.24
  16.8 2.7 collective-permute-start.12
  19.5 3.1 collective-permute-done.38
  22.6 2.0 collective-permute-start.39
  25.7 10.7 %collective-permute-done.12 = bf16[2,48,768]{2,1,0:T(8,128)(2,1)S(1)} collective-permute-done((bf16[2,48,768]{2,1,0:T(8,128)(2,1)S(1)}, bf16[2,48,768]{2,1,0:T(8,128)(2,1)S(1)}, u32[]{:S(2)}, u32[]{:S(2)}) %collective-permute-start.12) | collective-permute-done | bytes 147488 | tf_op jit(solution)/shard_map/ppermute | solution.py:362
  37.4 2.1 collective-permute-done.39
  40.6 3.9 %collective-permute-done.13.refs_1_ = bf16[4,48,768]{2,1,0:T(8,128)(2,1)S(1)} collective-permute-done((bf16[4,48,768]{2,1,0:T(8,128)(2,1)S(1)}, bf16[4,48,768]{2,1,0:T(8,128)(2,1)S(1)}, u32[]{:S(2)}, u32[]{:S(2)}) %collective-permute-start.13) | collective-permute-done | bytes 294944 | tf_op jit(solution)/shard_map/ppermute | solution.py:362
  44.5 1.2 collective-permute-done.14.refs_2_
  45.8 3.9 %collective-permute-done.40.refs_1_ = bf16[4,48,768]{2,1,0:T(8,128)(2,1)} collective-permute-done((bf16[4,48,768]{2,1,0:T(8,128)(2,1)S(1)}, bf16[4,48,768]{2,1,0:T(8,128)(2,1)}, u32[]{:S(2)}, u32[]{:S(2)}) %collective-permute-start.40) | collective-permute-done | bytes 294944 | tf_op jit(solution)/shard_map/ppermute | solution.py:362
  49.7 1.3 collective-permute-start.26
  52.0 9.6 %collective-permute-done.26 = bf16[16,2,352]{2,1,0:T(2,128)(2,1)S(1)} collective-permute-done((bf16[16,2,352]{2,1,0:T(2,128)(2,1)S(1)}, bf16[16,2,352]{2,1,0:T(2,128)(2,1)S(1)}, u32[]{:S(2)}, u32[]{:S(2)}) %collective-permute-start.26) | collective-permute-done | bytes 22560 | tf_op jit(solution)/shard_map/ppermute | solution.py:362
  61.7 1.3 collective-permute-start.15
  64.5 1.2 collective-permute-start.43
  68.4 1.4 collective-permute-done.16.refs_4_
  70.5 2.4 collective-permute-done.43.refs_4_
  75.5 1.7 bitcast_convert_fusion.resid_ref
  79.0 8.1 %collective-permute-done.2.refs_1_ = bf16[4,24,3456]{2,1,0:T(8,128)(2,1)S(1)} collective-permute-done((bf16[4,24,3456]{2,1,0:T(8,128)(2,1)S(1)}, bf16[4,24,3456]{2,1,0:T(8,128)(2,1)S(1)}, u32[]{:S(2)}, u32[]{:S(2)}) %collective-permute-start.2) | collective-permute-done | bytes 663584 | tf_op jit(solution)/shard_map/ppermute | solution.py:362
  90.2 1.8 collective-permute-done.3.refs_2_
  92.0 7.9 %collective-permute-done.29.refs_1_ = bf16[4,24,3456]{2,1,0:T(8,128)(2,1)S(1)} collective-permute-done((bf16[4,24,3456]{2,1,0:T(8,128)(2,1)S(1)}, bf16[4,24,3456]{2,1,0:T(8,128)(2,1)S(1)}, u32[]{:S(2)}, u32[]{:S(2)}) %collective-permute-start.29) | collective-permute-done | bytes 663584 | tf_op jit(solution)/shard_map/ppermute | solution.py:362
  104.5 1.6 collective-permute-done.30.refs_2_
  107.6 5.7 %collective-permute-done.4.refs_3_ = bf16[2,24,3456]{2,1,0:T(8,128)(2,1)} collective-permute-done((bf16[2,24,3456]{2,1,0:T(8,128)(2,1)S(1)}, bf16[2,24,3456]{2,1,0:T(8,128)(2,1)}, u32[]{:S(2)}, u32[]{:S(2)}) %collective-permute-start.4) | collective-permute-done | bytes 331808 | tf_op jit(solution)/shard_map/ppermute | solution.py:362
  113.6 6.3 %collective-permute-done.31.refs_3_ = bf16[2,24,3456]{2,1,0:T(8,128)(2,1)S(1)} collective-permute-done((bf16[2,24,3456]{2,1,0:T(8,128)(2,1)S(1)}, bf16[2,24,3456]{2,1,0:T(8,128)(2,1)S(1)}, u32[]{:S(2)}, u32[]{:S(2)}) %collective-permute-start.31) | collective-permute-done | bytes 331808 | tf_op jit(solution)/shard_map/ppermute | solution.py:362
  124.3 1.4 reshape.469.norm_ref
  127.9 3.2 place.5
  131.1 3.2 place.7
  135.7 5.2 %place.4 = bf16[32,24,3456]{2,1,0:T(8,128)(2,1)} custom-call(s32[1]{0:T(128)} %bitcast.1.me_ref, bf16[4,24,3456]{2,1,0:T(8,128)(2,1)} %copy-done.2, bf16[4,24,3456]{2,1,0:T(8,128)(2,1)} %copy-done.4, bf16[4,24,3456]{2,1,0:T(8,128)(2,1)} %collective-permute-done.3.refs_2_, bf16[2,24,3456]{2,1,0:T(8,128)(2,1)} %collective-permute-done.4.refs_3_, ...), custom_call_target="tpu_custom_call" | custom-call | bytes 10000000 | tf_op jit(solution)/shard_map/place/pallas_call | solution.py:386
  140.9 12.0 %block_forward.2 = (f32[128,768]{1,0:T(8,128)}, f32[128,3456]{1,0:T(8,128)}, f32[128,1536]{1,0:T(8,128)}, bf16[128,768]{1,0:T(8,128)(2,1)}, bf16[128,1536]{1,0:T(8,128)(2,1)}) custom-call(f32[128,768]{1,0:T(8,128)} %bitcast_convert_fusion.resid_ref, bf16[768,3456]{1,0:T(8,128)(2,1)} %bitcast.200, bf16[1536,768]{1,0:T(8,128)(2,1)} %bitcast.204, ...), custom_call_target="tpu_custom_call" | custom-call | flops 40000000000 | bytes 12000000 | tf_op jit(solution)/shard_map/block_forward/pallas_call | solution.py:317
  155.1 5.1 %place.6 = bf16[32,24,3456]{2,1,0:T(8,128)(2,1)} custom-call(s32[1]{0:T(128)} %bitcast.1.me_ref, bf16[4,24,3456]{2,1,0:T(8,128)(2,1)} %copy-done.3, bf16[4,24,3456]{2,1,0:T(8,128)(2,1)} %copy-done.5, bf16[4,24,3456]{2,1,0:T(8,128)(2,1)} %copy-done.6, bf16[2,24,3456]{2,1,0:T(8,128)(2,1)} %copy-done.19, bf16[2,24,3456]{2,1,0:T(8,128)(2,1)} %copy-done.21, ...), custom_call_target="tpu_custom_call" | custom-call | bytes 10000000 | tf_op jit(solution)/shard_map/place/pallas_call | solution.py:386
  160.2 11.9 %block_forward.3 = (f32[128,768]{1,0:T(8,128)}, f32[128,3456]{1,0:T(8,128)}, f32[128,1536]{1,0:T(8,128)}, bf16[128,768]{1,0:T(8,128)(2,1)}, bf16[128,1536]{1,0:T(8,128)(2,1)}) custom-call(f32[128,768]{1,0:T(8,128)} %get-tuple-element.33.resid_ref, bf16[768,3456]{1,0:T(8,128)(2,1)} %bitcast.202, bf16[1536,768]{1,0:T(8,128)(2,1)} %bitcast.206, ...), custom_call_target="tpu_custom_call" | custom-call | flops 40000000000 | bytes 12000000 | tf_op jit(solution)/shard_map/block_forward/pallas_call | solution.py:317
  172.1 1.9 convert_multiply_fusion
  174.0 22.8 %block_backward.2 = (f32[128,768]{1,0:T(8,128)}, bf16[4,4,24,3456]{3,2,1,0:T(8,128)(2,1)}, bf16[4,4,24,3456]{3,2,1,0:T(8,128)(2,1)}, bf16[4,4,48,768]{3,2,1,0:T(...) custom-call(s32[1]{0:T(128)} %bitcast.1.me_ref, f32[128,768]{1,0:T(8,128)} %get-tuple-element.97.grad_ref, ...), custom_call_target="tpu_custom_call" | custom-call | flops 60000002048 | bytes 24000000 | tf_op jit(solution)/shard_map/block_backward/pallas_call | solution.py:339
  196.9 22.9 %block_backward.3 = (f32[128,768]{1,0:T(8,128)}, bf16[4,4,24,3456]{3,2,1,0:T(8,128)(2,1)}, bf16[4,4,24,3456]{3,2,1,0:T(8,128)(2,1)}, bf16[4,4,48,768]{3,2,1,0:T(...) custom-call(s32[1]{0:T(128)} %bitcast.1.me_ref, f32[128,768]{1,0:T(8,128)} %get-tuple-element.39.grad_ref, ...), custom_call_target="tpu_custom_call" | custom-call | flops 60000002048 | bytes 24000000 | tf_op jit(solution)/shard_map/block_backward/pallas_call | solution.py:339
  223.5 5.0 %collective-permute-done.50 = f32[2,8,1792]{2,1,0:T(8,128)S(1)} collective-permute-done((f32[2,8,1792]{2,1,0:T(8,128)S(1)}, f32[2,8,1792]{2,1,0:T(8,128)S(1)}, u32[]{:S(2)}, u32[]{:S(2)}) %collective-permute-start.50) | collective-permute-done | bytes 114720 | tf_op jit(solution)/shard_map/ppermute | solution.py:362
  230.1 4.1 %collective-permute-done.51 = f32[2,8,1792]{2,1,0:T(8,128)S(1)} collective-permute-done((f32[2,8,1792]{2,1,0:T(8,128)S(1)}, f32[2,8,1792]{2,1,0:T(8,128)S(1)}, u32[]{:S(2)}, u32[]{:S(2)}) %collective-permute-start.51) | collective-permute-done | bytes 114720 | tf_op jit(solution)/shard_map/ppermute | solution.py:362
  234.4 4.7 %collective-permute-done.52 = f32[2,8,1792]{2,1,0:T(8,128)S(1)} collective-permute-done((f32[2,8,1792]{2,1,0:T(8,128)S(1)}, f32[2,8,1792]{2,1,0:T(8,128)S(1)}, u32[]{:S(2)}, u32[]{:S(2)}) %collective-permute-start.52) | collective-permute-done | bytes 114720 | tf_op jit(solution)/shard_map/ppermute | solution.py:362
  241.4 5.3 %collective-permute-done.53 = f32[2,8,1792]{2,1,0:T(8,128)} collective-permute-done((f32[2,8,1792]{2,1,0:T(8,128)}, f32[2,8,1792]{2,1,0:T(8,128)}, u32[]{:S(2)}, u32[]{:S(2)}) %collective-permute-start.53) | collective-permute-done | bytes 114720 | tf_op jit(solution)/shard_map/ppermute | solution.py:362
  251.7 1.3 fusion.38
  253.0 1.4 collective-permute-start.69
  254.4 2.9 collective-permute-done.76
  261.0 1.4 collective-permute-done.71
  265.3 1.4 collective-permute-done.79
  268.5 1.4 reduce_sum.9
  271.7 2.0 collective-permute-done.70
  275.7 5.4 %collective-permute-done.80 = bf16[2,48,768]{2,1,0:T(8,128)(2,1)S(1)} collective-permute-done((bf16[2,48,768]{2,1,0:T(8,128)(2,1)S(1)}, bf16[2,48,768]{2,1,0:T(8,128)(2,1)S(1)}, u32[]{:S(2)}, u32[]{:S(2)}) %collective-permute-start.80) | collective-permute-done | bytes 147488 | tf_op jit(solution)/shard_map/ppermute | solution.py:362
  283.7 1.5 collective-permute-start.74
  285.3 1.2 collective-permute-done.81
  289.9 1.7 fusion.12
  293.4 1.6 fusion.8
  295.9 1.5 collective-permute-start.57
  297.4 5.0 %collective-permute-done.62 = bf16[2,24,3456]{2,1,0:T(8,128)(2,1)S(1)} collective-permute-done((bf16[2,24,3456]{2,1,0:T(8,128)(2,1)S(1)}, bf16[2,24,3456]{2,1,0:T(8,128)(2,1)S(1)}, u32[]{:S(2)}, u32[]{:S(2)}) %collective-permute-start.62) | collective-permute-done | bytes 331808 | tf_op jit(solution)/shard_map/ppermute | solution.py:362
  302.4 1.3 fusion.3
  303.8 2.1 collective-permute-start.65
  306.6 3.0 collective-permute-done.55
  309.6 1.3 fusion.7
  311.0 2.1 collective-permute-start.58
  313.7 10.1 %collective-permute-done.65 = bf16[4,24,3456]{2,1,0:T(8,128)(2,1)S(1)} collective-permute-done((bf16[4,24,3456]{2,1,0:T(8,128)(2,1)S(1)}, bf16[4,24,3456]{2,1,0:T(8,128)(2,1)S(1)}, u32[]{:S(2)}, u32[]{:S(2)}) %collective-permute-start.65) | collective-permute-done | bytes 663584 | tf_op jit(solution)/shard_map/ppermute | solution.py:362
  325.1 1.5 collective-permute-start.66
  326.6 5.5 %collective-permute-done.58 = bf16[4,24,3456]{2,1,0:T(8,128)(2,1)S(1)} collective-permute-done((bf16[4,24,3456]{2,1,0:T(8,128)(2,1)S(1)}, bf16[4,24,3456]{2,1,0:T(8,128)(2,1)S(1)}, u32[]{:S(2)}, u32[]{:S(2)}) %collective-permute-start.58) | collective-permute-done | bytes 663584 | tf_op jit(solution)/shard_map/ppermute | solution.py:362
  334.6 12.2 %collective-permute-done.66 = bf16[2,24,3456]{2,1,0:T(8,128)(2,1)S(1)} collective-permute-done((bf16[2,24,3456]{2,1,0:T(8,128)(2,1)S(1)}, bf16[2,24,3456]{2,1,0:T(8,128)(2,1)S(1)}, u32[]{:S(2)}, u32[]{:S(2)}) %collective-permute-start.66) | collective-permute-done | bytes 331808 | tf_op jit(solution)/shard_map/ppermute | solution.py:362
  347.9 3.0 collective-permute-done.59
  352.0 2.7 collective-permute-done.67
  355.8 1.6 collective-permute-done.60
  (300 shorter events, 86.8 us)
Async XLA Ops:
  7.4 17.3 %collective-permute-start = (bf16[1,24,3456]{2,1,0:T(8,128)(2,1)S(1)}, bf16[1,24,3456]{2,1,0:T(8,128)(2,1)S(1)}, u32[]{:S(2)}, u32[]{:S(2)}) collective-permute-start(bf16[1,24,3456]{2,1,0:T(8,128)(2,1)S(1)} %get-tuple-element.80), channel_id=1, source_target_pairs={{0,8},{1,9},{2,10},{3,11},{4,12},{5,13},{6,14},{7,15},{8,0},{9,1},... | collective-permute-start | bytes 497672 | tf_op jit(solution)/shard_map/ppermute | solution.py:362
  12.6 24.7 %collective-permute-start.27 = (bf16[1,24,3456]{2,1,0:T(8,128)(2,1)S(1)}, bf16[1,24,3456]{2,1,0:T(8,128)(2,1)S(1)}, u32[]{:S(2)}, u32[]{:S(2)}) collective-permute-start(bf16[1,24,3456]{2,1,0:T(8,128)(2,1)S(1)} %get-tuple-element.79), channel_id=1, source_target_pairs={{0,8},{1,9},{2,10},{3,11},{4,12},{5,13},{6,14},{7,15},{8,0},{9,1},... | collective-permute-start | bytes 497672 | tf_op jit(solution)/shard_map/ppermute | solution.py:362
  13.6 8.9 %collective-permute-start.38 = (bf16[1,48,768]{2,1,0:T(8,128)(2,1)S(1)}, bf16[1,48,768]{2,1,0:T(8,128)(2,1)S(1)}, u32[]{:S(2)}, u32[]{:S(2)}) collective-permute-start(bf16[1,48,768]{2,1,0:T(8,128)(2,1)S(1)} %get-tuple-element.81), channel_id=1, source_target_pairs={{0,8},{1,9},{2,10},{3,11},{4,12},{5,13},{6,14},{7,15},{8,0},{9,1},... | collective-permute-start | bytes 221192 | tf_op jit(solution)/shard_map/ppermute | solution.py:362
  14.7 25.0 %collective-permute-start.25 = (bf16[8,2,352]{2,1,0:T(2,128)(2,1)S(1)}, bf16[8,2,352]{2,1,0:T(2,128)(2,1)S(1)}, u32[]{:S(2)}, u32[]{:S(2)}) collective-permute-start(bf16[8,2,352]{2,1,0:T(2,128)(2,1)S(1)} %broadcast_select_fusion.2), channel_id=1, source_target_pairs={{0,8},{1,9},{2,10},{3,11},{4,12},{5,13},{6,14},{7,15},{8,0},{9,1},... | collective-permute-start | bytes 33800 | tf_op jit(solution)/shard_map/ppermute | solution.py:362
  16.8 19.6 %collective-permute-start.12 = (bf16[2,48,768]{2,1,0:T(8,128)(2,1)S(1)}, bf16[2,48,768]{2,1,0:T(8,128)(2,1)S(1)}, u32[]{:S(2)}, u32[]{:S(2)}) collective-permute-start(bf16[2,48,768]{2,1,0:T(8,128)(2,1)S(1)} %pad_maximum_fusion.16), channel_id=1, source_target_pairs={{0,16},{1,17},{2,18},{3,19},{4,20},{5,21},{6,22},{7,23},{8,24},{9,... | collective-permute-start | bytes 442376 | tf_op jit(solution)/shard_map/ppermute | solution.py:362
  22.6 17.0 %collective-permute-start.39 = (bf16[2,48,768]{2,1,0:T(8,128)(2,1)S(1)}, bf16[2,48,768]{2,1,0:T(8,128)(2,1)S(1)}, u32[]{:S(2)}, u32[]{:S(2)}) collective-permute-start(bf16[2,48,768]{2,1,0:T(8,128)(2,1)S(1)} %pad_maximum_fusion.17), channel_id=1, source_target_pairs={{0,16},{1,17},{2,18},{3,19},{4,20},{5,21},{6,22},{7,23},{8,24},{9,... | collective-permute-start | bytes 442376 | tf_op jit(solution)/shard_map/ppermute | solution.py:362
  24.7 38.3 %collective-permute-start.1 = (bf16[2,24,3456]{2,1,0:T(8,128)(2,1)S(1)}, bf16[2,24,3456]{2,1,0:T(8,128)(2,1)}, u32[]{:S(2)}, u32[]{:S(2)}) collective-permute-start(bf16[2,24,3456]{2,1,0:T(8,128)(2,1)S(1)} %pad_maximum_fusion.7), channel_id=1, source_target_pairs={{0,16},{1,17},{2,18},{3,19},{4,20},{5,21},{6,22},{7,23},{8,24},{9,... | collective-permute-start | bytes 995336 | tf_op jit(solution)/shard_map/ppermute | solution.py:362
  36.5 8.1 %collective-permute-start.13 = (bf16[4,48,768]{2,1,0:T(8,128)(2,1)S(1)}, bf16[4,48,768]{2,1,0:T(8,128)(2,1)S(1)}, u32[]{:S(2)}, u32[]{:S(2)}) collective-permute-start(bf16[4,48,768]{2,1,0:T(8,128)(2,1)S(1)} %pad_maximum_fusion.9.refs_0_), channel_id=1, source_target_pairs={{0,2},{1,3},{2,0},{3,1},{4,6},{5,7},{6,4},{7,5},{8,10},{9,11},{10,... | collective-permute-start | bytes 884744 | tf_op jit(solution)/shard_map/ppermute | solution.py:362
  37.4 8.4 %collective-permute-start.14 = (bf16[4,48,768]{2,1,0:T(8,128)(2,1)S(1)}, bf16[4,48,768]{2,1,0:T(8,128)(2,1)S(1)}, u32[]{:S(2)}, u32[]{:S(2)}) collective-permute-start(bf16[4,48,768]{2,1,0:T(8,128)(2,1)S(1)} %pad_maximum_fusion.9.refs_0_), channel_id=1, source_target_pairs={{0,4},{1,5},{2,6},{3,7},{4,0},{5,1},{6,2},{7,3},{8,12},{9,13},{10,... | collective-permute-start | bytes 884744 | tf_op jit(solution)/shard_map/ppermute | solution.py:362
  39.6 24.0 %collective-permute-start.28 = (bf16[2,24,3456]{2,1,0:T(8,128)(2,1)S(1)}, bf16[2,24,3456]{2,1,0:T(8,128)(2,1)S(1)}, u32[]{:S(2)}, u32[]{:S(2)}) collective-permute-start(bf16[2,24,3456]{2,1,0:T(8,128)(2,1)S(1)} %pad_maximum_fusion.8), channel_id=1, source_target_pairs={{0,16},{1,17},{2,18},{3,19},{4,20},{5,21},{6,22},{7,23},{8,24},{9,... | collective-permute-start | bytes 995336 | tf_op jit(solution)/shard_map/ppermute | solution.py:362
  39.7 10.0 %collective-permute-start.40 = (bf16[4,48,768]{2,1,0:T(8,128)(2,1)S(1)}, bf16[4,48,768]{2,1,0:T(8,128)(2,1)}, u32[]{:S(2)}, u32[]{:S(2)}) collective-permute-start(bf16[4,48,768]{2,1,0:T(8,128)(2,1)S(1)} %pad_maximum_fusion.10.refs_0_), channel_id=1, source_target_pairs={{0,2},{1,3},{2,0},{3,1},{4,6},{5,7},{6,4},{7,5},{8,10},{9,11},{10,... | collective-permute-start | bytes 884744 | tf_op jit(solution)/shard_map/ppermute | solution.py:362
  44.5 7.4 %collective-permute-start.41 = (bf16[4,48,768]{2,1,0:T(8,128)(2,1)S(1)}, bf16[4,48,768]{2,1,0:T(8,128)(2,1)S(1)}, u32[]{:S(2)}, u32[]{:S(2)}) collective-permute-start(bf16[4,48,768]{2,1,0:T(8,128)(2,1)S(1)} %pad_maximum_fusion.10.refs_0_), channel_id=1, source_target_pairs={{0,4},{1,5},{2,6},{3,7},{4,0},{5,1},{6,2},{7,3},{8,12},{9,13},{10,... | collective-permute-start | bytes 884744 | tf_op jit(solution)/shard_map/ppermute | solution.py:362
  45.8 18.8 %collective-permute-start.17 = (bf16[4,48,768]{2,1,0:T(8,128)(2,1)S(1)}, bf16[4,48,768]{2,1,0:T(8,128)(2,1)}, u32[]{:S(2)}, u32[]{:S(2)}) collective-permute-start(bf16[4,48,768]{2,1,0:T(8,128)(2,1)S(1)} %pad_maximum_fusion.9.refs_0_), channel_id=1, source_target_pairs={{0,1},{1,0},{2,3},{3,2},{4,5},{5,4},{6,7},{7,6},{8,9},{9,8},{10,11... | collective-permute-start | bytes 884744 | tf_op jit(solution)/shard_map/ppermute | solution.py:362
  49.7 12.0 %collective-permute-start.26 = (bf16[16,2,352]{2,1,0:T(2,128)(2,1)S(1)}, bf16[16,2,352]{2,1,0:T(2,128)(2,1)S(1)}, u32[]{:S(2)}, u32[]{:S(2)}) collective-permute-start(bf16[16,2,352]{2,1,0:T(2,128)(2,1)S(1)} %broadcast_select_fusion.1), channel_id=1, source_target_pairs={{0,16},{1,17},{2,18},{3,19},{4,20},{5,21},{6,22},{7,23},{8,24},{9,... | collective-permute-start | bytes 67592 | tf_op jit(solution)/shard_map/ppermute | solution.py:362
  51.9 14.9 %collective-permute-start.44 = (bf16[4,48,768]{2,1,0:T(8,128)(2,1)S(1)}, bf16[4,48,768]{2,1,0:T(8,128)(2,1)S(1)}, u32[]{:S(2)}, u32[]{:S(2)}) collective-permute-start(bf16[4,48,768]{2,1,0:T(8,128)(2,1)S(1)} %pad_maximum_fusion.10.refs_0_), channel_id=1, source_target_pairs={{0,1},{1,0},{2,3},{3,2},{4,5},{5,4},{6,7},{7,6},{8,9},{9,8},{10,11... | collective-permute-start | bytes 884744 | tf_op jit(solution)/shard_map/ppermute | solution.py:362
  61.7 6.7 %collective-permute-start.15 = (bf16[2,48,768]{2,1,0:T(8,128)(2,1)S(1)}, bf16[2,48,768]{2,1,0:T(8,128)(2,1)S(1)}, u32[]{:S(2)}, u32[]{:S(2)}) collective-permute-start(bf16[2,48,768]{2,1,0:T(8,128)(2,1)S(1)} %slice.568), channel_id=1, source_target_pairs={{0,4},{1,5},{2,6},{3,7},{4,0},{5,1},{6,2},{7,3},{8,12},{9,13},{10,... | collective-permute-start | bytes 442376 | tf_op jit(solution)/shard_map/ppermute | solution.py:362
  63.0 6.8 %collective-permute-start.16 = (bf16[2,48,768]{2,1,0:T(8,128)(2,1)S(1)}, bf16[2,48,768]{2,1,0:T(8,128)(2,1)S(1)}, u32[]{:S(2)}, u32[]{:S(2)}) collective-permute-start(bf16[2,48,768]{2,1,0:T(8,128)(2,1)S(1)} %slice.569), channel_id=1, source_target_pairs={{0,2},{1,3},{2,0},{3,1},{4,6},{5,7},{6,4},{7,5},{8,10},{9,11},{10,... | collective-permute-start | bytes 442376 | tf_op jit(solution)/shard_map/ppermute | solution.py:362
  63.5 7.0 %collective-permute-start.42 = (bf16[2,48,768]{2,1,0:T(8,128)(2,1)S(1)}, bf16[2,48,768]{2,1,0:T(8,128)(2,1)}, u32[]{:S(2)}, u32[]{:S(2)}) collective-permute-start(bf16[2,48,768]{2,1,0:T(8,128)(2,1)S(1)} %slice.577), channel_id=1, source_target_pairs={{0,4},{1,5},{2,6},{3,7},{4,0},{5,1},{6,2},{7,3},{8,12},{9,13},{10,... | collective-permute-start | bytes 442376 | tf_op jit(solution)/shard_map/ppermute | solution.py:362
  64.5 8.4 %collective-permute-start.43 = (bf16[2,48,768]{2,1,0:T(8,128)(2,1)S(1)}, bf16[2,48,768]{2,1,0:T(8,128)(2,1)S(1)}, u32[]{:S(2)}, u32[]{:S(2)}) collective-permute-start(bf16[2,48,768]{2,1,0:T(8,128)(2,1)S(1)} %slice.578), channel_id=1, source_target_pairs={{0,2},{1,3},{2,0},{3,1},{4,6},{5,7},{6,4},{7,5},{8,10},{9,11},{10,... | collective-permute-start | bytes 442376 | tf_op jit(solution)/shard_map/ppermute | solution.py:362
  66.8 20.3 %collective-permute-start.2 = (bf16[4,24,3456]{2,1,0:T(8,128)(2,1)S(1)}, bf16[4,24,3456]{2,1,0:T(8,128)(2,1)S(1)}, u32[]{:S(2)}, u32[]{:S(2)}) collective-permute-start(bf16[4,24,3456]{2,1,0:T(8,128)(2,1)S(1)} %pad_maximum_fusion.refs_0_), channel_id=1, source_target_pairs={{0,2},{1,3},{2,0},{3,1},{4,6},{5,7},{6,4},{7,5},{8,10},{9,11},{10,... | collective-permute-start | bytes 1990664 | tf_op jit(solution)/shard_map/ppermute | solution.py:362
  70.5 7.4 %collective-permute-start.45 = (bf16[4,48,768]{2,1,0:T(8,128)(2,1)}, bf16[4,48,768]{2,1,0:T(8,128)(2,1)S(1)}, u32[]{:S(2)}, u32[]{:S(2)}) collective-permute-start(bf16[4,48,768]{2,1,0:T(8,128)(2,1)} %collective-permute-done.40.refs_1_), channel_id=1, source_target_pairs={{0,1},{1,0},{2,3},{3,2},{4,5},{5,4},{6,7},{7,6},{8,9},{9,8},{10,11... | collective-permute-start | bytes 884744 | tf_op jit(solution)/shard_map/ppermute | solution.py:362
  74.1 17.9 %collective-permute-start.3 = (bf16[4,24,3456]{2,1,0:T(8,128)(2,1)S(1)}, bf16[4,24,3456]{2,1,0:T(8,128)(2,1)}, u32[]{:S(2)}, u32[]{:S(2)}) collective-permute-start(bf16[4,24,3456]{2,1,0:T(8,128)(2,1)S(1)} %pad_maximum_fusion.refs_0_), channel_id=1, source_target_pairs={{0,4},{1,5},{2,6},{3,7},{4,0},{5,1},{6,2},{7,3},{8,12},{9,13},{10,... | collective-permute-start | bytes 1990664 | tf_op jit(solution)/shard_map/ppermute | solution.py:362
  74.9 25.0 %collective-permute-start.29 = (bf16[4,24,3456]{2,1,0:T(8,128)(2,1)S(1)}, bf16[4,24,3456]{2,1,0:T(8,128)(2,1)S(1)}, u32[]{:S(2)}, u32[]{:S(2)}) collective-permute-start(bf16[4,24,3456]{2,1,0:T(8,128)(2,1)S(1)} %pad_maximum_fusion.1.refs_0_), channel_id=1, source_target_pairs={{0,2},{1,3},{2,0},{3,1},{4,6},{5,7},{6,4},{7,5},{8,10},{9,11},{10,... | collective-permute-start | bytes 1990664 | tf_op jit(solution)/shard_map/ppermute | solution.py:362
  77.2 27.3 %collective-permute-start.6 = (bf16[4,24,3456]{2,1,0:T(8,128)(2,1)S(1)}, bf16[4,24,3456]{2,1,0:T(8,128)(2,1)}, u32[]{:S(2)}, u32[]{:S(2)}) collective-permute-start(bf16[4,24,3456]{2,1,0:T(8,128)(2,1)S(1)} %pad_maximum_fusion.refs_0_), channel_id=1, source_target_pairs={{0,1},{1,0},{2,3},{3,2},{4,5},{5,4},{6,7},{7,6},{8,9},{9,8},{10,11... | collective-permute-start | bytes 1990664 | tf_op jit(solution)/shard_map/ppermute | solution.py:362
  77.9 28.2 %collective-permute-start.30 = (bf16[4,24,3456]{2,1,0:T(8,128)(2,1)S(1)}, bf16[4,24,3456]{2,1,0:T(8,128)(2,1)S(1)}, u32[]{:S(2)}, u32[]{:S(2)}) collective-permute-start(bf16[4,24,3456]{2,1,0:T(8,128)(2,1)S(1)} %pad_maximum_fusion.1.refs_0_), channel_id=1, source_target_pairs={{0,4},{1,5},{2,6},{3,7},{4,0},{5,1},{6,2},{7,3},{8,12},{9,13},{10,... | collective-permute-start | bytes 1990664 | tf_op jit(solution)/shard_map/ppermute | solution.py:362
  87.2 14.0 %collective-permute-start.46 = (bf16[4,48,768]{2,1,0:T(8,128)(2,1)}, bf16[4,48,768]{2,1,0:T(8,128)(2,1)}, u32[]{:S(2)}, u32[]{:S(2)}) collective-permute-start(bf16[4,48,768]{2,1,0:T(8,128)(2,1)} %copy-done.14), channel_id=1, source_target_pairs={{0,1},{1,0},{2,3},{3,2},{4,5},{5,4},{6,7},{7,6},{8,9},{9,8},{10,11... | collective-permute-start | bytes 884744 | tf_op jit(solution)/shard_map/ppermute | solution.py:362
  92.0 10.0 %collective-permute-start.47 = (bf16[2,48,768]{2,1,0:T(8,128)(2,1)}, bf16[2,48,768]{2,1,0:T(8,128)(2,1)S(1)}, u32[]{:S(2)}, u32[]{:S(2)}) collective-permute-start(bf16[2,48,768]{2,1,0:T(8,128)(2,1)} %collective-permute-done.42.refs_3_), channel_id=1, source_target_pairs={{0,1},{1,0},{2,3},{3,2},{4,5},{5,4},{6,7},{7,6},{8,9},{9,8},{10,11... | collective-permute-start | bytes 442376 | tf_op jit(solution)/shard_map/ppermute | solution.py:362
  101.1 12.2 %collective-permute-start.4 = (bf16[2,24,3456]{2,1,0:T(8,128)(2,1)S(1)}, bf16[2,24,3456]{2,1,0:T(8,128)(2,1)}, u32[]{:S(2)}, u32[]{:S(2)}) collective-permute-start(bf16[2,24,3456]{2,1,0:T(8,128)(2,1)S(1)} %slice.566), channel_id=1, source_target_pairs={{0,4},{1,5},{2,6},{3,7},{4,0},{5,1},{6,2},{7,3},{8,12},{9,13},{10,... | collective-permute-start | bytes 995336 | tf_op jit(solution)/shard_map/ppermute | solution.py:362
  102.0 11.6 %collective-permute-start.5 = (bf16[2,24,3456]{2,1,0:T(8,128)(2,1)S(1)}, bf16[2,24,3456]{2,1,0:T(8,128)(2,1)}, u32[]{:S(2)}, u32[]{:S(2)}) collective-permute-start(bf16[2,24,3456]{2,1,0:T(8,128)(2,1)S(1)} %slice.567), channel_id=1, source_target_pairs={{0,2},{1,3},{2,0},{3,1},{4,6},{5,7},{6,4},{7,5},{8,10},{9,11},{10,... | collective-permute-start | bytes 995336 | tf_op jit(solution)/shard_map/ppermute | solution.py:362
  102.7 17.2 %collective-permute-start.31 = (bf16[2,24,3456]{2,1,0:T(8,128)(2,1)S(1)}, bf16[2,24,3456]{2,1,0:T(8,128)(2,1)S(1)}, u32[]{:S(2)}, u32[]{:S(2)}) collective-permute-start(bf16[2,24,3456]{2,1,0:T(8,128)(2,1)S(1)} %slice.575), channel_id=1, source_target_pairs={{0,4},{1,5},{2,6},{3,7},{4,0},{5,1},{6,2},{7,3},{8,12},{9,13},{10,... | collective-permute-start | bytes 995336 | tf_op jit(solution)/shard_map/ppermute | solution.py:362
  104.5 30.0 %collective-permute-start.7 = (bf16[4,24,3456]{2,1,0:T(8,128)(2,1)S(1)}, bf16[4,24,3456]{2,1,0:T(8,128)(2,1)}, u32[]{:S(2)}, u32[]{:S(2)}) collective-permute-start(bf16[4,24,3456]{2,1,0:T(8,128)(2,1)S(1)} %collective-permute-done.2.refs_1_), channel_id=1, source_target_pairs={{0,1},{1,0},{2,3},{3,2},{4,5},{5,4},{6,7},{7,6},{8,9},{9,8},{10,11... | collective-permute-start | bytes 1990664 | tf_op jit(solution)/shard_map/ppermute | solution.py:362
  106.1 28.8 %collective-permute-start.8 = (bf16[4,24,3456]{2,1,0:T(8,128)(2,1)}, bf16[4,24,3456]{2,1,0:T(8,128)(2,1)}, u32[]{:S(2)}, u32[]{:S(2)}) collective-permute-start(bf16[4,24,3456]{2,1,0:T(8,128)(2,1)} %collective-permute-done.3.refs_2_), channel_id=1, source_target_pairs={{0,1},{1,0},{2,3},{3,2},{4,5},{5,4},{6,7},{7,6},{8,9},{9,8},{10,11... | collective-permute-start | bytes 1990664 | tf_op jit(solution)/shard_map/ppermute | solution.py:362
  113.3 21.0 %collective-permute-start.32 = (bf16[2,24,3456]{2,1,0:T(8,128)(2,1)}, bf16[2,24,3456]{2,1,0:T(8,128)(2,1)S(1)}, u32[]{:S(2)}, u32[]{:S(2)}) collective-permute-start(bf16[2,24,3456]{2,1,0:T(8,128)(2,1)} %slice.576), channel_id=1, source_target_pairs={{0,2},{1,3},{2,0},{3,1},{4,6},{5,7},{6,4},{7,5},{8,10},{9,11},{10,... | collective-permute-start | bytes 995336 | tf_op jit(solution)/shard_map/ppermute | solution.py:362
  113.6 21.4 %collective-permute-start.9 = (bf16[2,24,3456]{2,1,0:T(8,128)(2,1)}, bf16[2,24,3456]{2,1,0:T(8,128)(2,1)S(1)}, u32[]{:S(2)}, u32[]{:S(2)}) collective-permute-start(bf16[2,24,3456]{2,1,0:T(8,128)(2,1)} %collective-permute-done.4.refs_3_), channel_id=1, source_target_pairs={{0,1},{1,0},{2,3},{3,2},{4,5},{5,4},{6,7},{7,6},{8,9},{9,8},{10,11... | collective-permute-start | bytes 995336 | tf_op jit(solution)/shard_map/ppermute | solution.py:362
  119.9 15.6 %collective-permute-start.10 = (bf16[2,24,3456]{2,1,0:T(8,128)(2,1)}, bf16[2,24,3456]{2,1,0:T(8,128)(2,1)}, u32[]{:S(2)}, u32[]{:S(2)}) collective-permute-start(bf16[2,24,3456]{2,1,0:T(8,128)(2,1)} %collective-permute-done.5.refs_4_), channel_id=1, source_target_pairs={{0,1},{1,0},{2,3},{3,2},{4,5},{5,4},{6,7},{7,6},{8,9},{9,8},{10,11... | collective-permute-start | bytes 995336 | tf_op jit(solution)/shard_map/ppermute | solution.py:362
  134.3 18.6 %collective-permute-start.33 = (bf16[4,24,3456]{2,1,0:T(8,128)(2,1)S(1)}, bf16[4,24,3456]{2,1,0:T(8,128)(2,1)S(1)}, u32[]{:S(2)}, u32[]{:S(2)}) collective-permute-start(bf16[4,24,3456]{2,1,0:T(8,128)(2,1)S(1)} %pad_maximum_fusion.1.refs_0_), channel_id=1, source_target_pairs={{0,1},{1,0},{2,3},{3,2},{4,5},{5,4},{6,7},{7,6},{8,9},{9,8},{10,11... | collective-permute-start | bytes 1990664 | tf_op jit(solution)/shard_map/ppermute | solution.py:362
  134.5 18.5 %collective-permute-start.34 = (bf16[4,24,3456]{2,1,0:T(8,128)(2,1)S(1)}, bf16[4,24,3456]{2,1,0:T(8,128)(2,1)S(1)}, u32[]{:S(2)}, u32[]{:S(2)}) collective-permute-start(bf16[4,24,3456]{2,1,0:T(8,128)(2,1)S(1)} %collective-permute-done.29.refs_1_), channel_id=1, source_target_pairs={{0,1},{1,0},{2,3},{3,2},{4,5},{5,4},{6,7},{7,6},{8,9},{9,8},{10,11... | collective-permute-start | bytes 1990664 | tf_op jit(solution)/shard_map/ppermute | solution.py:362
  134.9 18.1 %collective-permute-start.35 = (bf16[4,24,3456]{2,1,0:T(8,128)(2,1)S(1)}, bf16[4,24,3456]{2,1,0:T(8,128)(2,1)S(1)}, u32[]{:S(2)}, u32[]{:S(2)}) collective-permute-start(bf16[4,24,3456]{2,1,0:T(8,128)(2,1)S(1)} %collective-permute-done.30.refs_2_), channel_id=1, source_target_pairs={{0,1},{1,0},{2,3},{3,2},{4,5},{5,4},{6,7},{7,6},{8,9},{9,8},{10,11... | collective-permute-start | bytes 1990664 | tf_op jit(solution)/shard_map/ppermute | solution.py:362
  135.0 18.0 %collective-permute-start.36 = (bf16[2,24,3456]{2,1,0:T(8,128)(2,1)S(1)}, bf16[2,24,3456]{2,1,0:T(8,128)(2,1)S(1)}, u32[]{:S(2)}, u32[]{:S(2)}) collective-permute-start(bf16[2,24,3456]{2,1,0:T(8,128)(2,1)S(1)} %copy-done.20), channel_id=1, source_target_pairs={{0,1},{1,0},{2,3},{3,2},{4,5},{5,4},{6,7},{7,6},{8,9},{9,8},{10,11... | collective-permute-start | bytes 995336 | tf_op jit(solution)/shard_map/ppermute | solution.py:362
  135.5 17.5 %collective-permute-start.37 = (bf16[2,24,3456]{2,1,0:T(8,128)(2,1)S(1)}, bf16[2,24,3456]{2,1,0:T(8,128)(2,1)S(1)}, u32[]{:S(2)}, u32[]{:S(2)}) collective-permute-start(bf16[2,24,3456]{2,1,0:T(8,128)(2,1)S(1)} %collective-permute-done.32.refs_4_), channel_id=1, source_target_pairs={{0,1},{1,0},{2,3},{3,2},{4,5},{5,4},{6,7},{7,6},{8,9},{9,8},{10,11... | collective-permute-start | bytes 995336 | tf_op jit(solution)/shard_map/ppermute | solution.py:362
  223.4 26.9 %collective-permute-start.75 = (bf16[4,4,48,768]{3,2,1,0:T(8,128)(2,1)}, bf16[4,4,48,768]{3,2,1,0:T(8,128)(2,1)S(1)}, u32[]{:S(2)}, u32[]{:S(2)}) collective-permute-start(bf16[4,4,48,768]{3,2,1,0:T(8,128)(2,1)} %get-tuple-element.54), channel_id=1, source_target_pairs={{0,1},{1,0},{2,3},{3,2},{4,5},{5,4},{6,7},{7,6},{8,9},{9,8},{10,11... | collective-permute-start | bytes 3538952 | tf_op jit(solution)/shard_map/ppermute | solution.py:362
  234.3 17.4 %collective-permute-start.68 = (bf16[4,4,48,768]{3,2,1,0:T(8,128)(2,1)}, bf16[4,4,48,768]{3,2,1,0:T(8,128)(2,1)}, u32[]{:S(2)}, u32[]{:S(2)}) collective-permute-start(bf16[4,4,48,768]{3,2,1,0:T(8,128)(2,1)} %get-tuple-element.52), channel_id=1, source_target_pairs={{0,1},{1,0},{2,3},{3,2},{4,5},{5,4},{6,7},{7,6},{8,9},{9,8},{10,11... | collective-permute-start | bytes 3538952 | tf_op jit(solution)/shard_map/ppermute | solution.py:362
  239.8 6.9 %collective-permute-start.53 = (f32[2,8,1792]{2,1,0:T(8,128)}, f32[2,8,1792]{2,1,0:T(8,128)}, u32[]{:S(2)}, u32[]{:S(2)}) collective-permute-start(f32[2,8,1792]{2,1,0:T(8,128)} %add.430), channel_id=1, source_target_pairs={{0,16},{1,17},{2,18},{3,19},{4,20},{5,21},{6,22},{7,23},{8,24},{9,... | collective-permute-start | bytes 344072 | tf_op jit(solution)/shard_map/ppermute | solution.py:362
  240.9 49.0 %collective-permute-start.61 = (bf16[4,4,24,3456]{3,2,1,0:T(8,128)(2,1)}, bf16[4,4,24,3456]{3,2,1,0:T(8,128)(2,1)}, u32[]{:S(2)}, u32[]{:S(2)}) collective-permute-start(bf16[4,4,24,3456]{3,2,1,0:T(8,128)(2,1)} %get-tuple-element.50), channel_id=1, source_target_pairs={{0,1},{1,0},{2,3},{3,2},{4,5},{5,4},{6,7},{7,6},{8,9},{9,8},{10,11... | collective-permute-start | bytes 7962632 | tf_op jit(solution)/shard_map/ppermute | solution.py:362
  240.9 52.5 %collective-permute-start.54 = (bf16[4,4,24,3456]{3,2,1,0:T(8,128)(2,1)}, bf16[4,4,24,3456]{3,2,1,0:T(8,128)(2,1)}, u32[]{:S(2)}, u32[]{:S(2)}) collective-permute-start(bf16[4,4,24,3456]{3,2,1,0:T(8,128)(2,1)} %get-tuple-element.48), channel_id=1, source_target_pairs={{0,1},{1,0},{2,3},{3,2},{4,5},{5,4},{6,7},{7,6},{8,9},{9,8},{10,11... | collective-permute-start | bytes 7962632 | tf_op jit(solution)/shard_map/ppermute | solution.py:362
  250.5 6.8 %collective-permute-start.76 = (bf16[2,48,768]{2,1,0:T(8,128)(2,1)S(1)}, bf16[2,48,768]{2,1,0:T(8,128)(2,1)S(1)}, u32[]{:S(2)}, u32[]{:S(2)}) collective-permute-start(bf16[2,48,768]{2,1,0:T(8,128)(2,1)S(1)} %get-tuple-element.75), channel_id=1, source_target_pairs={{0,4},{1,5},{2,6},{3,7},{4,0},{5,1},{6,2},{7,3},{8,12},{9,13},{10,... | collective-permute-start | bytes 442376 | tf_op jit(solution)/shard_map/ppermute | solution.py:362
  253.0 7.4 %collective-permute-start.69 = (bf16[2,48,768]{2,1,0:T(8,128)(2,1)S(1)}, bf16[2,48,768]{2,1,0:T(8,128)(2,1)S(1)}, u32[]{:S(2)}, u32[]{:S(2)}) collective-permute-start(bf16[2,48,768]{2,1,0:T(8,128)(2,1)S(1)} %get-tuple-element.69), channel_id=1, source_target_pairs={{0,4},{1,5},{2,6},{3,7},{4,0},{5,1},{6,2},{7,3},{8,12},{9,13},{10,... | collective-permute-start | bytes 442376 | tf_op jit(solution)/shard_map/ppermute | solution.py:362
  257.4 9.3 %collective-permute-start.79 = (bf16[4,48,768]{2,1,0:T(8,128)(2,1)S(1)}, bf16[4,48,768]{2,1,0:T(8,128)(2,1)S(1)}, u32[]{:S(2)}, u32[]{:S(2)}) collective-permute-start(bf16[4,48,768]{2,1,0:T(8,128)(2,1)S(1)} %pad_maximum_fusion.14), channel_id=1, source_target_pairs={{0,4},{1,5},{2,6},{3,7},{4,0},{5,1},{6,2},{7,3},{8,12},{9,13},{10,... | collective-permute-start | bytes 884744 | tf_op jit(solution)/shard_map/ppermute | solution.py:362
  260.4 9.5 %collective-permute-start.77 = (bf16[4,48,768]{2,1,0:T(8,128)(2,1)}, bf16[4,48,768]{2,1,0:T(8,128)(2,1)S(1)}, u32[]{:S(2)}, u32[]{:S(2)}) collective-permute-start(bf16[4,48,768]{2,1,0:T(8,128)(2,1)} %pad_maximum_fusion.13), channel_id=1, source_target_pairs={{0,2},{1,3},{2,0},{3,1},{4,6},{5,7},{6,4},{7,5},{8,10},{9,11},{10,... | collective-permute-start | bytes 884744 | tf_op jit(solution)/shard_map/ppermute | solution.py:362
  264.2 7.5 %collective-permute-start.72 = (bf16[4,48,768]{2,1,0:T(8,128)(2,1)}, bf16[4,48,768]{2,1,0:T(8,128)(2,1)S(1)}, u32[]{:S(2)}, u32[]{:S(2)}) collective-permute-start(bf16[4,48,768]{2,1,0:T(8,128)(2,1)} %pad_maximum_fusion.12), channel_id=1, source_target_pairs={{0,4},{1,5},{2,6},{3,7},{4,0},{5,1},{6,2},{7,3},{8,12},{9,13},{10,... | collective-permute-start | bytes 884744 | tf_op jit(solution)/shard_map/ppermute | solution.py:362
  266.7 7.0 %collective-permute-start.70 = (bf16[4,48,768]{2,1,0:T(8,128)(2,1)}, bf16[4,48,768]{2,1,0:T(8,128)(2,1)}, u32[]{:S(2)}, u32[]{:S(2)}) collective-permute-start(bf16[4,48,768]{2,1,0:T(8,128)(2,1)} %pad_maximum_fusion.11), channel_id=1, source_target_pairs={{0,2},{1,3},{2,0},{3,1},{4,6},{5,7},{6,4},{7,5},{8,10},{9,11},{10,... | collective-permute-start | bytes 884744 | tf_op jit(solution)/shard_map/ppermute | solution.py:362
  271.0 10.1 %collective-permute-start.80 = (bf16[2,48,768]{2,1,0:T(8,128)(2,1)S(1)}, bf16[2,48,768]{2,1,0:T(8,128)(2,1)S(1)}, u32[]{:S(2)}, u32[]{:S(2)}) collective-permute-start(bf16[2,48,768]{2,1,0:T(8,128)(2,1)S(1)} %fusion.31), channel_id=1, source_target_pairs={{0,16},{1,17},{2,18},{3,19},{4,20},{5,21},{6,22},{7,23},{8,24},{9,... | collective-permute-start | bytes 442376 | tf_op jit(solution)/shard_map/ppermute | solution.py:362
  274.9 7.8 %collective-permute-start.73 = (bf16[2,48,768]{2,1,0:T(8,128)(2,1)S(1)}, bf16[2,48,768]{2,1,0:T(8,128)(2,1)S(1)}, u32[]{:S(2)}, u32[]{:S(2)}) collective-permute-start(bf16[2,48,768]{2,1,0:T(8,128)(2,1)S(1)} %fusion.35), channel_id=1, source_target_pairs={{0,16},{1,17},{2,18},{3,19},{4,20},{5,21},{6,22},{7,23},{8,24},{9,... | collective-permute-start | bytes 442376 | tf_op jit(solution)/shard_map/ppermute | solution.py:362
  291.6 10.8 %collective-permute-start.62 = (bf16[2,24,3456]{2,1,0:T(8,128)(2,1)S(1)}, bf16[2,24,3456]{2,1,0:T(8,128)(2,1)S(1)}, u32[]{:S(2)}, u32[]{:S(2)}) collective-permute-start(bf16[2,24,3456]{2,1,0:T(8,128)(2,1)S(1)} %get-tuple-element.63), channel_id=1, source_target_pairs={{0,4},{1,5},{2,6},{3,7},{4,0},{5,1},{6,2},{7,3},{8,12},{9,13},{10,... | collective-permute-start | bytes 995336 | tf_op jit(solution)/shard_map/ppermute | solution.py:362
  292.3 10.1 %collective-permute-start.64 = (bf16[2,24,3456]{2,1,0:T(8,128)(2,1)S(1)}, bf16[2,24,3456]{2,1,0:T(8,128)(2,1)S(1)}, u32[]{:S(2)}, u32[]{:S(2)}) collective-permute-start(bf16[2,24,3456]{2,1,0:T(8,128)(2,1)S(1)} %get-tuple-element.64), channel_id=1, source_target_pairs={{0,2},{1,3},{2,0},{3,1},{4,6},{5,7},{6,4},{7,5},{8,10},{9,11},{10,... | collective-permute-start | bytes 995336 | tf_op jit(solution)/shard_map/ppermute | solution.py:362
  295.0 14.5 %collective-permute-start.55 = (bf16[2,24,3456]{2,1,0:T(8,128)(2,1)S(1)}, bf16[2,24,3456]{2,1,0:T(8,128)(2,1)S(1)}, u32[]{:S(2)}, u32[]{:S(2)}) collective-permute-start(bf16[2,24,3456]{2,1,0:T(8,128)(2,1)S(1)} %get-tuple-element.57), channel_id=1, source_target_pairs={{0,4},{1,5},{2,6},{3,7},{4,0},{5,1},{6,2},{7,3},{8,12},{9,13},{10,... | collective-permute-start | bytes 995336 | tf_op jit(solution)/shard_map/ppermute | solution.py:362
  295.9 13.7 %collective-permute-start.57 = (bf16[2,24,3456]{2,1,0:T(8,128)(2,1)S(1)}, bf16[2,24,3456]{2,1,0:T(8,128)(2,1)S(1)}, u32[]{:S(2)}, u32[]{:S(2)}) collective-permute-start(bf16[2,24,3456]{2,1,0:T(8,128)(2,1)S(1)} %get-tuple-element.58), channel_id=1, source_target_pairs={{0,2},{1,3},{2,0},{3,1},{4,6},{5,7},{6,4},{7,5},{8,10},{9,11},{10,... | collective-permute-start | bytes 995336 | tf_op jit(solution)/shard_map/ppermute | solution.py:362
  303.8 19.9 %collective-permute-start.65 = (bf16[4,24,3456]{2,1,0:T(8,128)(2,1)S(1)}, bf16[4,24,3456]{2,1,0:T(8,128)(2,1)S(1)}, u32[]{:S(2)}, u32[]{:S(2)}) collective-permute-start(bf16[4,24,3456]{2,1,0:T(8,128)(2,1)S(1)} %pad_maximum_fusion.5), channel_id=1, source_target_pairs={{0,4},{1,5},{2,6},{3,7},{4,0},{5,1},{6,2},{7,3},{8,12},{9,13},{10,... | collective-permute-start | bytes 1990664 | tf_op jit(solution)/shard_map/ppermute | solution.py:362
  306.0 17.9 %collective-permute-start.63 = (bf16[4,24,3456]{2,1,0:T(8,128)(2,1)S(1)}, bf16[4,24,3456]{2,1,0:T(8,128)(2,1)S(1)}, u32[]{:S(2)}, u32[]{:S(2)}) collective-permute-start(bf16[4,24,3456]{2,1,0:T(8,128)(2,1)S(1)} %pad_maximum_fusion.4), channel_id=1, source_target_pairs={{0,2},{1,3},{2,0},{3,1},{4,6},{5,7},{6,4},{7,5},{8,10},{9,11},{10,... | collective-permute-start | bytes 1990664 | tf_op jit(solution)/shard_map/ppermute | solution.py:362
  311.0 21.2 %collective-permute-start.58 = (bf16[4,24,3456]{2,1,0:T(8,128)(2,1)S(1)}, bf16[4,24,3456]{2,1,0:T(8,128)(2,1)S(1)}, u32[]{:S(2)}, u32[]{:S(2)}) collective-permute-start(bf16[4,24,3456]{2,1,0:T(8,128)(2,1)S(1)} %pad_maximum_fusion.3), channel_id=1, source_target_pairs={{0,4},{1,5},{2,6},{3,7},{4,0},{5,1},{6,2},{7,3},{8,12},{9,13},{10,... | collective-permute-start | bytes 1990664 | tf_op jit(solution)/shard_map/ppermute | solution.py:362
  313.1 19.1 %collective-permute-start.56 = (bf16[4,24,3456]{2,1,0:T(8,128)(2,1)S(1)}, bf16[4,24,3456]{2,1,0:T(8,128)(2,1)S(1)}, u32[]{:S(2)}, u32[]{:S(2)}) collective-permute-start(bf16[4,24,3456]{2,1,0:T(8,128)(2,1)S(1)} %pad_maximum_fusion.2), channel_id=1, source_target_pairs={{0,2},{1,3},{2,0},{3,1},{4,6},{5,7},{6,4},{7,5},{8,10},{9,11},{10,... | collective-permute-start | bytes 1990664 | tf_op jit(solution)/shard_map/ppermute | solution.py:362
  325.1 21.7 %collective-permute-start.66 = (bf16[2,24,3456]{2,1,0:T(8,128)(2,1)S(1)}, bf16[2,24,3456]{2,1,0:T(8,128)(2,1)S(1)}, u32[]{:S(2)}, u32[]{:S(2)}) collective-permute-start(bf16[2,24,3456]{2,1,0:T(8,128)(2,1)S(1)} %fusion.1), channel_id=1, source_target_pairs={{0,16},{1,17},{2,18},{3,19},{4,20},{5,21},{6,22},{7,23},{8,24},{9,... | collective-permute-start | bytes 995336 | tf_op jit(solution)/shard_map/ppermute | solution.py:362
  333.4 17.5 %collective-permute-start.59 = (bf16[2,24,3456]{2,1,0:T(8,128)(2,1)S(1)}, bf16[2,24,3456]{2,1,0:T(8,128)(2,1)S(1)}, u32[]{:S(2)}, u32[]{:S(2)}) collective-permute-start(bf16[2,24,3456]{2,1,0:T(8,128)(2,1)S(1)} %fusion.5), channel_id=1, source_target_pairs={{0,16},{1,17},{2,18},{3,19},{4,20},{5,21},{6,22},{7,23},{8,24},{9,... | collective-permute-start | bytes 995336 | tf_op jit(solution)/shard_map/ppermute | solution.py:362
  347.8 6.9 %collective-permute-start.67 = (bf16[1,24,3456]{2,1,0:T(8,128)(2,1)S(1)}, bf16[1,24,3456]{2,1,0:T(8,128)(2,1)S(1)}, u32[]{:S(2)}, u32[]{:S(2)}) collective-permute-start(bf16[1,24,3456]{2,1,0:T(8,128)(2,1)S(1)} %fusion.18), channel_id=1, source_target_pairs={{0,8},{1,9},{2,10},{3,11},{4,12},{5,13},{6,14},{7,15},{8,0},{9,1},... | collective-permute-start | bytes 497672 | tf_op jit(solution)/shard_map/ppermute | solution.py:362
  (59 other events, 890.6 us)

commit v2 on v1

v2 whole, which is shorter than its diff:
```python
from functools import partial

import jax
import jax.numpy as jnp
from jax import lax
from jax.experimental import pallas as pl
from jax.experimental.pallas import tpu as pltpu
from jax.sharding import PartitionSpec as P

HEADS = 24
HEADDIM = 64
STATE = 128
CONV = 4
BLOCK = 64
WIDTH = 768
INNER = HEADS * HEADDIM
CONVCH = INNER + 2 * STATE
PROJ = INNER + CONVCH + HEADS
LANES = 128
PADDED = INNER + CONVCH + LANES
PAIRS = INNER // LANES
STEP_AT = INNER + CONVCH
SMALL_ROWS = 8
PARTS = 32
EPSILON = 1e-05
EXACT = lax.Precision.HIGHEST
F32 = jnp.float32
LOW = jnp.bfloat16
NT = (((1,), (1,)), ((), ()))
TN = (((0,), (0,)), ((), ()))
VMEM_LIMIT = 56 * 1024 * 1024


def tile(index):
    return pl.ds(pl.multiple_of(index * LANES, LANES), LANES)


def iota(shape, dim):
    return lax.broadcasted_iota(jnp.int32, shape, dim)


def split(values):
    high = values.astype(LOW)
    return high, (values - high.astype(F32)).astype(LOW)


def low_half():
    return iota((1, LANES), 1) < HEADDIM


def set_masks(seg_col, seg_row, allowed_ref, taps_ref):
    rows = seg_col.shape[0]
    t, s = iota((rows, rows), 0), iota((rows, rows), 1)
    tri = (t >= s) & (t // BLOCK == s // BLOCK)
    allowed_ref[...] = jnp.where(tri & (seg_col == seg_row), 1.0, 0.0)
    wide = jnp.broadcast_to(seg_col, (rows, LANES))
    place = iota((rows, LANES), 0) % BLOCK
    for tap in range(1, CONV):
        earlier = pltpu.roll(wide, tap, axis=0)
        taps_ref[tap - 1] = jnp.where((earlier == wide) & (place >= tap), 1.0, 0.0)
    return jnp.where(tri, 1.0, 0.0)


def conv_tile(signal, weight_ref, taps_ref, at):
    total = weight_ref[CONV : CONV + 1, at] + signal * weight_ref[CONV - 1 : CONV, at]
    for tap in range(1, CONV):
        shifted = pltpu.roll(signal, tap, axis=0) * taps_ref[tap - 1]
        total = total + shifted * weight_ref[CONV - 1 - tap : CONV - tap, at]
    return total


def steps(raw, heads_ref):
    raw = raw + heads_ref[2:3]
    step = jnp.maximum(raw, 0.0) + jnp.log1p(jnp.exp(-jnp.abs(raw)))
    return raw, step, step * -jnp.exp(heads_ref[0:1])


def spread_heads(high, low, index):
    head = iota((LANES, LANES), 0)
    lane = iota((LANES, LANES), 1)
    pick = jnp.where(head == 2 * index + lane // HEADDIM, 1.0, 0.0).astype(LOW)
    return jnp.dot(high, pick, preferred_element_type=F32) + jnp.dot(
        low, pick, preferred_element_type=F32
    )


def decays(turned_ref, allowed, head):
    rows = allowed.shape[0]
    across = jnp.broadcast_to(turned_ref[pl.ds(head, 1), :], (rows, rows))
    gaps = jnp.where(allowed > 0.0, across.T - across, -1e30)
    return jnp.exp(gaps)


def forward_kernel(
    resid_ref, in_ref, norm_ref, conv_ref, gate_ref, heads_ref, skip_ref, col_ref, row_ref,
    hidden_ref, mixed_ref, normed_ref, gated_ref,
    allowed_ref, taps_ref, turned_ref, scores_ref, product_ref,
):
    tri = set_masks(col_ref[...], row_ref[...], allowed_ref, taps_ref)
    resid = resid_ref[...]
    scale = lax.rsqrt(jnp.mean(resid * resid, axis=-1, keepdims=True) + EPSILON)
    normed_ref[...] = (resid * scale * norm_ref[...]).astype(LOW)

    def project(index, carry):
        at = pl.ds(pl.multiple_of(index * 3 * LANES, LANES), 3 * LANES)
        hidden_ref[:, at] = jnp.dot(normed_ref[...], in_ref[:, at], preferred_element_type=F32)
        return carry

    lax.fori_loop(0, PADDED // (3 * LANES), project, 0)
    raw, step, rate = steps(hidden_ref[:, STEP_AT:], heads_ref)
    turned_ref[...] = jnp.dot(tri, rate, precision=EXACT, preferred_element_type=F32).T
    high, low = split(step)
    pair = []
    for index in (0, 1):
        at = pl.ds(INNER + index * STATE, STATE)
        total = conv_tile(hidden_ref[:, pl.ds(2 * INNER + index * STATE, STATE)], conv_ref, taps_ref, at)
        pair.append(total * jax.nn.sigmoid(total))
    scores_ref[...] = lax.dot_general(pair[1], pair[0], NT, precision=EXACT, preferred_element_type=F32)
    first = low_half()

    def heads(index, squares):
        at = tile(index)
        total = conv_tile(hidden_ref[:, tile(index + PAIRS)], conv_ref, taps_ref, at)
        values = total * jax.nn.sigmoid(total)
        scaled = values * spread_heads(high, low, index)
        allowed = allowed_ref[...]
        scores = scores_ref[...]
        weights = jnp.concatenate(
            [(scores * decays(turned_ref, allowed, 2 * index + head)).astype(LOW) for head in (0, 1)], axis=1
        )
        both = jnp.concatenate([jnp.where(first, scaled, 0.0), jnp.where(first, 0.0, scaled)], axis=0).astype(LOW)
        mixed = jnp.dot(weights, both, preferred_element_type=F32)
        mixed_ref[:, at] = mixed
        gate = hidden_ref[:, at]
        product = (mixed + values * skip_ref[:, at]) * (gate * jax.nn.sigmoid(gate))
        product_ref[:, at] = product
        return squares + product * product

    squares = lax.fori_loop(0, PAIRS, heads, jnp.zeros((resid.shape[0], LANES), F32))
    scale = lax.rsqrt(jnp.sum(squares, axis=-1, keepdims=True) / INNER + EPSILON)
    gated_ref[...] = (product_ref[...] * scale * gate_ref[...]).astype(LOW)


def out_back(me_ref, grad_ref, gated_ref, out_ref, gated_grad_ref, store):
    core = me_ref[0] % 2
    chip = me_ref[0] // 2
    grad_low = grad_ref[...].astype(LOW)
    depth = INNER // PARTS
    pairs = 3 * LANES // (2 * depth)

    def step(index, carry):
        at = pl.ds(pl.multiple_of(index * 3 * LANES, LANES), 3 * LANES)
        gated_grad_ref[:, at] = lax.dot_general(grad_low, out_ref[at, :], NT, preferred_element_type=F32)
        part = lax.dot_general(gated_ref[:, at], grad_low, TN, preferred_element_type=F32)
        for pair in range(pairs):
            even = part[2 * pair * depth : (2 * pair + 1) * depth]
            odd = part[(2 * pair + 1) * depth : (2 * pair + 2) * depth]
            store((index * pairs + pair) ^ chip, jnp.where(core == 0, even, odd), jnp.where(core == 0, odd, even))
        return carry

    lax.fori_loop(0, INNER // (3 * LANES), step, 0)


def backward_out_kernel(me_ref, grad_ref, gated_ref, out_ref, gated_grad_ref, keep_ref, send_ref):
    def store(other, keep, send):
        keep_ref[other % 4, other // 4] = keep.astype(LOW)
        send_ref[other % 4, other // 4] = send.astype(LOW)

    out_back(me_ref, grad_ref, gated_ref, out_ref, gated_grad_ref, store)


def backward_mixer_kernel(
    gated_grad_ref, hidden_ref, mixed_ref, conv_ref, gate_ref, heads_ref, skip_ref, col_ref, row_ref,
    dhidden_ref, small_ref,
    allowed_ref, taps_ref, turned_ref, scores_ref, dscores_ref, values_ref, slope_ref,
):
    tri = set_masks(col_ref[...], row_ref[...], allowed_ref, taps_ref)
    rows = hidden_ref.shape[0]
    small_ref[...] = jnp.zeros_like(small_ref)
    raw, step, rate = steps(hidden_ref[:, STEP_AT:], heads_ref)
    turned_ref[...] = jnp.dot(tri, rate, precision=EXACT, preferred_element_type=F32).T
    high, low = split(step)

    def again(index, carry):
        at = tile(index)
        total = conv_tile(hidden_ref[:, tile(index + PAIRS)], conv_ref, taps_ref, at)
        sigmoid = jax.nn.sigmoid(total)
        values_ref[:, at] = total * sigmoid
        slope_ref[:, at] = sigmoid * (1.0 + total * (1.0 - sigmoid))
        return carry

    lax.fori_loop(0, PAIRS + 2, again, 0)
    inputs_b = values_ref[:, INNER : INNER + STATE]
    outputs_c = values_ref[:, INNER + STATE :]
    scores_ref[...] = lax.dot_general(outputs_c, inputs_b, NT, precision=EXACT, preferred_element_type=F32)
    dscores_ref[...] = jnp.zeros_like(dscores_ref)

    def measure(index, carry):
        squares, dots = carry
        at = tile(index)
        gate = hidden_ref[:, at]
        product = (mixed_ref[:, at] + values_ref[:, at] * skip_ref[:, at]) * (gate * jax.nn.sigmoid(gate))
        return squares + product * product, dots + product * gated_grad_ref[:, at] * gate_ref[:, at]

    zero = jnp.zeros((rows, LANES), F32)
    squares, dots = lax.fori_loop(0, PAIRS, measure, (zero, zero))
    scale = lax.rsqrt(jnp.sum(squares, axis=-1, keepdims=True) / INNER + EPSILON)
    pull = scale * scale * scale * (jnp.sum(dots, axis=-1, keepdims=True) / INNER)
    first = low_half()

    def conv_back(index, du):
        at = tile(index)
        signal = hidden_ref[:, tile(index + PAIRS)]
        small_ref[5:6, at] = jnp.sum(du, axis=0, keepdims=True)
        small_ref[CONV : CONV + 1, at] = jnp.sum(du * signal, axis=0, keepdims=True)
        total = du * conv_ref[CONV - 1 : CONV, at]
        for tap in range(1, CONV):
            masked = du * taps_ref[tap - 1]
            shifted = pltpu.roll(signal, tap, axis=0)
            small_ref[CONV - tap : CONV - tap + 1, at] = jnp.sum(masked * shifted, axis=0, keepdims=True)
            total = total + pltpu.roll(masked, rows - tap, axis=0) * conv_ref[CONV - 1 - tap : CONV - tap, at]
        dhidden_ref[:, tile(index + PAIRS)] = total.astype(LOW)

    def heads(index, carry):
        dcum, dstep = carry
        at = tile(index)
        gate = hidden_ref[:, at]
        sigmoid = jax.nn.sigmoid(gate)
        silu = gate * sigmoid
        values = values_ref[:, at]
        mixed = mixed_ref[:, at]
        skip = skip_ref[:, at]
        states = mixed + values * skip
        product = states * silu
        gated_grad = gated_grad_ref[:, at]
        small_ref[6:7, at] = jnp.sum(gated_grad * product * scale, axis=0, keepdims=True)
        dproduct = scale * (gated_grad * gate_ref[:, at]) - product * pull
        dhidden_ref[:, at] = (dproduct * states * (sigmoid * (1.0 + gate * (1.0 - sigmoid)))).astype(LOW)
        dstates = dproduct * silu
        small_ref[7:8, at] = jnp.sum(dstates * values, axis=0, keepdims=True)
        step_wide = spread_heads(high, low, index)
        scaled = (values * step_wide).astype(LOW)
        dlow = dstates.astype(LOW)
        none = jnp.zeros_like(dlow)
        stacked = jnp.concatenate([jnp.where(first, dlow, none), jnp.where(first, none, dlow)], axis=0)
        allowed = allowed_ref[...]
        scores = scores_ref[...]
        factors = [decays(turned_ref, allowed, 2 * index + head) for head in (0, 1)]
        weights = jnp.concatenate([(scores * factor).astype(LOW) for factor in factors], axis=0)
        dweights = lax.dot_general(stacked, scaled, NT, preferred_element_type=F32)
        dscores_ref[...] += dweights[:rows] * factors[0] + dweights[rows:] * factors[1]
        dscaled = lax.dot_general(weights, stacked, TN, preferred_element_type=F32)
        head = iota((LANES, LANES), 1)
        lane = iota((LANES, LANES), 0)
        pick = jnp.where(head == 2 * index + lane // HEADDIM, 1.0, 0.0).astype(LOW)
        gained = split(dlow.astype(F32) * mixed - scaled.astype(F32) * dscaled)
        dcum = dcum + sum(jnp.dot(item, pick, preferred_element_type=F32) for item in gained)
        gained = split(values * dscaled)
        dstep = dstep + sum(jnp.dot(item, pick, preferred_element_type=F32) for item in gained)
        dvalues = step_wide * dscaled + skip * dstates
        conv_back(index, dvalues * slope_ref[:, at])
        return dcum, dstep

    dcum, dstep = lax.fori_loop(0, PAIRS, heads, (zero, zero))
    dscores = dscores_ref[...]
    dinputs = lax.dot_general(dscores, outputs_c, TN, precision=EXACT, preferred_element_type=F32)
    doutputs = jnp.dot(dscores, inputs_b, precision=EXACT, preferred_element_type=F32)
    conv_back(PAIRS, dinputs * slope_ref[:, INNER : INNER + STATE])
    conv_back(PAIRS + 1, doutputs * slope_ref[:, INNER + STATE :])
    drate = lax.dot_general(tri, dcum, TN, precision=EXACT, preferred_element_type=F32)
    small_ref[0:1, :LANES] = jnp.sum(drate * rate, axis=0, keepdims=True)
    draw = (dstep - drate * jnp.exp(heads_ref[0:1])) * jax.nn.sigmoid(raw)
    small_ref[0:1, LANES : 2 * LANES] = jnp.sum(draw, axis=0, keepdims=True)
    dhidden_ref[:, STEP_AT:] = draw.astype(LOW)


def backward_in_kernel(
    me_ref, grad_ref, resid_ref, normed_ref, dhidden_ref, in_ref, norm_ref,
    back_ref, in_keep_ref, in_send_ref, norm_grad_ref,
    gathered_ref, turned_norm_ref, dnorm_ref, first=0,
):
    core = me_ref[0] % 2
    chip = me_ref[0] // 2
    turned_norm_ref[...] = normed_ref[...].T
    dnorm_ref[...] = jnp.zeros_like(dnorm_ref)

    def in_back(index, carry):
        at = pl.ds(pl.multiple_of(index * 3 * LANES, LANES), 3 * LANES)
        to = pl.ds(pl.multiple_of(first + index * 3 * LANES, LANES), 3 * LANES)
        dhidden = dhidden_ref[:, at]
        dnorm_ref[...] += lax.dot_general(dhidden, in_ref[:, at], NT, preferred_element_type=F32)
        gathered_ref[...] = jnp.dot(turned_norm_ref[...], dhidden, preferred_element_type=F32)
        depth = WIDTH // PARTS
        for pair in range(PARTS // 2):
            even = gathered_ref[2 * pair * depth : (2 * pair + 1) * depth]
            odd = gathered_ref[(2 * pair + 1) * depth : (2 * pair + 2) * depth]
            other = pair ^ chip
            in_keep_ref[other % 4, other // 4, :, to] = jnp.where(core == 0, even, odd).astype(LOW)
            in_send_ref[other % 4, other // 4, :, to] = jnp.where(core == 0, odd, even).astype(LOW)
        return carry

    lax.fori_loop(0, PADDED // (3 * LANES), in_back, 0)
    resid = resid_ref[...]
    scale = lax.rsqrt(jnp.mean(resid * resid, axis=-1, keepdims=True) + EPSILON)
    dnorm = dnorm_ref[...]
    norm_grad_ref[...] = jnp.sum(dnorm * resid * scale, axis=0, keepdims=True)
    gained = dnorm * norm_ref[...]
    pull = scale * scale * scale * jnp.mean(gained * resid, axis=-1, keepdims=True)
    back_ref[...] = grad_ref[...] + scale * gained - resid * pull


def backward_both_kernel(
    me_ref, grad_ref, resid_ref, normed_ref, dhidden_ref, in_ref, norm_ref, gated_ref, out_ref,
    back_ref, keep_ref, send_ref, norm_grad_ref, gated_grad_ref, *scratch,
):
    backward_in_kernel(
        me_ref, grad_ref, resid_ref, normed_ref, dhidden_ref, in_ref, norm_ref,
        back_ref, keep_ref, send_ref, norm_grad_ref, *scratch, first=2 * WIDTH,
    )
    depth = WIDTH // PARTS

    def store(other, keep, send):
        for half in (0, 1):
            at = pl.ds(half * WIDTH, WIDTH)
            rows = slice(half * depth, (half + 1) * depth)
            keep_ref[other % 4, other // 4, :, at] = keep[rows].astype(LOW)
            send_ref[other % 4, other // 4, :, at] = send[rows].astype(LOW)

    out_back(me_ref, back_ref, gated_ref, out_ref, gated_grad_ref, store)


def shape(*dims, dtype=F32):
    return jax.ShapeDtypeStruct(dims, dtype)


def mixer_scratch(rows):
    return [
        pltpu.VMEM((rows, rows), F32),
        pltpu.VMEM((CONV - 1, rows, LANES), F32),
        pltpu.VMEM((LANES, rows), F32),
        pltpu.VMEM((rows, rows), F32),
    ]


VMEM = pl.BlockSpec(memory_space=pltpu.VMEM)
SMEM = pl.BlockSpec(memory_space=pltpu.SMEM)


def call(kernel, name, flops, size, outs, scratch, *args):
    return pl.pallas_call(
        kernel,
        out_shape=outs,
        in_specs=[SMEM if item.shape == (1,) else VMEM for item in args],
        out_specs=(VMEM,) * len(outs),
        scratch_shapes=scratch,
        compiler_params=pltpu.CompilerParams(vmem_limit_bytes=VMEM_LIMIT),
        cost_estimate=pl.CostEstimate(flops=flops, bytes_accessed=size, transcendentals=0),
        name=name,
    )(*args)


def forward(resid, in_full, small, segs):
    rows = resid.shape[0]
    outs = (
        shape(rows, PADDED), shape(rows, INNER), shape(rows, WIDTH, dtype=LOW), shape(rows, INNER, dtype=LOW),
    )
    scratch = mixer_scratch(rows) + [pltpu.VMEM((rows, INNER), F32)]
    return call(
        forward_kernel, "mix_forward", 10_000_000_000, 10_000_000, outs, scratch, resid, in_full, *small, *segs
    )


def backward_out(me, grad, gated, out_full):
    part = shape(4, 4, INNER // PARTS, WIDTH, dtype=LOW)
    outs = (shape(grad.shape[0], INNER), part, part)
    return call(backward_out_kernel, "out_backward", 2_000_000_000, 8_000_000, outs, [], me, grad, gated, out_full)


def backward_mixer(gated_grad, hidden, mixed, small, segs):
    rows = hidden.shape[0]
    outs = (shape(rows, PADDED, dtype=LOW), shape(SMALL_ROWS, CONVCH))
    scratch = mixer_scratch(rows) + [
        pltpu.VMEM((rows, rows), F32), pltpu.VMEM((rows, CONVCH), F32), pltpu.VMEM((rows, CONVCH), F32),
    ]
    return call(
        backward_mixer_kernel, "mix_backward", 12_000_000_000, 5_000_000, outs, scratch,
        gated_grad, hidden, mixed, *small[1:], *segs,
    )


def backward_in(me, grad, resid, normed, dhidden, in_full, norm):
    rows = resid.shape[0]
    part = shape(4, 4, WIDTH // PARTS, PADDED, dtype=LOW)
    outs = (shape(rows, WIDTH), part, part, shape(1, WIDTH))
    scratch = [
        pltpu.VMEM((WIDTH, 3 * LANES), F32), pltpu.VMEM((WIDTH, rows), LOW), pltpu.VMEM((rows, WIDTH), F32),
    ]
    return call(
        backward_in_kernel, "in_backward", 6_000_000_000, 14_000_000, outs, scratch,
        me, grad, resid, normed, dhidden, in_full, norm,
    )


def backward_both(me, grad, resid, normed, dhidden, in_full, norm, gated, out_full):
    rows = resid.shape[0]
    part = shape(4, 4, WIDTH // PARTS, 2 * WIDTH + PADDED, dtype=LOW)
    outs = (shape(rows, WIDTH), part, part, shape(1, WIDTH), shape(rows, INNER))
    scratch = [
        pltpu.VMEM((WIDTH, 3 * LANES), F32), pltpu.VMEM((WIDTH, rows), LOW), pltpu.VMEM((rows, WIDTH), F32),
    ]
    return call(
        backward_both_kernel, "both_backward", 8_000_000_000, 22_000_000, outs, scratch,
        me, grad, resid, normed, dhidden, in_full, norm, gated, out_full,
    )


def swap(values, bit, count):
    return lax.ppermute(values, "fsdp", [(index, index ^ bit) for index in range(count)])


def place_kernel(cuts, me_ref, own_ref, other_ref, *whole_refs):
    me = me_ref[0]

    def step(item, carry):
        away = 2 * (4 * (item % 4) + item // 4)
        for core, ref in ((0, own_ref), (1, other_ref)):
            for starts, whole_ref in zip(cuts, whole_refs):
                for part, low in enumerate(starts):
                    high = low + whole_ref.shape[3]
                    whole_ref[me ^ (away + core), part] = ref[item, :, low:high]
        return carry

    lax.fori_loop(0, PARTS // 2, step, 0, unroll=4)


def phase(earlier, *items):
    held = lax.optimization_barrier(tuple(item[0] for item in items) + tuple(earlier))
    return [swap(value, item[1], PARTS) for value, item in zip(held, items)]


def after(earlier, *values):
    return lax.optimization_barrier(tuple(values) + tuple(earlier))[: len(values)]


def along_z(own):
    return [(own, 8), (own, 16), (own, 24)]


def along_xy(cur):
    return [(cur, 2), (cur, 4)]


def across(right, up):
    return [(right[:2], 4), (up[2:], 2)]


def join(own, others):
    return jnp.concatenate([own, *others], axis=0)


def put_together(me, own, other, *cuts):
    depth = own.shape[1]
    outs = tuple(shape(PARTS, len(starts), depth, width, dtype=LOW) for starts, width in cuts)
    kernel = partial(place_kernel, [starts for starts, width in cuts])
    wholes = call(kernel, "place", 0, 4 * own.size, outs, [], me, own, other)
    return [whole.reshape(-1, whole.shape[3]) for whole in wholes]


class Sums:
    def __init__(self, keep):
        self.keep = keep

    def add_core(self, other):
        self.other = other

    def local(self, group, low, high):
        return self.keep[group, low:high].astype(F32) + self.other[group, low:high].astype(F32)

    def across(self):
        return [(self.local(3, 0, 2).astype(LOW), 4), (self.local(3, 2, 4).astype(LOW), 2)]

    def along_xy(self, far_a, far_b):
        right = jnp.concatenate([self.local(1, 0, 2) + far_a.astype(F32), self.local(1, 2, 4)]).astype(LOW)
        up = jnp.concatenate([self.local(2, 0, 2), self.local(2, 2, 4) + far_b.astype(F32)]).astype(LOW)
        return [(right, 2), (up, 4)]

    def add_xy(self, right, up):
        self.mine = lambda low, high: (
            self.local(0, low, high) + right[low:high].astype(F32) + up[low:high].astype(F32)
        )

    def along_z(self):
        return [(self.mine(item, item + 1).astype(LOW), 8 * item) for item in (1, 2, 3)]

    def result(self, *parts):
        return sum([item.astype(F32) for item in parts], self.mine(0, 1))[0]

    def far_z(self):
        return [(self.mine(2, 4).astype(LOW), 16)]

    def near_z(self, far):
        self.far = far
        return [((self.mine(1, 2) + far[1:].astype(F32)).astype(LOW), 8)]

    def end(self, near):
        return self.result(self.far[:1], near)


def grow(values, other, me, bit):
    upper = (me & bit) > 0
    return jnp.where(upper, join(other, [values]), join(values, [other]))


def gather_small(values, me, count):
    bit = 1
    while bit < count:
        values = grow(values, swap(values, bit, count), me, bit)
        bit *= 2
    return values


def sum_small(values, count):
    bit = 1
    while bit < count:
        values = values + swap(values, bit, count)
        bit *= 2
    return values


def small_arrays(packed, count, widths, log_decay, skip_gain, step_bias):
    layers = packed.shape[1]
    norms, taps, gates = widths
    held = packed.astype(F32)

    def full(low, rows, width):
        part = held[:, :, low : low + rows * width].reshape(count, layers, rows, width)
        return jnp.transpose(part, (1, 2, 0, 3)).reshape(layers, rows, count * width)

    norm = full(0, 1, norms)
    conv = full(norms, CONV + 1, taps)
    gate = full(norms + (CONV + 1) * taps, 1, gates)
    heads = jnp.pad(jnp.stack([log_decay, skip_gain, step_bias], axis=1), ((0, 0), (0, 0), (0, LANES - HEADS)))
    skip = jnp.repeat(skip_gain, HEADDIM, axis=1)[:, None]
    return [[item[layer] for item in (norm, conv, gate, heads, skip)] for layer in range(layers)]


def project(resid, gated, out_full):
    return resid + jnp.dot(gated, out_full, preferred_element_type=F32)


def finish(resid, cotangent, segs):
    valid = (segs[0] >= 0).astype(F32)
    return (resid * valid).astype(LOW), cotangent.astype(F32) * valid


def run_plain(count, me, resid, segs, cotangent, in_shards, out_shards, packed, small_of):
    layers = len(in_shards)
    place = (me * 0).astype(jnp.int32).reshape(1)
    packed = gather_small(packed, me, count)
    small = small_of(packed)

    def whole(shard):
        return lax.all_gather(shard, "fsdp", axis=0, tiled=True)

    def scatter(keep, send):
        both = jnp.stack([jnp.swapaxes(keep, 0, 1), jnp.swapaxes(send, 0, 1)], axis=2)
        both = both.reshape(-1, keep.shape[-1]).astype(F32)
        return lax.psum_scatter(both, "fsdp", scatter_dimension=0, tiled=True)

    in_full = [whole(shard) for shard in in_shards]
    out_full = [whole(shard) for shard in out_shards]
    kept = []
    for layer in range(layers):
        saved = forward(resid, in_full[layer], small[layer], segs)
        kept.append((resid, saved))
        resid = project(resid, saved[3], out_full[layer])
    mixed, grad = finish(resid, cotangent, segs)
    in_grads, out_grads, sums, norm_sums = ([None] * layers for item in range(4))
    for layer in reversed(range(layers)):
        resid, (hidden, ssm, normed, gated) = kept[layer]
        gated_grad, out_keep, out_send = backward_out(place, grad, gated, out_full[layer])
        dhidden, sums[layer] = backward_mixer(gated_grad, hidden, ssm, small[layer], segs)
        grad, in_keep, in_send, norm_sums[layer] = backward_in(
            place, grad, resid, normed, dhidden, in_full[layer], small[layer][0]
        )
        out_grads[layer] = scatter(out_keep, out_send)
        in_grads[layer] = scatter(in_keep, in_send)
    sums = sum_small(jnp.stack(sums), count)
    norm_sums = sum_small(jnp.concatenate(norm_sums), count)
    return mixed, grad, in_grads, out_grads, sums, norm_sums


def run_staged(me, resid, segs, cotangent, in_shards, out_shards, packed, small_of):
    place = me.astype(jnp.int32).reshape(1)
    in0, in1 = (shard[None] for shard in in_shards)
    out0, out1 = (shard[None] for shard in out_shards)

    depth = in0.shape[1]
    second = jnp.concatenate([out0[:, :depth], out0[:, depth:], in1], axis=2)
    last = out1

    *got, other = phase([], *along_z(in0), (packed, 1))
    cur_a = join(in0, got)
    packed = grow(packed, other, me, 1)
    packed = grow(packed, swap(packed, 2, PARTS), me, 2)

    right_a, up_a, near, other = phase([cur_a, packed], *along_xy(cur_a), (second, 8), (packed, 4))
    cur_b = join(second, [near])
    packed = grow(packed, other, me, 4)

    *far_a, other = phase([right_a, up_a, cur_b, packed], *across(right_a, up_a), (packed, 8))
    (far_b,) = phase([right_a, up_a], (cur_b, 16))
    own_a = join(cur_a, [right_a, up_a, *far_a])
    packed = grow(packed, other, me, 8)

    other_a, near, other = phase([own_a, packed], (own_a, 1), (last, 8), (packed, 16))
    cur_b = join(cur_b, [far_b])
    cur_c = join(last, [near])
    packed = grow(packed, other, me, 16)
    small = small_of(packed)

    (in0_full,) = put_together(place, own_a, other_a, ((0,), PADDED))
    right_b, up_b, far_c = phase([in0_full, cur_c], *along_xy(cur_b), (cur_c, 16))
    kept0 = forward(*after([cur_b, *small[1]], resid), in0_full, small[0], segs)
    cur_c = join(cur_c, [far_c])

    far_b = phase([right_b, up_b, kept0[3]], *across(right_b, up_b))
    own_b = join(cur_b, [right_b, up_b, *far_b])
    other_b, right_c, up_c = phase([own_b, cur_c], (own_b, 1), *along_xy(cur_c))

    ready = [other_b]
    far_c = phase([other_b, right_c, up_c], *across(right_c, up_c))
    out0_full, in1_full = put_together(
        place, own_b, *after(ready, other_b), ((0, WIDTH), WIDTH), ((2 * WIDTH,), PADDED)
    )
    resid1 = project(resid, kept0[3], out0_full)
    own_c = join(cur_c, [right_c, up_c, *far_c])
    ready = [own_c, resid1]
    (other_c,) = phase(ready, (own_c, 1))
    kept1 = forward(*after(ready, resid1), in1_full, small[1], segs)
    (out1_full,) = put_together(place, own_c, *after([kept1[3]], other_c), ((0,), WIDTH))
    mixed, grad = finish(project(resid1, kept1[3], out1_full), cotangent, segs)

    hidden, ssm, normed, gated = kept1
    gated_grad, keep, send = backward_out(place, grad, gated, out1_full)
    sum_c = Sums(keep)
    (core,) = phase([gated_grad], (send, 1))
    dhidden, small1 = backward_mixer(gated_grad, hidden, ssm, small[1], segs)
    sum_c.add_core(core)

    ready = [core, dhidden]
    far_c = phase(ready, *sum_c.across())
    grad, keep, send, norm1, gated_grad = backward_both(
        place, grad, resid1, normed, *after(ready, dhidden), in1_full, small[1][0], kept0[3], out0_full
    )
    sum_b = Sums(keep)

    hidden, ssm, normed, gated = kept0
    ready = [*far_c, gated_grad]
    core, *got = phase(ready, (send, 1), *sum_c.along_xy(*far_c))
    dhidden, small0 = backward_mixer(*after(ready, gated_grad), hidden, ssm, small[0], segs)
    sums = jnp.stack([small0, small1])
    sum_b.add_core(core)
    sum_c.add_xy(*got)

    ready = [core, *got, dhidden]
    *far_b, far_c = phase(ready, *sum_b.across(), *sum_c.far_z())
    grad, keep, send, norm0 = backward_in(
        place, grad, resid, normed, *after(ready, dhidden), in0_full, small[0][0]
    )
    sum_a = Sums(keep)
    norms = jnp.stack([norm0, norm1])
    sums = jnp.concatenate([jnp.concatenate([sums[:, :1, : 2 * LANES], norms, sums[:, :1, 2 * LANES + WIDTH :]], axis=2), sums[:, 1:]], axis=1)

    ready = [*far_b, far_c, grad]
    core, near_c, right_b, up_b = phase(ready, (send, 1), *sum_c.near_z(far_c), *sum_b.along_xy(*far_b))
    sum_a.add_core(core)
    sum_b.add_xy(right_b, up_b)

    far_a = phase([core, near_c], *sum_a.across())
    sums += swap(*after(far_a, sums), 1, PARTS)
    ready = [*far_a, right_b, up_b, sums]
    right_a, up_a, far_b, other = phase(ready, *sum_a.along_xy(*far_a), *sum_b.far_z(), (sums, 2))
    sums += other
    sums += swap(sums, 4, PARTS)
    sums += swap(sums, 8, PARTS)
    sum_a.add_xy(right_a, up_a)

    *parts, near_b = phase([right_a, up_a, far_b, sums], *sum_a.along_z(), *sum_b.near_z(far_b))
    sums += swap(*after([near_b], sums), 16, PARTS)
    both = sum_b.end(near_b)
    in_grads = [sum_a.result(*parts), both[:, 2 * WIDTH :]]
    out_grads = [jnp.concatenate([both[:, :WIDTH], both[:, WIDTH : 2 * WIDTH]]), sum_c.end(near_c)]
    return mixed, grad, in_grads, out_grads, sums, sums[:, 0, 2 * LANES : 2 * LANES + WIDTH]


def body(
    count, tokens, segments, norm_gain, in_weight, conv_weight, conv_bias,
    log_decay, skip_gain, step_bias, gate_gain, out_weight, cotangent,
):
    layers, in_rows = in_weight.shape[:2]
    rows = tokens.shape[0] * BLOCK
    me = lax.axis_index("fsdp")
    chans, gates = conv_bias.shape[1], gate_gain.shape[1]
    packed = jnp.concatenate([norm_gain, conv_weight.reshape(layers, -1), conv_bias, gate_gain], axis=1)[None]
    padded = jnp.pad(in_weight, ((0, 0), (0, 0), (0, PADDED - PROJ)))
    segs = (segments.reshape(rows, 1), segments.reshape(1, rows))

    def small_of(packed):
        return small_arrays(packed, count, (in_rows, chans, gates), log_decay, skip_gain, step_bias)

    run = run_staged if count == PARTS and layers == 2 else partial(run_plain, count)
    mixed, grad, in_grads, out_grads, sums, norms = run(
        me, tokens.reshape(rows, WIDTH).astype(F32), segs, cotangent.reshape(rows, WIDTH),
        [padded[layer] for layer in range(layers)], [out_weight[layer] for layer in range(layers)], packed, small_of,
    )
    total = sums

    def own(values, size):
        return lax.dynamic_slice_in_dim(values, me * size, size, axis=values.ndim - 1)

    by_head = total[:, 7, :INNER].reshape(layers, HEADS, HEADDIM).sum(axis=-1)
    return (
        mixed.reshape(tokens.shape),
        grad.reshape(tokens.shape),
        own(norms, in_rows),
        jnp.stack([item[:, :PROJ] for item in in_grads]),
        own(total[:, 1 : 1 + CONV], chans),
        own(total[:, 5], chans),
        total[:, 0, :HEADS],
        by_head,
        total[:, 0, LANES : LANES + HEADS],
        own(total[:, 6, :INNER], gates),
        jnp.stack(out_grads),
    )


def solution(mesh):
    split0 = P("fsdp", None, None)
    split1 = P(None, "fsdp", None)
    in_specs = (
        split0, P("fsdp", None), P(None, "fsdp"), split1, P(None, None, "fsdp"), P(None, "fsdp"),
        P(), P(), P(), P(None, "fsdp"), split1, split0,
    )
    out_specs = (
        split0, split0, P(None, "fsdp"), split1, P(None, None, "fsdp"), P(None, "fsdp"),
        P(), P(), P(), P(None, "fsdp"), split1,
    )
    return jax.shard_map(
        partial(body, mesh.shape["fsdp"]), mesh=mesh, in_specs=in_specs, out_specs=out_specs, check_vma=False
    )
```

time: 361 us -> 333 us (0.922)
  waiting for transfers between devices: 153 us -> 108 us
  local copies, waits for them, and re-layouts: 23 us -> 43.6 us
  other arithmetic: 39.4 us -> 30 us
  matrix products: 0 us -> 5.05 us
  Pallas kernels: 86.3 us -> 91.2 us
  starting transfers between devices: 56.1 us -> 52.3 us
    ppermute x82 -> x54, waiting for transfers between devices: 153 us -> 108 us  [swap(): lax.ppermute(values, 'fsdp', [(index, index ^ bit) for index in range(cou...]
    unnamed x83 -> x92, local copies, waits for them, and re-layouts: 3.02 us -> 12.9 us
    squeeze x1 -> x7, local copies, waits for them, and re-layouts: 0.01 us -> 9.39 us  [small_arrays(): item[layer]]
    convert_element_type x15 -> x8, other arithmetic: 15.1 us -> 8.88 us  [the longest x2 3.05 us: far_z(): return [(self.mine(2, 4).astype(LOW), 16)]]
    dot_general x0 -> x2, matrix products: none -> 5.05 us  [project(): return resid + jnp.dot(gated, out_full, preferred_element_type=F32)]
    pallas_call x8 -> x10, Pallas kernels: 86.3 us -> 91.2 us  [call(): pl.pallas_call(kernel, out_shape=outs, in_specs=[SMEM if item.shape == (1...]
    reshape x12 -> x1, local copies, waits for them, and re-layouts: 6.4 us -> 1.71 us  [full(): held[:, :, low:low + rows * width].reshape(count, layers, rows, width)]
    ppermute x82 -> x54, starting transfers between devices: 56.1 us -> 52.3 us  [swap(): lax.ppermute(values, 'fsdp', [(index, index ^ bit) for index in range(cou...]
  transfers between devices with their start and end apart: 82 -> 54, of which waited for: 43 -> 27; matrix products, arithmetic and copies ran while one was open for 15% -> 18% of each run, Pallas kernels for 7% -> 21%
where the time goes in v2:
time: 333 us; the launch traced here: 332 us
  waiting for transfers between devices  108 us (32%)
  Pallas kernels  91.2 us (27%)
  starting transfers between devices  52.3 us (16%)
  local copies, waits for them, and re-layouts  43.6 us (13%)
  other arithmetic  30 us (9%)
  matrix products  5.05 us (2%)
    ppermute x54, waiting for transfers between devices, swap(): lax.ppermute(values, 'fsdp', [(index, index ^ bit) for index in range(cou...  108 us
    pallas_call x10, Pallas kernels, call(): pl.pallas_call(kernel, out_shape=outs, in_specs=[SMEM if item.shape == (1...  91.2 us
    ppermute x54, starting transfers between devices, swap(): lax.ppermute(values, 'fsdp', [(index, index ^ bit) for index in range(cou...  52.3 us
    unnamed x92, local copies, waits for them, and re-layouts  12.9 us
    squeeze x7, local copies, waits for them, and re-layouts, small_arrays(): item[layer]  9.39 us
    slice x6, local copies, waits for them, and re-layouts, small_arrays(): item[layer]  6.94 us
  transfers between devices with their start and end apart: 54, of which 27 were waited for; matrix products, arithmetic and copies ran while one was open for 18% of the time, Pallas kernels for 21%

profile of v2, /device:TPU:0, one launch (start us, length us, event | category | flops | bytes accessed | tf_op | source)
XLA Modules:
  0.0 331.5 jit_solution(2022849595425408579)
XLA Ops:
  3.3 5.1 %collective-permute-start.2 = (bf16[1,24,3456]{2,1,0:T(8,128)(2,1)S(1)}, bf16[1,24,3456]{2,1,0:T(8,128)(2,1)S(1)}, u32[]{:S(2)}, u32[]{:S(2)}) collective-permute-start(bf16[1,24,3456]{2,1,0:T(8,128)(2,1)S(1)} %get-tuple-element.95), channel_id=1, source_target_pairs={{0,24},{1,25},{2,26},{3,27},{4,28},{5,29},{6,30},{7,31},{8,16},{9,... | collective-permute-start | bytes 497672 | tf_op jit(solution)/shard_map/ppermute | solution.py:418
  9.8 1.6 constant_dynamic-update-slice_fusion.21
  11.4 1.7 bitcast_convert_fusion.resid_ref
  15.3 1.7 collective-permute-start.4
  17.7 1.4 reshape.446.col_ref
  25.1 1.5 collective-permute-start.7
  28.1 13.4 %collective-permute-done.9 = bf16[4,2,352]{2,1,0:T(2,128)(2,1)S(1)} collective-permute-done((bf16[4,2,352]{2,1,0:T(2,128)(2,1)S(1)}, bf16[4,2,352]{2,1,0:T(2,128)(2,1)S(1)}, u32[]{:S(2)}, u32[]{:S(2)}) %collective-permute-start.9) | collective-permute-done | bytes 5664 | tf_op jit(solution)/shard_map/ppermute | solution.py:418
  43.6 1.5 collective-permute-start.10
  46.5 4.3 %collective-permute-done.10 = bf16[2,24,3456]{2,1,0:T(8,128)(2,1)S(1)} collective-permute-done((bf16[2,24,3456]{2,1,0:T(8,128)(2,1)S(1)}, bf16[2,24,3456]{2,1,0:T(8,128)(2,1)S(1)}, u32[]{:S(2)}, u32[]{:S(2)}) %collective-permute-start.10) | collective-permute-done | bytes 331808 | tf_op jit(solution)/shard_map/ppermute | solution.py:418
  50.7 1.5 collective-permute-done.11
  52.2 3.1 collective-permute-start.13
  59.2 1.7 reshape.432
  61.7 1.7 fusion.60
  64.1 1.4 squeeze.24.norm_ref
  65.5 1.6 copy.32
  67.0 1.6 squeeze.25.conv_ref
  70.2 1.4 squeeze.26.gate_ref
  71.6 1.4 squeeze.28.norm_ref
  73.0 1.6 copy.36
  74.5 1.6 squeeze.29.conv_ref
  76.1 1.4 squeeze.30.gate_ref
  78.5 2.3 collective-permute-done.8
  82.5 5.3 %place.3 = bf16[32,1,24,3456]{3,2,1,0:T(8,128)(2,1)} custom-call(s32[1]{0:T(128)} %bitcast.16.me_ref, bf16[16,24,3456]{2,1,0:T(8,128)(2,1)} %copy-done.4, bf16[16,24,3456]{2,1,0:T(8,128)(2,1)} %collective-permute-done.14.other_ref), custom_call_target="tpu_custom_call" | custom-call | bytes 5308416 | tf_op jit(solution)/shard_map/place/pallas_call | solution.py:350
  87.8 1.7 collective-permute-start.16
  90.4 11.2 %mix_forward.2 = (f32[128,3456]{1,0:T(8,128)}, f32[128,1536]{1,0:T(8,128)}, bf16[128,768]{1,0:T(8,128)(2,1)}, bf16[128,1536]{1,0:T(8,128)(2,1)}) custom-call(f32[128,768]{1,0:T(8,128)} %bitcast_convert_fusion.resid_ref, bf16[768,3456]{1,0:T(8,128)(2,1)} %bitcast.196, f32[1,768]{1,0:T(1,128)} %squeeze.28.norm_ref, f32[5,1792]{1,0:T(8,128)} %squeeze.29.conv_ref, ...), custom_call_target="tpu_custom_call" | custom-call | flops 10000000000 | bytes 10000000 | tf_op jit(solution)/shard_map/mix_forward/pallas_call | solution.py:350
  102.6 8.1 %collective-permute-done.16 = bf16[4,24,4992]{2,1,0:T(8,128)(2,1)S(1)} collective-permute-done((bf16[4,24,4992]{2,1,0:T(8,128)(2,1)S(1)}, bf16[4,24,4992]{2,1,0:T(8,128)(2,1)S(1)}, u32[]{:S(2)}, u32[]{:S(2)}) %collective-permute-start.16) | collective-permute-done | bytes 958496 | tf_op jit(solution)/shard_map/ppermute | solution.py:418
  110.7 1.4 collective-permute-done.17
  115.1 8.5 %collective-permute-done.18 = bf16[2,24,4992]{2,1,0:T(8,128)(2,1)S(1)} collective-permute-done((bf16[2,24,4992]{2,1,0:T(8,128)(2,1)S(1)}, bf16[2,24,4992]{2,1,0:T(8,128)(2,1)S(1)}, u32[]{:S(2)}, u32[]{:S(2)}) %collective-permute-start.18) | collective-permute-done | bytes 479264 | tf_op jit(solution)/shard_map/ppermute | solution.py:418
  127.8 6.9 %collective-permute-done.22 = bf16[4,48,768]{2,1,0:T(8,128)(2,1)S(1)} collective-permute-done((bf16[4,48,768]{2,1,0:T(8,128)(2,1)S(1)}, bf16[4,48,768]{2,1,0:T(8,128)(2,1)S(1)}, u32[]{:S(2)}, u32[]{:S(2)}) %collective-permute-start.22) | collective-permute-done | bytes 294944 | tf_op jit(solution)/shard_map/ppermute | solution.py:418
  135.2 1.9 copy-done.3
  137.0 6.8 %place.4 = (bf16[32,2,24,768]{3,2,1,0:T(8,128)(2,1)}, bf16[32,1,24,3456]{3,2,1,0:T(8,128)(2,1)}) custom-call(s32[1]{0:T(128)} %bitcast.16.me_ref, bf16[16,24,4992]{2,1,0:T(8,128)(2,1)} %constant_dynamic-update-slice_fusion.8.own_ref, bf16[16,24,4992]{2,1,0:T(8,128)(2,1)} %copy-done.3), custom_call_target="tpu_custom_call" | custom-call | bytes 7667712 | tf_op jit(solution)/shard_map/place/pallas_call | solution.py:350
  144.8 1.4 collective-permute-start.25
  146.2 2.9 convolution_add_fusion.1.resid_ref
  151.1 11.2 %mix_forward.3 = (f32[128,3456]{1,0:T(8,128)}, f32[128,1536]{1,0:T(8,128)}, bf16[128,768]{1,0:T(8,128)(2,1)}, bf16[128,1536]{1,0:T(8,128)(2,1)}) custom-call(f32[128,768]{1,0:T(8,128)} %convolution_add_fusion.1.resid_ref, bf16[768,3456]{1,0:T(8,128)(2,1)} %bitcast.222, f32[1,768]{1,0:T(1,128)} %squeeze.24.norm_ref, f32[5,1792]{1,0:T(8,128)} %squeeze.25.conv_ref, ...), custom_call_target="tpu_custom_call" | custom-call | flops 10000000000 | bytes 10000000 | tf_op jit(solution)/shard_map/mix_forward/pallas_call | solution.py:350
  163.4 3.3 place.5
  166.7 5.5 %out_backward.1 = (f32[128,1536]{1,0:T(8,128)}, bf16[4,4,48,768]{3,2,1,0:T(8,128)(2,1)}, bf16[4,4,48,768]{3,2,1,0:T(8,128)(2,1)}) custom-call(s32[1]{0:T(128)} %bitcast.16.me_ref, f32[128,768]{1,0:T(8,128)} %convert_multiply_fusion.grad_ref, bf16[128,1536]{1,0:T(8,128)(2,1)} %get-tuple-element.126.gated_ref, bf16[1536,768]{1,0:T(8,128)(2,1)} %bitcast.194), custom_call_target="tpu_custom_call" | custom-call | flops 2000000000 | bytes 8000000 | tf_op jit(solution)/shard_map/out_backward/pallas_call | solution.py:350
  172.5 11.9 %mix_backward.2 = (bf16[128,3456]{1,0:T(8,128)(2,1)}, f32[8,1792]{1,0:T(8,128)}) custom-call(f32[128,1536]{1,0:T(8,128)} %get-tuple-element.130.gated_grad_ref, f32[128,3456]{1,0:T(8,128)} %get-tuple-element.131.hidden_ref, f32[128,1536]{1,0:T(8,128)} %get-tuple-element.132.mixed_ref, f32[5,1792]{1,0:T(8,128)} %squeeze.25.conv_ref, ...), custom_call_target="tpu_custom_call" | custom-call | flops 12000000000 | bytes 5000000 | tf_op jit(solution)/shard_map/mix_backward/pallas_call | solution.py:350
  185.8 1.4 collective-permute-start.29
  187.1 13.7 %both_backward.1 = (f32[128,768]{1,0:T(8,128)}, bf16[4,4,24,4992]{3,2,1,0:T(8,128)(2,1)}, bf16[4,4,24,4992]{3,2,1,0:T(8,128)(2,1)}, f32[1,768]{1,0:T(1,128)}, f32[128,1536]{1,0:T(8,128)}) custom-call(s32[1]{0:T(128)} %bitcast.16.me_ref, f32[128,768]{1,0:T(8,128)} %convert_multiply_fusion.grad_ref, f32[128,768]{1,0:T(8,128)} %convolution_add_fusion.1.resid_ref, ...), custom_call_target="tpu_custom_call" | custom-call | flops 8000000000 | bytes 22000000 | tf_op jit(solution)/shard_map/both_backward/pallas_call | solution.py:350
  203.5 12.0 %mix_backward.3 = (bf16[128,3456]{1,0:T(8,128)(2,1)}, f32[8,1792]{1,0:T(8,128)}) custom-call(f32[128,1536]{1,0:T(8,128)} %get-tuple-element.143.gated_grad_ref, f32[128,3456]{1,0:T(8,128)} %get-tuple-element.144.hidden_ref, f32[128,1536]{1,0:T(8,128)} %get-tuple-element.145.mixed_ref, f32[5,1792]{1,0:T(8,128)} %squeeze.29.conv_ref, ...), custom_call_target="tpu_custom_call" | custom-call | flops 12000000000 | bytes 5000000 | tf_op jit(solution)/shard_map/mix_backward/pallas_call | solution.py:350
  215.5 1.9 fusion.35
  217.4 1.7 fusion.11
  220.0 1.4 collective-permute-start.35
  222.5 10.2 %in_backward.1 = (f32[128,768]{1,0:T(8,128)}, bf16[4,4,24,3456]{3,2,1,0:T(8,128)(2,1)}, bf16[4,4,24,3456]{3,2,1,0:T(8,128)(2,1)}, f32[1,768]{1,0:T(1,128)}) custom-call(s32[1]{0:T(128)} %bitcast.16.me_ref, f32[128,768]{1,0:T(8,128)} %get-tuple-element.137.grad_ref, f32[128,768]{1,0:T(8,128)} %bitcast_convert_fusion.resid_ref, ...), custom_call_target="tpu_custom_call" | custom-call | flops 6000000000 | bytes 14000000 | tf_op jit(solution)/shard_map/in_backward/pallas_call | solution.py:350
  233.9 1.7 fusion.4
  237.8 1.4 collective-permute-start.37
  239.2 1.7 collective-permute-done.36
  242.3 1.4 collective-permute-start.39
  244.5 15.5 %collective-permute-done.42 = bf16[4,24,4992]{2,1,0:T(8,128)(2,1)S(1)} collective-permute-done((bf16[4,24,4992]{2,1,0:T(8,128)(2,1)S(1)}, bf16[4,24,4992]{2,1,0:T(8,128)(2,1)S(1)}, u32[]{:S(2)}, u32[]{:S(2)}) %collective-permute-start.42) | collective-permute-done | bytes 958496 | tf_op jit(solution)/shard_map/ppermute | solution.py:418
  262.3 5.2 %collective-permute-done.39 = bf16[2,24,3456]{2,1,0:T(8,128)(2,1)S(1)} collective-permute-done((bf16[2,24,3456]{2,1,0:T(8,128)(2,1)S(1)}, bf16[2,24,3456]{2,1,0:T(8,128)(2,1)S(1)}, u32[]{:S(2)}, u32[]{:S(2)}) %collective-permute-start.39) | collective-permute-done | bytes 331808 | tf_op jit(solution)/shard_map/ppermute | solution.py:418
  269.6 2.1 collective-permute-start.48
  271.7 2.8 collective-permute-done.43
  275.5 4.0 %collective-permute-done.44 = f32[2,8,1792]{2,1,0:T(8,128)} collective-permute-done((f32[2,8,1792]{2,1,0:T(8,128)S(1)}, f32[2,8,1792]{2,1,0:T(8,128)}, u32[]{:S(2)}, u32[]{:S(2)}) %collective-permute-start.44) | collective-permute-done | bytes 114720 | tf_op jit(solution)/shard_map/ppermute | solution.py:418
  280.4 1.4 collective-permute-start.45
  281.8 2.2 fusion.1
  285.6 9.1 %collective-permute-done.45 = f32[2,8,1792]{2,1,0:T(8,128)S(1)} collective-permute-done((f32[2,8,1792]{2,1,0:T(8,128)S(1)}, f32[2,8,1792]{2,1,0:T(8,128)S(1)}, u32[]{:S(2)}, u32[]{:S(2)}) %collective-permute-start.45) | collective-permute-done | bytes 114720 | tf_op jit(solution)/shard_map/ppermute | solution.py:418
  296.0 3.3 %collective-permute-done.47 = bf16[4,24,3456]{2,1,0:T(8,128)(2,1)S(1)} collective-permute-done((bf16[4,24,3456]{2,1,0:T(8,128)(2,1)S(1)}, bf16[4,24,3456]{2,1,0:T(8,128)(2,1)S(1)}, u32[]{:S(2)}, u32[]{:S(2)}) %collective-permute-start.47) | collective-permute-done | bytes 663584 | tf_op jit(solution)/shard_map/ppermute | solution.py:418
  300.0 1.6 fusion.29
  301.6 2.3 collective-permute-start.53
  303.9 2.1 collective-permute-start.51
  307.1 3.5 %collective-permute-done.53 = bf16[1,24,3456]{2,1,0:T(8,128)(2,1)S(1)} collective-permute-done((bf16[1,24,3456]{2,1,0:T(8,128)(2,1)S(1)}, bf16[1,24,3456]{2,1,0:T(8,128)(2,1)S(1)}, u32[]{:S(2)}, u32[]{:S(2)}) %collective-permute-start.53) | collective-permute-done | bytes 165920 | tf_op jit(solution)/shard_map/ppermute | solution.py:418
  310.6 5.4 %collective-permute-done.52 = bf16[1,24,3456]{2,1,0:T(8,128)(2,1)S(1)} collective-permute-done((bf16[1,24,3456]{2,1,0:T(8,128)(2,1)S(1)}, bf16[1,24,3456]{2,1,0:T(8,128)(2,1)S(1)}, u32[]{:S(2)}, u32[]{:S(2)}) %collective-permute-start.52) | collective-permute-done | bytes 165920 | tf_op jit(solution)/shard_map/ppermute | solution.py:418
  317.3 2.0 collective-permute-done.49
  322.9 4.6 %collective-permute-done.50 = f32[2,8,1792]{2,1,0:T(8,128)S(1)} collective-permute-done((f32[2,8,1792]{2,1,0:T(8,128)S(1)}, f32[2,8,1792]{2,1,0:T(8,128)S(1)}, u32[]{:S(2)}, u32[]{:S(2)}) %collective-permute-start.50) | collective-permute-done | bytes 114720 | tf_op jit(solution)/shard_map/ppermute | solution.py:418
  (242 shorter events, 72.4 us)
Async XLA Ops:
  3.3 18.6 %collective-permute-start.2 = (bf16[1,24,3456]{2,1,0:T(8,128)(2,1)S(1)}, bf16[1,24,3456]{2,1,0:T(8,128)(2,1)S(1)}, u32[]{:S(2)}, u32[]{:S(2)}) collective-permute-start(bf16[1,24,3456]{2,1,0:T(8,128)(2,1)S(1)} %get-tuple-element.95), channel_id=1, source_target_pairs={{0,24},{1,25},{2,26},{3,27},{4,28},{5,29},{6,30},{7,31},{8,16},{9,... | collective-permute-start | bytes 497672 | tf_op jit(solution)/shard_map/ppermute | solution.py:418
  8.3 14.1 %collective-permute-start.1 = (bf16[1,24,3456]{2,1,0:T(8,128)(2,1)S(1)}, bf16[1,24,3456]{2,1,0:T(8,128)(2,1)S(1)}, u32[]{:S(2)}, u32[]{:S(2)}) collective-permute-start(bf16[1,24,3456]{2,1,0:T(8,128)(2,1)S(1)} %get-tuple-element.95), channel_id=1, source_target_pairs={{0,16},{1,17},{2,18},{3,19},{4,20},{5,21},{6,22},{7,23},{8,24},{9,... | collective-permute-start | bytes 497672 | tf_op jit(solution)/shard_map/ppermute | solution.py:418
  8.4 14.1 %collective-permute-start = (bf16[1,24,3456]{2,1,0:T(8,128)(2,1)S(1)}, bf16[1,24,3456]{2,1,0:T(8,128)(2,1)}, u32[]{:S(2)}, u32[]{:S(2)}) collective-permute-start(bf16[1,24,3456]{2,1,0:T(8,128)(2,1)S(1)} %get-tuple-element.95), channel_id=1, source_target_pairs={{0,8},{1,9},{2,10},{3,11},{4,12},{5,13},{6,14},{7,15},{8,0},{9,1},... | collective-permute-start | bytes 497672 | tf_op jit(solution)/shard_map/ppermute | solution.py:418
  9.0 6.2 %collective-permute-start.3 = (bf16[1,2,352]{2,1,0:T(2,128)(2,1)S(1)}, bf16[1,2,352]{2,1,0:T(2,128)(2,1)S(1)}, u32[]{:S(2)}, u32[]{:S(2)}) collective-permute-start(bf16[1,2,352]{2,1,0:T(2,128)(2,1)S(1)} %maximum_bitcast_fusion.1), channel_id=1, source_target_pairs={{0,1},{1,0},{2,3},{3,2},{4,5},{5,4},{6,7},{7,6},{8,9},{9,8},{10,11... | collective-permute-start | bytes 4232 | tf_op jit(solution)/shard_map/ppermute | solution.py:418
  9.8 32.5 %copy-start.21 = (bf16[1,24,768]{2,1,0:T(8,128)(2,1)}, bf16[1,24,768]{2,1,0:T(8,128)(2,1)S(1)}, u32[]{:S(2)}) copy-start(bf16[1,24,768]{2,1,0:T(8,128)(2,1)S(1)} %get-tuple-element.215) | copy-start | bytes 110596
  9.8 32.5 %copy-start.22 = (bf16[1,24,768]{2,1,0:T(8,128)(2,1)}, bf16[1,24,768]{2,1,0:T(8,128)(2,1)S(1)}, u32[]{:S(2)}) copy-start(bf16[1,24,768]{2,1,0:T(8,128)(2,1)S(1)} %get-tuple-element.216) | copy-start | bytes 110596
  15.3 6.6 %collective-permute-start.4 = (bf16[2,2,352]{2,1,0:T(2,128)(2,1)S(1)}, bf16[2,2,352]{2,1,0:T(2,128)(2,1)S(1)}, u32[]{:S(2)}, u32[]{:S(2)}) collective-permute-start(bf16[2,2,352]{2,1,0:T(2,128)(2,1)S(1)} %broadcast_select_fusion.4), channel_id=1, source_target_pairs={{0,2},{1,3},{2,0},{3,1},{4,6},{5,7},{6,4},{7,5},{8,10},{9,11},{10,... | collective-permute-start | bytes 8456 | tf_op jit(solution)/shard_map/ppermute | solution.py:418
  23.4 18.0 %collective-permute-start.5 = (bf16[1,24,4992]{2,1,0:T(8,128)(2,1)}, bf16[1,24,4992]{2,1,0:T(8,128)(2,1)S(1)}, u32[]{:S(2)}, u32[]{:S(2)}) collective-permute-start(bf16[1,24,4992]{2,1,0:T(8,128)(2,1)} %get-tuple-element.99), channel_id=1, source_target_pairs={{0,8},{1,9},{2,10},{3,11},{4,12},{5,13},{6,14},{7,15},{8,0},{9,1},... | collective-permute-start | bytes 718856 | tf_op jit(solution)/shard_map/ppermute | solution.py:418
  24.3 18.0 %collective-permute-start.6 = (bf16[4,24,3456]{2,1,0:T(8,128)(2,1)S(1)}, bf16[4,24,3456]{2,1,0:T(8,128)(2,1)S(1)}, u32[]{:S(2)}, u32[]{:S(2)}) collective-permute-start(bf16[4,24,3456]{2,1,0:T(8,128)(2,1)S(1)} %pad_maximum_fusion.3), channel_id=1, source_target_pairs={{0,2},{1,3},{2,0},{3,1},{4,6},{5,7},{6,4},{7,5},{8,10},{9,11},{10,... | collective-permute-start | bytes 1990664 | tf_op jit(solution)/shard_map/ppermute | solution.py:418
  25.1 17.3 %collective-permute-start.7 = (bf16[4,24,3456]{2,1,0:T(8,128)(2,1)S(1)}, bf16[4,24,3456]{2,1,0:T(8,128)(2,1)S(1)}, u32[]{:S(2)}, u32[]{:S(2)}) collective-permute-start(bf16[4,24,3456]{2,1,0:T(8,128)(2,1)S(1)} %pad_maximum_fusion.3), channel_id=1, source_target_pairs={{0,4},{1,5},{2,6},{3,7},{4,0},{5,1},{6,2},{7,3},{8,12},{9,13},{10,... | collective-permute-start | bytes 1990664 | tf_op jit(solution)/shard_map/ppermute | solution.py:418
  26.6 14.8 %collective-permute-start.9 = (bf16[4,2,352]{2,1,0:T(2,128)(2,1)S(1)}, bf16[4,2,352]{2,1,0:T(2,128)(2,1)S(1)}, u32[]{:S(2)}, u32[]{:S(2)}) collective-permute-start(bf16[4,2,352]{2,1,0:T(2,128)(2,1)S(1)} %broadcast_select_fusion.3), channel_id=1, source_target_pairs={{0,4},{1,5},{2,6},{3,7},{4,0},{5,1},{6,2},{7,3},{8,12},{9,13},{10,... | collective-permute-start | bytes 16904 | tf_op jit(solution)/shard_map/ppermute | solution.py:418
  42.4 4.0 %collective-permute-start.12 = (bf16[8,2,352]{2,1,0:T(2,128)(2,1)S(1)}, bf16[8,2,352]{2,1,0:T(2,128)(2,1)S(1)}, u32[]{:S(2)}, u32[]{:S(2)}) collective-permute-start(bf16[8,2,352]{2,1,0:T(2,128)(2,1)S(1)} %broadcast_select_fusion.2), channel_id=1, source_target_pairs={{0,8},{1,9},{2,10},{3,11},{4,12},{5,13},{6,14},{7,15},{8,0},{9,1},... | collective-permute-start | bytes 33800 | tf_op jit(solution)/shard_map/ppermute | solution.py:418
  43.6 7.2 %collective-permute-start.10 = (bf16[2,24,3456]{2,1,0:T(8,128)(2,1)S(1)}, bf16[2,24,3456]{2,1,0:T(8,128)(2,1)S(1)}, u32[]{:S(2)}, u32[]{:S(2)}) collective-permute-start(bf16[2,24,3456]{2,1,0:T(8,128)(2,1)S(1)} %slice.493), channel_id=1, source_target_pairs={{0,4},{1,5},{2,6},{3,7},{4,0},{5,1},{6,2},{7,3},{8,12},{9,13},{10,... | collective-permute-start | bytes 995336 | tf_op jit(solution)/shard_map/ppermute | solution.py:418
  45.1 7.1 %collective-permute-start.11 = (bf16[2,24,3456]{2,1,0:T(8,128)(2,1)S(1)}, bf16[2,24,3456]{2,1,0:T(8,128)(2,1)S(1)}, u32[]{:S(2)}, u32[]{:S(2)}) collective-permute-start(bf16[2,24,3456]{2,1,0:T(8,128)(2,1)S(1)} %slice.494), channel_id=1, source_target_pairs={{0,2},{1,3},{2,0},{3,1},{4,6},{5,7},{6,4},{7,5},{8,10},{9,11},{10,... | collective-permute-start | bytes 995336 | tf_op jit(solution)/shard_map/ppermute | solution.py:418
  52.2 30.3 %copy-start.4 = (bf16[16,24,3456]{2,1,0:T(8,128)(2,1)}, bf16[16,24,3456]{2,1,0:T(8,128)(2,1)S(1)}, u32[]{:S(2)}) copy-start(bf16[16,24,3456]{2,1,0:T(8,128)(2,1)S(1)} %constant_dynamic-update-slice_fusion.own_ref) | copy-start | bytes 7962628
  52.2 5.4 %collective-permute-start.13 = (bf16[16,2,352]{2,1,0:T(2,128)(2,1)S(1)}, bf16[16,2,352]{2,1,0:T(2,128)(2,1)S(1)}, u32[]{:S(2)}, u32[]{:S(2)}) collective-permute-start(bf16[16,2,352]{2,1,0:T(2,128)(2,1)S(1)} %broadcast_select_fusion.1), channel_id=1, source_target_pairs={{0,16},{1,17},{2,18},{3,19},{4,20},{5,21},{6,22},{7,23},{8,24},{9,... | collective-permute-start | bytes 67592 | tf_op jit(solution)/shard_map/ppermute | solution.py:418
  55.3 27.2 %collective-permute-start.14 = (bf16[16,24,3456]{2,1,0:T(8,128)(2,1)S(1)}, bf16[16,24,3456]{2,1,0:T(8,128)(2,1)}, u32[]{:S(2)}, u32[]{:S(2)}) collective-permute-start(bf16[16,24,3456]{2,1,0:T(8,128)(2,1)S(1)} %constant_dynamic-update-slice_fusion.own_ref), channel_id=1, source_target_pairs={{0,1},{1,0},{2,3},{3,2},{4,5},{5,4},{6,7},{7,6},{8,9},{9,8},{10,11... | collective-permute-start | bytes 7962632 | tf_op jit(solution)/shard_map/ppermute | solution.py:418
  56.1 24.7 %collective-permute-start.8 = (bf16[2,24,4992]{2,1,0:T(8,128)(2,1)}, bf16[2,24,4992]{2,1,0:T(8,128)(2,1)S(1)}, u32[]{:S(2)}, u32[]{:S(2)}) collective-permute-start(bf16[2,24,4992]{2,1,0:T(8,128)(2,1)} %pad_maximum_fusion.7), channel_id=1, source_target_pairs={{0,16},{1,17},{2,18},{3,19},{4,20},{5,21},{6,22},{7,23},{8,24},{9,... | collective-permute-start | bytes 1437704 | tf_op jit(solution)/shard_map/ppermute | solution.py:418
  56.3 21.2 %collective-permute-start.15 = (bf16[1,48,768]{2,1,0:T(8,128)(2,1)}, bf16[1,48,768]{2,1,0:T(8,128)(2,1)}, u32[]{:S(2)}, u32[]{:S(2)}) collective-permute-start(bf16[1,48,768]{2,1,0:T(8,128)(2,1)} %get-tuple-element.111), channel_id=1, source_target_pairs={{0,8},{1,9},{2,10},{3,11},{4,12},{5,13},{6,14},{7,15},{8,0},{9,1},... | collective-permute-start | bytes 221192 | tf_op jit(solution)/shard_map/ppermute | solution.py:418
  87.8 22.9 %collective-permute-start.16 = (bf16[4,24,4992]{2,1,0:T(8,128)(2,1)S(1)}, bf16[4,24,4992]{2,1,0:T(8,128)(2,1)S(1)}, u32[]{:S(2)}, u32[]{:S(2)}) collective-permute-start(bf16[4,24,4992]{2,1,0:T(8,128)(2,1)S(1)} %pad_maximum_fusion), channel_id=1, source_target_pairs={{0,2},{1,3},{2,0},{3,1},{4,6},{5,7},{6,4},{7,5},{8,10},{9,11},{10,... | collective-permute-start | bytes 2875400 | tf_op jit(solution)/shard_map/ppermute | solution.py:418
  89.5 22.6 %collective-permute-start.17 = (bf16[4,24,4992]{2,1,0:T(8,128)(2,1)S(1)}, bf16[4,24,4992]{2,1,0:T(8,128)(2,1)S(1)}, u32[]{:S(2)}, u32[]{:S(2)}) collective-permute-start(bf16[4,24,4992]{2,1,0:T(8,128)(2,1)S(1)} %pad_maximum_fusion), channel_id=1, source_target_pairs={{0,4},{1,5},{2,6},{3,7},{4,0},{5,1},{6,2},{7,3},{8,12},{9,13},{10,... | collective-permute-start | bytes 2875400 | tf_op jit(solution)/shard_map/ppermute | solution.py:418
  90.0 11.6 %collective-permute-start.20 = (bf16[2,48,768]{2,1,0:T(8,128)(2,1)S(1)}, bf16[2,48,768]{2,1,0:T(8,128)(2,1)S(1)}, u32[]{:S(2)}, u32[]{:S(2)}) collective-permute-start(bf16[2,48,768]{2,1,0:T(8,128)(2,1)S(1)} %pad_maximum_fusion.13), channel_id=1, source_target_pairs={{0,16},{1,17},{2,18},{3,19},{4,20},{5,21},{6,22},{7,23},{8,24},{9,... | collective-permute-start | bytes 442376 | tf_op jit(solution)/shard_map/ppermute | solution.py:418
  112.2 11.5 %collective-permute-start.18 = (bf16[2,24,4992]{2,1,0:T(8,128)(2,1)S(1)}, bf16[2,24,4992]{2,1,0:T(8,128)(2,1)S(1)}, u32[]{:S(2)}, u32[]{:S(2)}) collective-permute-start(bf16[2,24,4992]{2,1,0:T(8,128)(2,1)S(1)} %slice.506), channel_id=1, source_target_pairs={{0,4},{1,5},{2,6},{3,7},{4,0},{5,1},{6,2},{7,3},{8,12},{9,13},{10,... | collective-permute-start | bytes 1437704 | tf_op jit(solution)/shard_map/ppermute | solution.py:418
  112.7 11.7 %collective-permute-start.19 = (bf16[2,24,4992]{2,1,0:T(8,128)(2,1)S(1)}, bf16[2,24,4992]{2,1,0:T(8,128)(2,1)S(1)}, u32[]{:S(2)}, u32[]{:S(2)}) collective-permute-start(bf16[2,24,4992]{2,1,0:T(8,128)(2,1)S(1)} %slice.507), channel_id=1, source_target_pairs={{0,2},{1,3},{2,0},{3,1},{4,6},{5,7},{6,4},{7,5},{8,10},{9,11},{10,... | collective-permute-start | bytes 1437704 | tf_op jit(solution)/shard_map/ppermute | solution.py:418
  125.3 9.9 %collective-permute-start.21 = (bf16[16,24,4992]{2,1,0:T(8,128)(2,1)}, bf16[16,24,4992]{2,1,0:T(8,128)(2,1)S(1)}, u32[]{:S(2)}, u32[]{:S(2)}) collective-permute-start(bf16[16,24,4992]{2,1,0:T(8,128)(2,1)} %constant_dynamic-update-slice_fusion.8.own_ref), channel_id=1, source_target_pairs={{0,1},{1,0},{2,3},{3,2},{4,5},{5,4},{6,7},{7,6},{8,9},{9,8},{10,11... | collective-permute-start | bytes 11501576 | tf_op jit(solution)/shard_map/ppermute | solution.py:418
  125.3 9.4 %collective-permute-start.22 = (bf16[4,48,768]{2,1,0:T(8,128)(2,1)S(1)}, bf16[4,48,768]{2,1,0:T(8,128)(2,1)S(1)}, u32[]{:S(2)}, u32[]{:S(2)}) collective-permute-start(bf16[4,48,768]{2,1,0:T(8,128)(2,1)S(1)} %pad_maximum_fusion.8), channel_id=1, source_target_pairs={{0,2},{1,3},{2,0},{3,1},{4,6},{5,7},{6,4},{7,5},{8,10},{9,11},{10,... | collective-permute-start | bytes 884744 | tf_op jit(solution)/shard_map/ppermute | solution.py:418
  125.9 9.1 %collective-permute-start.23 = (bf16[4,48,768]{2,1,0:T(8,128)(2,1)S(1)}, bf16[4,48,768]{2,1,0:T(8,128)(2,1)S(1)}, u32[]{:S(2)}, u32[]{:S(2)}) collective-permute-start(bf16[4,48,768]{2,1,0:T(8,128)(2,1)S(1)} %pad_maximum_fusion.8), channel_id=1, source_target_pairs={{0,4},{1,5},{2,6},{3,7},{4,0},{5,1},{6,2},{7,3},{8,12},{9,13},{10,... | collective-permute-start | bytes 884744 | tf_op jit(solution)/shard_map/ppermute | solution.py:418
  143.9 5.2 %collective-permute-start.24 = (bf16[2,48,768]{2,1,0:T(8,128)(2,1)S(1)}, bf16[2,48,768]{2,1,0:T(8,128)(2,1)S(1)}, u32[]{:S(2)}, u32[]{:S(2)}) collective-permute-start(bf16[2,48,768]{2,1,0:T(8,128)(2,1)S(1)} %slice.508), channel_id=1, source_target_pairs={{0,4},{1,5},{2,6},{3,7},{4,0},{5,1},{6,2},{7,3},{8,12},{9,13},{10,... | collective-permute-start | bytes 442376 | tf_op jit(solution)/shard_map/ppermute | solution.py:418
  144.8 5.1 %collective-permute-start.25 = (bf16[2,48,768]{2,1,0:T(8,128)(2,1)S(1)}, bf16[2,48,768]{2,1,0:T(8,128)(2,1)S(1)}, u32[]{:S(2)}, u32[]{:S(2)}) collective-permute-start(bf16[2,48,768]{2,1,0:T(8,128)(2,1)S(1)} %slice.509), channel_id=1, source_target_pairs={{0,2},{1,3},{2,0},{3,1},{4,6},{5,7},{6,4},{7,5},{8,10},{9,11},{10,... | collective-permute-start | bytes 442376 | tf_op jit(solution)/shard_map/ppermute | solution.py:418
  150.0 12.4 %collective-permute-start.26 = (bf16[16,48,768]{2,1,0:T(8,128)(2,1)S(1)}, bf16[16,48,768]{2,1,0:T(8,128)(2,1)S(1)}, u32[]{:S(2)}, u32[]{:S(2)}) collective-permute-start(bf16[16,48,768]{2,1,0:T(8,128)(2,1)S(1)} %constant_dynamic-update-slice_fusion.15.own_ref), channel_id=1, source_target_pairs={{0,1},{1,0},{2,3},{3,2},{4,5},{5,4},{6,7},{7,6},{8,9},{9,8},{10,11... | collective-permute-start | bytes 3538952 | tf_op jit(solution)/shard_map/ppermute | solution.py:418
  172.1 12.3 %collective-permute-start.27 = (bf16[4,4,48,768]{3,2,1,0:T(8,128)(2,1)}, bf16[4,4,48,768]{3,2,1,0:T(8,128)(2,1)S(1)}, u32[]{:S(2)}, u32[]{:S(2)}) collective-permute-start(bf16[4,4,48,768]{3,2,1,0:T(8,128)(2,1)} %get-tuple-element.135), channel_id=1, source_target_pairs={{0,1},{1,0},{2,3},{3,2},{4,5},{5,4},{6,7},{7,6},{8,9},{9,8},{10,11... | collective-permute-start | bytes 3538952 | tf_op jit(solution)/shard_map/ppermute | solution.py:418
  184.6 16.3 %collective-permute-start.28 = (bf16[2,48,768]{2,1,0:T(8,128)(2,1)S(1)}, bf16[2,48,768]{2,1,0:T(8,128)(2,1)S(1)}, u32[]{:S(2)}, u32[]{:S(2)}) collective-permute-start(bf16[2,48,768]{2,1,0:T(8,128)(2,1)S(1)} %get-tuple-element.141), channel_id=1, source_target_pairs={{0,4},{1,5},{2,6},{3,7},{4,0},{5,1},{6,2},{7,3},{8,12},{9,13},{10,... | collective-permute-start | bytes 442376 | tf_op jit(solution)/shard_map/ppermute | solution.py:418
  185.8 15.1 %collective-permute-start.29 = (bf16[2,48,768]{2,1,0:T(8,128)(2,1)S(1)}, bf16[2,48,768]{2,1,0:T(8,128)(2,1)S(1)}, u32[]{:S(2)}, u32[]{:S(2)}) collective-permute-start(bf16[2,48,768]{2,1,0:T(8,128)(2,1)S(1)} %get-tuple-element.142), channel_id=1, source_target_pairs={{0,2},{1,3},{2,0},{3,1},{4,6},{5,7},{6,4},{7,5},{8,10},{9,11},{10,... | collective-permute-start | bytes 442376 | tf_op jit(solution)/shard_map/ppermute | solution.py:418
  201.9 15.5 %collective-permute-start.30 = (bf16[4,4,24,4992]{3,2,1,0:T(8,128)(2,1)}, bf16[4,4,24,4992]{3,2,1,0:T(8,128)(2,1)S(1)}, u32[]{:S(2)}, u32[]{:S(2)}) collective-permute-start(bf16[4,4,24,4992]{3,2,1,0:T(8,128)(2,1)} %get-tuple-element.148), channel_id=1, source_target_pairs={{0,1},{1,0},{2,3},{3,2},{4,5},{5,4},{6,7},{7,6},{8,9},{9,8},{10,11... | collective-permute-start | bytes 11501576 | tf_op jit(solution)/shard_map/ppermute | solution.py:418
  201.9 13.6 %collective-permute-start.31 = (bf16[4,48,768]{2,1,0:T(8,128)(2,1)}, bf16[4,48,768]{2,1,0:T(8,128)(2,1)S(1)}, u32[]{:S(2)}, u32[]{:S(2)}) collective-permute-start(bf16[4,48,768]{2,1,0:T(8,128)(2,1)} %get-tuple-element.149), channel_id=1, source_target_pairs={{0,2},{1,3},{2,0},{3,1},{4,6},{5,7},{6,4},{7,5},{8,10},{9,11},{10,... | collective-permute-start | bytes 884744 | tf_op jit(solution)/shard_map/ppermute | solution.py:418
  202.5 12.9 %collective-permute-start.32 = (bf16[4,48,768]{2,1,0:T(8,128)(2,1)}, bf16[4,48,768]{2,1,0:T(8,128)(2,1)S(1)}, u32[]{:S(2)}, u32[]{:S(2)}) collective-permute-start(bf16[4,48,768]{2,1,0:T(8,128)(2,1)} %get-tuple-element.150), channel_id=1, source_target_pairs={{0,4},{1,5},{2,6},{3,7},{4,0},{5,1},{6,2},{7,3},{8,12},{9,13},{10,... | collective-permute-start | bytes 884744 | tf_op jit(solution)/shard_map/ppermute | solution.py:418
  217.4 43.8 %copy-start.2 = (bf16[4,4,24,4992]{3,2,1,0:T(8,128)(2,1)}, bf16[4,4,24,4992]{3,2,1,0:T(8,128)(2,1)S(1)}, u32[]{:S(2)}) copy-start(bf16[4,4,24,4992]{3,2,1,0:T(8,128)(2,1)S(1)} %collective-permute-done.30) | copy-start | bytes 11501572
  219.2 13.5 %collective-permute-start.33 = (bf16[2,48,768]{2,1,0:T(8,128)(2,1)}, bf16[2,48,768]{2,1,0:T(8,128)(2,1)S(1)}, u32[]{:S(2)}, u32[]{:S(2)}) collective-permute-start(bf16[2,48,768]{2,1,0:T(8,128)(2,1)} %fusion.35), channel_id=1, source_target_pairs={{0,16},{1,17},{2,18},{3,19},{4,20},{5,21},{6,22},{7,23},{8,24},{9,... | collective-permute-start | bytes 442376 | tf_op jit(solution)/shard_map/ppermute | solution.py:418
  220.0 13.8 %collective-permute-start.35 = (bf16[2,24,4992]{2,1,0:T(8,128)(2,1)}, bf16[2,24,4992]{2,1,0:T(8,128)(2,1)}, u32[]{:S(2)}, u32[]{:S(2)}) collective-permute-start(bf16[2,24,4992]{2,1,0:T(8,128)(2,1)} %get-tuple-element.162), channel_id=1, source_target_pairs={{0,2},{1,3},{2,0},{3,1},{4,6},{5,7},{6,4},{7,5},{8,10},{9,11},{10,... | collective-permute-start | bytes 1437704 | tf_op jit(solution)/shard_map/ppermute | solution.py:418
  221.4 12.6 %collective-permute-start.34 = (bf16[2,24,4992]{2,1,0:T(8,128)(2,1)}, bf16[2,24,4992]{2,1,0:T(8,128)(2,1)}, u32[]{:S(2)}, u32[]{:S(2)}) collective-permute-start(bf16[2,24,4992]{2,1,0:T(8,128)(2,1)} %get-tuple-element.161), channel_id=1, source_target_pairs={{0,4},{1,5},{2,6},{3,7},{4,0},{5,1},{6,2},{7,3},{8,12},{9,13},{10,... | collective-permute-start | bytes 1437704 | tf_op jit(solution)/shard_map/ppermute | solution.py:418
  236.0 5.0 %collective-permute-start.36 = (bf16[4,4,24,3456]{3,2,1,0:T(8,128)(2,1)S(1)}, bf16[4,4,24,3456]{3,2,1,0:T(8,128)(2,1)S(1)}, u32[]{:S(2)}, u32[]{:S(2)}) collective-permute-start(bf16[4,4,24,3456]{3,2,1,0:T(8,128)(2,1)S(1)} %copy-done.36), channel_id=1, source_target_pairs={{0,1},{1,0},{2,3},{3,2},{4,5},{5,4},{6,7},{7,6},{8,9},{9,8},{10,11... | collective-permute-start | bytes 7962632 | tf_op jit(solution)/shard_map/ppermute | solution.py:418
  236.0 24.1 %collective-permute-start.42 = (bf16[4,24,4992]{2,1,0:T(8,128)(2,1)S(1)}, bf16[4,24,4992]{2,1,0:T(8,128)(2,1)S(1)}, u32[]{:S(2)}, u32[]{:S(2)}) collective-permute-start(bf16[4,24,4992]{2,1,0:T(8,128)(2,1)S(1)} %pad_maximum_fusion.2), channel_id=1, source_target_pairs={{0,4},{1,5},{2,6},{3,7},{4,0},{5,1},{6,2},{7,3},{8,12},{9,13},{10,... | collective-permute-start | bytes 2875400 | tf_op jit(solution)/shard_map/ppermute | solution.py:418
  237.1 24.1 %collective-permute-start.41 = (bf16[4,24,4992]{2,1,0:T(8,128)(2,1)S(1)}, bf16[4,24,4992]{2,1,0:T(8,128)(2,1)S(1)}, u32[]{:S(2)}, u32[]{:S(2)}) collective-permute-start(bf16[4,24,4992]{2,1,0:T(8,128)(2,1)S(1)} %pad_maximum_fusion.1), channel_id=1, source_target_pairs={{0,2},{1,3},{2,0},{3,1},{4,6},{5,7},{6,4},{7,5},{8,10},{9,11},{10,... | collective-permute-start | bytes 2875400 | tf_op jit(solution)/shard_map/ppermute | solution.py:418
  237.8 4.4 %collective-permute-start.37 = (bf16[1,48,768]{2,1,0:T(8,128)(2,1)S(1)}, bf16[1,48,768]{2,1,0:T(8,128)(2,1)S(1)}, u32[]{:S(2)}, u32[]{:S(2)}) collective-permute-start(bf16[1,48,768]{2,1,0:T(8,128)(2,1)S(1)} %fusion.47), channel_id=1, source_target_pairs={{0,8},{1,9},{2,10},{3,11},{4,12},{5,13},{6,14},{7,15},{8,0},{9,1},... | collective-permute-start | bytes 221192 | tf_op jit(solution)/shard_map/ppermute | solution.py:418
  240.9 26.6 %copy-start.6 = (bf16[4,4,24,3456]{3,2,1,0:T(8,128)(2,1)}, bf16[4,4,24,3456]{3,2,1,0:T(8,128)(2,1)S(1)}, u32[]{:S(2)}) copy-start(bf16[4,4,24,3456]{3,2,1,0:T(8,128)(2,1)S(1)} %collective-permute-done.36) | copy-start | bytes 7962628
  242.3 25.7 %copy-start.31 = (bf16[1,48,768]{2,1,0:T(8,128)(2,1)}, bf16[1,48,768]{2,1,0:T(8,128)(2,1)S(1)}, u32[]{:S(2)}) copy-start(bf16[1,48,768]{2,1,0:T(8,128)(2,1)S(1)} %collective-permute-done.37) | copy-start | bytes 221188
  242.3 25.3 %collective-permute-start.39 = (bf16[2,24,3456]{2,1,0:T(8,128)(2,1)S(1)}, bf16[2,24,3456]{2,1,0:T(8,128)(2,1)S(1)}, u32[]{:S(2)}, u32[]{:S(2)}) collective-permute-start(bf16[2,24,3456]{2,1,0:T(8,128)(2,1)S(1)} %get-tuple-element.166), channel_id=1, source_target_pairs={{0,2},{1,3},{2,0},{3,1},{4,6},{5,7},{6,4},{7,5},{8,10},{9,11},{10,... | collective-permute-start | bytes 995336 | tf_op jit(solution)/shard_map/ppermute | solution.py:418
  243.6 23.9 %collective-permute-start.38 = (bf16[2,24,3456]{2,1,0:T(8,128)(2,1)S(1)}, bf16[2,24,3456]{2,1,0:T(8,128)(2,1)S(1)}, u32[]{:S(2)}, u32[]{:S(2)}) collective-permute-start(bf16[2,24,3456]{2,1,0:T(8,128)(2,1)S(1)} %get-tuple-element.165), channel_id=1, source_target_pairs={{0,4},{1,5},{2,6},{3,7},{4,0},{5,1},{6,2},{7,3},{8,12},{9,13},{10,... | collective-permute-start | bytes 995336 | tf_op jit(solution)/shard_map/ppermute | solution.py:418
  262.3 19.5 %copy-start = (bf16[32,1,48,768]{3,2,1,0:T(8,128)(2,1)S(1)}, bf16[32,1,48,768]{3,2,1,0:T(8,128)(2,1)}, u32[]{:S(2)}) copy-start(bf16[32,1,48,768]{3,2,1,0:T(8,128)(2,1)} %place.5) | copy-start | bytes 7077892
  262.3 19.5 %copy-start.9 = (f32[128,768]{1,0:T(8,128)S(1)}, f32[128,768]{1,0:T(8,128)}, u32[]{:S(2)}) copy-start(f32[128,768]{1,0:T(8,128)} %convolution_add_fusion.1.resid_ref) | copy-start | bytes 1179652
  267.5 1.3 collective-permute-start.40
  268.9 5.6 %collective-permute-start.43 = (f32[2,8,1792]{2,1,0:T(8,128)S(1)}, f32[2,8,1792]{2,1,0:T(8,128)S(1)}, u32[]{:S(2)}, u32[]{:S(2)}) collective-permute-start(f32[2,8,1792]{2,1,0:T(8,128)S(1)} %fusion.68), channel_id=1, source_target_pairs={{0,2},{1,3},{2,0},{3,1},{4,6},{5,7},{6,4},{7,5},{8,10},{9,11},{10,... | collective-permute-start | bytes 344072 | tf_op jit(solution)/shard_map/ppermute | solution.py:418
  269.6 25.1 %collective-permute-start.48 = (bf16[2,24,4992]{2,1,0:T(8,128)(2,1)}, bf16[2,24,4992]{2,1,0:T(8,128)(2,1)}, u32[]{:S(2)}, u32[]{:S(2)}) collective-permute-start(bf16[2,24,4992]{2,1,0:T(8,128)(2,1)} %fusion.3), channel_id=1, source_target_pairs={{0,16},{1,17},{2,18},{3,19},{4,20},{5,21},{6,22},{7,23},{8,24},{9,... | collective-permute-start | bytes 1437704 | tf_op jit(solution)/shard_map/ppermute | solution.py:418
  274.5 5.0 %collective-permute-start.44 = (f32[2,8,1792]{2,1,0:T(8,128)S(1)}, f32[2,8,1792]{2,1,0:T(8,128)}, u32[]{:S(2)}, u32[]{:S(2)}) collective-permute-start(f32[2,8,1792]{2,1,0:T(8,128)S(1)} %fusion.69), channel_id=1, source_target_pairs={{0,4},{1,5},{2,6},{3,7},{4,0},{5,1},{6,2},{7,3},{8,12},{9,13},{10,... | collective-permute-start | bytes 344072 | tf_op jit(solution)/shard_map/ppermute | solution.py:418
  280.4 14.2 %collective-permute-start.45 = (f32[2,8,1792]{2,1,0:T(8,128)S(1)}, f32[2,8,1792]{2,1,0:T(8,128)S(1)}, u32[]{:S(2)}, u32[]{:S(2)}) collective-permute-start(f32[2,8,1792]{2,1,0:T(8,128)S(1)} %add.413), channel_id=1, source_target_pairs={{0,8},{1,9},{2,10},{3,11},{4,12},{5,13},{6,14},{7,15},{8,0},{9,1},... | collective-permute-start | bytes 344072 | tf_op jit(solution)/shard_map/ppermute | solution.py:418
  284.0 22.0 %copy-start.30 = (bf16[2,48,768]{2,1,0:T(8,128)(2,1)S(1)}, bf16[2,48,768]{2,1,0:T(8,128)(2,1)}, u32[]{:S(2)}) copy-start(bf16[2,48,768]{2,1,0:T(8,128)(2,1)} %copy-done.29) | copy-start | bytes 442372
  284.0 22.0 %copy-start.32 = (bf16[1,48,768]{2,1,0:T(8,128)(2,1)S(1)}, bf16[1,48,768]{2,1,0:T(8,128)(2,1)}, u32[]{:S(2)}) copy-start(bf16[1,48,768]{2,1,0:T(8,128)(2,1)} %copy-done.31) | copy-start | bytes 221188
  284.0 15.4 %collective-permute-start.47 = (bf16[4,24,3456]{2,1,0:T(8,128)(2,1)S(1)}, bf16[4,24,3456]{2,1,0:T(8,128)(2,1)S(1)}, u32[]{:S(2)}, u32[]{:S(2)}) collective-permute-start(bf16[4,24,3456]{2,1,0:T(8,128)(2,1)S(1)} %copy-done.20), channel_id=1, source_target_pairs={{0,4},{1,5},{2,6},{3,7},{4,0},{5,1},{6,2},{7,3},{8,12},{9,13},{10,... | collective-permute-start | bytes 1990664 | tf_op jit(solution)/shard_map/ppermute | solution.py:418
  284.9 15.1 %collective-permute-start.46 = (bf16[4,24,3456]{2,1,0:T(8,128)(2,1)S(1)}, bf16[4,24,3456]{2,1,0:T(8,128)(2,1)S(1)}, u32[]{:S(2)}, u32[]{:S(2)}) collective-permute-start(bf16[4,24,3456]{2,1,0:T(8,128)(2,1)S(1)} %pad_maximum_fusion.4), channel_id=1, source_target_pairs={{0,2},{1,3},{2,0},{3,1},{4,6},{5,7},{6,4},{7,5},{8,10},{9,11},{10,... | collective-permute-start | bytes 1990664 | tf_op jit(solution)/shard_map/ppermute | solution.py:418
  301.6 9.0 %collective-permute-start.53 = (bf16[1,24,3456]{2,1,0:T(8,128)(2,1)S(1)}, bf16[1,24,3456]{2,1,0:T(8,128)(2,1)S(1)}, u32[]{:S(2)}, u32[]{:S(2)}) collective-permute-start(bf16[1,24,3456]{2,1,0:T(8,128)(2,1)S(1)} %get-tuple-element.178), channel_id=1, source_target_pairs={{0,24},{1,25},{2,26},{3,27},{4,28},{5,29},{6,30},{7,31},{8,16},{9,... | collective-permute-start | bytes 497672 | tf_op jit(solution)/shard_map/ppermute | solution.py:418
  303.9 12.1 %collective-permute-start.52 = (bf16[1,24,3456]{2,1,0:T(8,128)(2,1)S(1)}, bf16[1,24,3456]{2,1,0:T(8,128)(2,1)S(1)}, u32[]{:S(2)}, u32[]{:S(2)}) collective-permute-start(bf16[1,24,3456]{2,1,0:T(8,128)(2,1)S(1)} %get-tuple-element.177), channel_id=1, source_target_pairs={{0,16},{1,17},{2,18},{3,19},{4,20},{5,21},{6,22},{7,23},{8,24},{9,... | collective-permute-start | bytes 497672 | tf_op jit(solution)/shard_map/ppermute | solution.py:418
  303.9 12.2 %collective-permute-start.51 = (bf16[1,24,3456]{2,1,0:T(8,128)(2,1)S(1)}, bf16[1,24,3456]{2,1,0:T(8,128)(2,1)S(1)}, u32[]{:S(2)}, u32[]{:S(2)}) collective-permute-start(bf16[1,24,3456]{2,1,0:T(8,128)(2,1)S(1)} %get-tuple-element.176), channel_id=1, source_target_pairs={{0,8},{1,9},{2,10},{3,11},{4,12},{5,13},{6,14},{7,15},{8,0},{9,1},... | collective-permute-start | bytes 497672 | tf_op jit(solution)/shard_map/ppermute | solution.py:418
  307.1 12.2 %collective-permute-start.49 = (bf16[1,24,4992]{2,1,0:T(8,128)(2,1)S(1)}, bf16[1,24,4992]{2,1,0:T(8,128)(2,1)S(1)}, u32[]{:S(2)}, u32[]{:S(2)}) collective-permute-start(bf16[1,24,4992]{2,1,0:T(8,128)(2,1)S(1)} %fusion.18), channel_id=1, source_target_pairs={{0,8},{1,9},{2,10},{3,11},{4,12},{5,13},{6,14},{7,15},{8,0},{9,1},... | collective-permute-start | bytes 718856 | tf_op jit(solution)/shard_map/ppermute | solution.py:418
  320.7 6.8 %collective-permute-start.50 = (f32[2,8,1792]{2,1,0:T(8,128)S(1)}, f32[2,8,1792]{2,1,0:T(8,128)S(1)}, u32[]{:S(2)}, u32[]{:S(2)}) collective-permute-start(f32[2,8,1792]{2,1,0:T(8,128)S(1)} %add.414), channel_id=1, source_target_pairs={{0,16},{1,17},{2,18},{3,19},{4,20},{5,21},{6,22},{7,23},{8,24},{9,... | collective-permute-start | bytes 344072 | tf_op jit(solution)/shard_map/ppermute | solution.py:418
  (27 other events, 194.9 us)

commit v3 on v2

--- a/solution.py
+++ b/solution.py
@@ -276,7 +276,7 @@
 
 def backward_in_kernel(
     me_ref, grad_ref, resid_ref, normed_ref, dhidden_ref, in_ref, norm_ref,
-    back_ref, in_keep_ref, in_send_ref, norm_grad_ref,
+    back_ref, in_keep_ref, in_send_ref,
     gathered_ref, turned_norm_ref, dnorm_ref, first=0,
 ):
     core = me_ref[0] % 2
@@ -290,20 +290,27 @@
         dhidden = dhidden_ref[:, at]
         dnorm_ref[...] += lax.dot_general(dhidden, in_ref[:, at], NT, preferred_element_type=F32)
         gathered_ref[...] = jnp.dot(turned_norm_ref[...], dhidden, preferred_element_type=F32)
+        store(slice(None), to)
+        return carry
+
+    def store(part, to):
         depth = WIDTH // PARTS
         for pair in range(PARTS // 2):
-            even = gathered_ref[2 * pair * depth : (2 * pair + 1) * depth]
-            odd = gathered_ref[(2 * pair + 1) * depth : (2 * pair + 2) * depth]
+            even = gathered_ref[2 * pair * depth : (2 * pair + 1) * depth, part]
+            odd = gathered_ref[(2 * pair + 1) * depth : (2 * pair + 2) * depth, part]
             other = pair ^ chip
             in_keep_ref[other % 4, other // 4, :, to] = jnp.where(core == 0, even, odd).astype(LOW)
             in_send_ref[other % 4, other // 4, :, to] = jnp.where(core == 0, odd, even).astype(LOW)
-        return carry
 
     lax.fori_loop(0, PADDED // (3 * LANES), in_back, 0)
     resid = resid_ref[...]
     scale = lax.rsqrt(jnp.mean(resid * resid, axis=-1, keepdims=True) + EPSILON)
     dnorm = dnorm_ref[...]
-    norm_grad_ref[...] = jnp.sum(dnorm * resid * scale, axis=0, keepdims=True)
+    norm_grad = jnp.sum(dnorm * resid * scale, axis=0, keepdims=True)
+    column = jnp.broadcast_to(norm_grad, (LANES, WIDTH)).T
+    spare = iota((1, LANES), 1) == HEADS
+    gathered_ref[:, 2 * LANES :] = jnp.where(spare, column, gathered_ref[:, 2 * LANES :])
+    store(slice(2 * LANES, 3 * LANES), pl.ds(first + STEP_AT, LANES))
     gained = dnorm * norm_ref[...]
     pull = scale * scale * scale * jnp.mean(gained * resid, axis=-1, keepdims=True)
     back_ref[...] = grad_ref[...] + scale * gained - resid * pull
@@ -311,11 +318,11 @@
 
 def backward_both_kernel(
     me_ref, grad_ref, resid_ref, normed_ref, dhidden_ref, in_ref, norm_ref, gated_ref, out_ref,
-    back_ref, keep_ref, send_ref, norm_grad_ref, gated_grad_ref, *scratch,
+    back_ref, keep_ref, send_ref, gated_grad_ref, *scratch,
 ):
     backward_in_kernel(
         me_ref, grad_ref, resid_ref, normed_ref, dhidden_ref, in_ref, norm_ref,
-        back_ref, keep_ref, send_ref, norm_grad_ref, *scratch, first=2 * WIDTH,
+        back_ref, keep_ref, send_ref, *scratch, first=2 * WIDTH,
     )
     depth = WIDTH // PARTS
 
@@ -344,29 +351,35 @@
 
 VMEM = pl.BlockSpec(memory_space=pltpu.VMEM)
 SMEM = pl.BlockSpec(memory_space=pltpu.SMEM)
-
-
-def call(kernel, name, flops, size, outs, scratch, *args):
+ANY = pl.BlockSpec(memory_space=pl.ANY)
+
+
+def skip_first(kernel, count, *refs):
+    kernel(*refs[count:])
+
+
+def call(kernel, name, flops, size, outs, scratch, *args, awaited=()):
     return pl.pallas_call(
-        kernel,
+        partial(skip_first, kernel, len(awaited)),
         out_shape=outs,
-        in_specs=[SMEM if item.shape == (1,) else VMEM for item in args],
+        in_specs=[ANY] * len(awaited) + [SMEM if item.shape == (1,) else VMEM for item in args],
         out_specs=(VMEM,) * len(outs),
         scratch_shapes=scratch,
         compiler_params=pltpu.CompilerParams(vmem_limit_bytes=VMEM_LIMIT),
         cost_estimate=pl.CostEstimate(flops=flops, bytes_accessed=size, transcendentals=0),
         name=name,
-    )(*args)
-
-
-def forward(resid, in_full, small, segs):
+    )(*awaited, *args)
+
+
+def forward(resid, in_full, small, segs, *awaited):
     rows = resid.shape[0]
     outs = (
         shape(rows, PADDED), shape(rows, INNER), shape(rows, WIDTH, dtype=LOW), shape(rows, INNER, dtype=LOW),
     )
     scratch = mixer_scratch(rows) + [pltpu.VMEM((rows, INNER), F32)]
     return call(
-        forward_kernel, "mix_forward", 10_000_000_000, 10_000_000, outs, scratch, resid, in_full, *small, *segs
+        forward_kernel, "mix_forward", 10_000_000_000, 10_000_000, outs, scratch,
+        resid, in_full, *small, *segs, awaited=awaited,
     )
 
 
@@ -376,7 +389,7 @@
     return call(backward_out_kernel, "out_backward", 2_000_000_000, 8_000_000, outs, [], me, grad, gated, out_full)
 
 
-def backward_mixer(gated_grad, hidden, mixed, small, segs):
+def backward_mixer(gated_grad, hidden, mixed, small, segs, *awaited):
     rows = hidden.shape[0]
     outs = (shape(rows, PADDED, dtype=LOW), shape(SMALL_ROWS, CONVCH))
     scratch = mixer_scratch(rows) + [
@@ -384,33 +397,33 @@
     ]
     return call(
         backward_mixer_kernel, "mix_backward", 12_000_000_000, 5_000_000, outs, scratch,
-        gated_grad, hidden, mixed, *small[1:], *segs,
-    )
-
-
-def backward_in(me, grad, resid, normed, dhidden, in_full, norm):
+        gated_grad, hidden, mixed, *small[1:], *segs, awaited=awaited,
+    )
+
+
+def backward_in(me, grad, resid, normed, dhidden, in_full, norm, *awaited):
     rows = resid.shape[0]
     part = shape(4, 4, WIDTH // PARTS, PADDED, dtype=LOW)
-    outs = (shape(rows, WIDTH), part, part, shape(1, WIDTH))
+    outs = (shape(rows, WIDTH), part, part)
     scratch = [
         pltpu.VMEM((WIDTH, 3 * LANES), F32), pltpu.VMEM((WIDTH, rows), LOW), pltpu.VMEM((rows, WIDTH), F32),
     ]
     return call(
         backward_in_kernel, "in_backward", 6_000_000_000, 14_000_000, outs, scratch,
-        me, grad, resid, normed, dhidden, in_full, norm,
-    )
-
-
-def backward_both(me, grad, resid, normed, dhidden, in_full, norm, gated, out_full):
+        me, grad, resid, normed, dhidden, in_full, norm, awaited=awaited,
+    )
+
+
+def backward_both(me, grad, resid, normed, dhidden, in_full, norm, gated, out_full, *awaited):
     rows = resid.shape[0]
     part = shape(4, 4, WIDTH // PARTS, 2 * WIDTH + PADDED, dtype=LOW)
-    outs = (shape(rows, WIDTH), part, part, shape(1, WIDTH), shape(rows, INNER))
+    outs = (shape(rows, WIDTH), part, part, shape(rows, INNER))
     scratch = [
         pltpu.VMEM((WIDTH, 3 * LANES), F32), pltpu.VMEM((WIDTH, rows), LOW), pltpu.VMEM((rows, WIDTH), F32),
     ]
     return call(
         backward_both_kernel, "both_backward", 8_000_000_000, 22_000_000, outs, scratch,
-        me, grad, resid, normed, dhidden, in_full, norm, gated, out_full,
+        me, grad, resid, normed, dhidden, in_full, norm, gated, out_full, awaited=awaited,
     )
 
 
@@ -418,19 +431,16 @@
     return lax.ppermute(values, "fsdp", [(index, index ^ bit) for index in range(count)])
 
 
-def place_kernel(cuts, me_ref, own_ref, other_ref, *whole_refs):
+def place_kernel(cuts, me_ref, *refs):
     me = me_ref[0]
-
-    def step(item, carry):
-        away = 2 * (4 * (item % 4) + item // 4)
-        for core, ref in ((0, own_ref), (1, other_ref)):
-            for starts, whole_ref in zip(cuts, whole_refs):
-                for part, low in enumerate(starts):
-                    high = low + whole_ref.shape[3]
-                    whole_ref[me ^ (away + core), part] = ref[item, :, low:high]
-        return carry
-
-    lax.fori_loop(0, PARTS // 2, step, 0, unroll=4)
+    whole_refs = refs[10:]
+    for core in (0, 1):
+        for group, ref in enumerate(refs[5 * core : 5 * core + 5]):
+            for item in range(ref.shape[0]):
+                away = 2 * (4 * (item + 2 * (group == 4)) + min(group, 3)) + core
+                for starts, whole_ref in zip(cuts, whole_refs):
+                    for part, low in enumerate(starts):
+                        whole_ref[me ^ away, part] = ref[item, :, low : low + whole_ref.shape[3]]
 
 
 def phase(earlier, *items):
@@ -458,11 +468,12 @@
     return jnp.concatenate([own, *others], axis=0)
 
 
-def put_together(me, own, other, *cuts):
-    depth = own.shape[1]
+def put_together(me, own, *cuts):
+    depth = own[0].shape[1]
+    other = [swap(piece, 1, PARTS) for piece in own]
     outs = tuple(shape(PARTS, len(starts), depth, width, dtype=LOW) for starts, width in cuts)
     kernel = partial(place_kernel, [starts for starts, width in cuts])
-    wholes = call(kernel, "place", 0, 4 * own.size, outs, [], me, own, other)
+    wholes = call(kernel, "place", 0, 64 * own[0].size, outs, [], me, *own, *other)
     return [whole.reshape(-1, whole.shape[3]) for whole in wholes]
 
 
@@ -480,9 +491,10 @@
         return [(self.local(3, 0, 2).astype(LOW), 4), (self.local(3, 2, 4).astype(LOW), 2)]
 
     def along_xy(self, far_a, far_b):
-        right = jnp.concatenate([self.local(1, 0, 2) + far_a.astype(F32), self.local(1, 2, 4)]).astype(LOW)
-        up = jnp.concatenate([self.local(2, 0, 2), self.local(2, 2, 4) + far_b.astype(F32)]).astype(LOW)
-        return [(right, 2), (up, 4)]
+        none = ((0, 0, 0),) * 2
+        right = self.local(1, 0, 4) + lax.pad(far_a.astype(F32), 0.0, ((0, 2, 0), *none))
+        up = self.local(2, 0, 4) + lax.pad(far_b.astype(F32), 0.0, ((2, 0, 0), *none))
+        return [(right.astype(LOW), 2), (up.astype(LOW), 4)]
 
     def add_xy(self, right, up):
         self.mine = lambda low, high: (
@@ -504,6 +516,21 @@
 
     def end(self, near):
         return self.result(self.far[:1], near)
+
+
+def nothing(values):
+    return values[(slice(0, 1),) * values.ndim].reshape(()) * 0
+
+
+class Total:
+    def __init__(self, values):
+        self.values = values
+
+    def add(self, bit, awaited=None):
+        low = self.values.astype(LOW)
+        if awaited is not None:
+            low = low + nothing(awaited)
+        self.values = low.astype(F32) + swap(low, bit, PARTS).astype(F32)
 
 
 def grow(values, other, me, bit):
@@ -527,21 +554,37 @@
     return values
 
 
-def small_arrays(packed, count, widths, log_decay, skip_gain, step_bias):
+def unpack_kernel(count, fields, packed_ref, *refs):
+    packed = packed_ref[...]
+    layers = len(refs) // 3
+    for item, row, low, width in (
+        (0, 0, 0, fields[0]),
+        *((1, tap, fields[0] + tap * fields[1], fields[1]) for tap in range(CONV + 1)),
+        (2, 0, fields[0] + (CONV + 1) * fields[1], fields[2]),
+    ):
+        whole = refs[item].shape[1]
+        place = iota((1, whole), 1)
+        owner = jnp.floor((place.astype(F32) + 0.5) * (1.0 / width)).astype(jnp.int32)
+        source = low + place - owner * width
+        pick = jnp.where(iota((packed.shape[1], whole), 0) == source, 1.0, 0.0).astype(LOW)
+        picked = jnp.dot(packed, pick, preferred_element_type=F32)
+        for layer in range(layers):
+            mine = iota((packed.shape[0], whole), 0) == owner * layers + layer
+            refs[3 * layer + item][row : row + 1, :] = jnp.sum(jnp.where(mine, picked, 0.0), axis=0, keepdims=True)
+
+
+def head_arrays(log_decay, skip_gain, step_bias):
+    heads = jnp.pad(jnp.stack([log_decay, skip_gain, step_bias], axis=1), ((0, 0), (0, 0), (0, LANES - HEADS)))
+    return heads, jnp.repeat(skip_gain, HEADDIM, axis=1)[:, None]
+
+
+def small_arrays(packed, count, fields, held):
     layers = packed.shape[1]
-    norms, taps, gates = widths
-    held = packed.astype(F32)
-
-    def full(low, rows, width):
-        part = held[:, :, low : low + rows * width].reshape(count, layers, rows, width)
-        return jnp.transpose(part, (1, 2, 0, 3)).reshape(layers, rows, count * width)
-
-    norm = full(0, 1, norms)
-    conv = full(norms, CONV + 1, taps)
-    gate = full(norms + (CONV + 1) * taps, 1, gates)
-    heads = jnp.pad(jnp.stack([log_decay, skip_gain, step_bias], axis=1), ((0, 0), (0, 0), (0, LANES - HEADS)))
-    skip = jnp.repeat(skip_gain, HEADDIM, axis=1)[:, None]
-    return [[item[layer] for item in (norm, conv, gate, heads, skip)] for layer in range(layers)]
+    outs = (shape(1, WIDTH), shape(CONV + 1, CONVCH), shape(1, INNER)) * layers
+    rows = packed.reshape(count * layers, packed.shape[2])
+    rows = jnp.pad(rows, ((0, 0), (0, -rows.shape[1] % LANES)))
+    wide = call(partial(unpack_kernel, count, fields), "unpack", 0, 200_000, outs, [], rows)
+    return [[*wide[3 * layer : 3 * layer + 3], *(item[layer] for item in held)] for layer in range(layers)]
 
 
 def project(resid, gated, out_full):
@@ -575,123 +618,122 @@
         kept.append((resid, saved))
         resid = project(resid, saved[3], out_full[layer])
     mixed, grad = finish(resid, cotangent, segs)
-    in_grads, out_grads, sums, norm_sums = ([None] * layers for item in range(4))
+    in_grads, out_grads, sums = ([None] * layers for item in range(3))
     for layer in reversed(range(layers)):
         resid, (hidden, ssm, normed, gated) = kept[layer]
         gated_grad, out_keep, out_send = backward_out(place, grad, gated, out_full[layer])
         dhidden, sums[layer] = backward_mixer(gated_grad, hidden, ssm, small[layer], segs)
-        grad, in_keep, in_send, norm_sums[layer] = backward_in(
+        grad, in_keep, in_send = backward_in(
             place, grad, resid, normed, dhidden, in_full[layer], small[layer][0]
         )
         out_grads[layer] = scatter(out_keep, out_send)
         in_grads[layer] = scatter(in_keep, in_send)
     sums = sum_small(jnp.stack(sums), count)
-    norm_sums = sum_small(jnp.concatenate(norm_sums), count)
-    return mixed, grad, in_grads, out_grads, sums, norm_sums
-
-
-def run_staged(me, resid, segs, cotangent, in_shards, out_shards, packed, small_of):
+    return mixed, grad, in_grads, out_grads, sums
+
+
+def run_staged(me, resid, segs, cotangent, in_shards, out_shards, packed, small_from):
     place = me.astype(jnp.int32).reshape(1)
-    in0, in1 = (shard[None] for shard in in_shards)
+    depth = in_shards[0].shape[0]
+    size = packed.size
+    columns = -(-size // depth)
+    spare = jnp.pad(packed.reshape(size), (0, columns * depth - size)).reshape(depth, columns)
+    in0 = jnp.concatenate(
+        [in_shards[0][:, :PROJ], spare, jnp.zeros((depth, PADDED - PROJ - columns), LOW)], axis=1
+    )[None]
+    in1 = in_shards[1][None]
+
+    def small_of(full):
+        held = full[:, PROJ : PROJ + columns].reshape(PARTS, depth * columns)[:, :size]
+        return small_from(held.reshape((PARTS,) + packed.shape[1:]))
+
     out0, out1 = (shard[None] for shard in out_shards)
 
-    depth = in0.shape[1]
-    second = jnp.concatenate([out0[:, :depth], out0[:, depth:], in1], axis=2)
-    last = out1
-
-    *got, other = phase([], *along_z(in0), (packed, 1))
-    cur_a = join(in0, got)
-    packed = grow(packed, other, me, 1)
-    packed = grow(packed, swap(packed, 2, PARTS), me, 2)
-
-    right_a, up_a, near, other = phase([cur_a, packed], *along_xy(cur_a), (second, 8), (packed, 4))
-    cur_b = join(second, [near])
-    packed = grow(packed, other, me, 4)
-
-    *far_a, other = phase([right_a, up_a, cur_b, packed], *across(right_a, up_a), (packed, 8))
-    (far_b,) = phase([right_a, up_a], (cur_b, 16))
-    own_a = join(cur_a, [right_a, up_a, *far_a])
-    packed = grow(packed, other, me, 8)
-
-    other_a, near, other = phase([own_a, packed], (own_a, 1), (last, 8), (packed, 16))
-    cur_b = join(cur_b, [far_b])
-    cur_c = join(last, [near])
-    packed = grow(packed, other, me, 16)
-    small = small_of(packed)
-
-    (in0_full,) = put_together(place, own_a, other_a, ((0,), PADDED))
-    right_b, up_b, far_c = phase([in0_full, cur_c], *along_xy(cur_b), (cur_c, 16))
-    kept0 = forward(*after([cur_b, *small[1]], resid), in0_full, small[0], segs)
-    cur_c = join(cur_c, [far_c])
-
-    far_b = phase([right_b, up_b, kept0[3]], *across(right_b, up_b))
-    own_b = join(cur_b, [right_b, up_b, *far_b])
-    other_b, right_c, up_c = phase([own_b, cur_c], (own_b, 1), *along_xy(cur_c))
-
-    ready = [other_b]
-    far_c = phase([other_b, right_c, up_c], *across(right_c, up_c))
-    out0_full, in1_full = put_together(
-        place, own_b, *after(ready, other_b), ((0, WIDTH), WIDTH), ((2 * WIDTH,), PADDED)
+    others = [swap(in0, bit, PARTS) for bit in (8, 16, 24)]
+    cur_a = join(in0, others)
+    rest = jnp.concatenate(
+        [out0[:, :depth], out0[:, depth:], in1, out1[:, :depth], out1[:, depth:]], axis=2
+    ) + nothing(others[0])
+    others = [swap(rest, bit, PARTS) for bit in (8, 16, 24)]
+    right_a, up_a = phase([], *along_xy(cur_a))
+    arrived = sum([nothing(item) for item in others])
+    far_a = phase([], *across(right_a + arrived, up_a + arrived))
+    arrived = nothing(far_a[0]) + nothing(far_a[1])
+    cur_b = join(rest, [item + arrived for item in others])
+    right_b, up_b = phase([], *along_xy(cur_b))
+    (in0_full,) = put_together(place, [cur_a, right_a, up_a, *far_a], ((0,), PADDED))
+    small = small_of(in0_full)
+    arrived = nothing(small[0][0]).astype(LOW)
+    near_right, near_up = right_b[:2] + arrived, up_b[2:] + arrived
+    kept0 = forward(resid, in0_full, small[0], segs, near_right, near_up)
+    arrived = nothing(kept0[3])
+    far_b = [swap(near_right, 4, PARTS) + arrived, swap(near_up, 2, PARTS) + arrived]
+    pieces = [cur_b, right_b, up_b, *far_b]
+    start = 2 * WIDTH + PADDED
+    out0_full, in1_full, out1_full = put_together(
+        place, pieces, ((0, WIDTH), WIDTH), ((2 * WIDTH,), PADDED), ((start, start + WIDTH), WIDTH)
     )
     resid1 = project(resid, kept0[3], out0_full)
-    own_c = join(cur_c, [right_c, up_c, *far_c])
-    ready = [own_c, resid1]
-    (other_c,) = phase(ready, (own_c, 1))
-    kept1 = forward(*after(ready, resid1), in1_full, small[1], segs)
-    (out1_full,) = put_together(place, own_c, *after([kept1[3]], other_c), ((0,), WIDTH))
+    kept1 = forward(resid1, in1_full, small[1], segs)
     mixed, grad = finish(project(resid1, kept1[3], out1_full), cotangent, segs)
 
     hidden, ssm, normed, gated = kept1
     gated_grad, keep, send = backward_out(place, grad, gated, out1_full)
     sum_c = Sums(keep)
-    (core,) = phase([gated_grad], (send, 1))
+    core = swap(send, 1, PARTS)
     dhidden, small1 = backward_mixer(gated_grad, hidden, ssm, small[1], segs)
     sum_c.add_core(core)
 
-    ready = [core, dhidden]
-    far_c = phase(ready, *sum_c.across())
-    grad, keep, send, norm1, gated_grad = backward_both(
-        place, grad, resid1, normed, *after(ready, dhidden), in1_full, small[1][0], kept0[3], out0_full
+    to_far_c = sum_c.across()
+    far_c = phase([], *to_far_c)
+    grad, keep, send, gated_grad = backward_both(
+        place, grad, resid1, normed, dhidden, in1_full, small[1][0], kept0[3], out0_full,
+        *[item[0] for item in to_far_c],
     )
     sum_b = Sums(keep)
 
     hidden, ssm, normed, gated = kept0
-    ready = [*far_c, gated_grad]
-    core, *got = phase(ready, (send, 1), *sum_c.along_xy(*far_c))
-    dhidden, small0 = backward_mixer(*after(ready, gated_grad), hidden, ssm, small[0], segs)
-    sums = jnp.stack([small0, small1])
+    core = swap(send, 1, PARTS)
+    to_xy_c = sum_c.along_xy(*far_c)
+    got = phase([], *to_xy_c)
+    dhidden, small0 = backward_mixer(
+        gated_grad, hidden, ssm, small[0], segs, *[item[0] for item in to_xy_c]
+    )
+    sums = Total(jnp.stack([small0, small1]))
     sum_b.add_core(core)
     sum_c.add_xy(*got)
 
-    ready = [core, *got, dhidden]
-    *far_b, far_c = phase(ready, *sum_b.across(), *sum_c.far_z())
-    grad, keep, send, norm0 = backward_in(
-        place, grad, resid, normed, *after(ready, dhidden), in0_full, small[0][0]
+    to_far_b = sum_b.across()
+    far_b = phase([], *to_far_b)
+    (far_c,) = phase([], *sum_c.far_z())
+    sums.add(1)
+    grad, keep, send = backward_in(
+        place, grad, resid, normed, dhidden, in0_full, small[0][0], *[item[0] for item in to_far_b]
     )
     sum_a = Sums(keep)
-    norms = jnp.stack([norm0, norm1])
-    sums = jnp.concatenate([jnp.concatenate([sums[:, :1, : 2 * LANES], norms, sums[:, :1, 2 * LANES + WIDTH :]], axis=2), sums[:, 1:]], axis=1)
-
-    ready = [*far_b, far_c, grad]
-    core, near_c, right_b, up_b = phase(ready, (send, 1), *sum_c.near_z(far_c), *sum_b.along_xy(*far_b))
+
+    core = swap(send, 1, PARTS)
+    to_xy = sum_b.along_xy(*far_b)
+    right_b, up_b = phase([], *to_xy)
+    (near_c,) = phase([], *sum_c.near_z(far_c))
+    sums.add(8)
     sum_a.add_core(core)
+    far_a = phase([], *sum_a.across())
+    sums.add(16)
+    to_xy = sum_a.along_xy(*far_a)
     sum_b.add_xy(right_b, up_b)
-
-    far_a = phase([core, near_c], *sum_a.across())
-    sums += swap(*after(far_a, sums), 1, PARTS)
-    ready = [*far_a, right_b, up_b, sums]
-    right_a, up_a, far_b, other = phase(ready, *sum_a.along_xy(*far_a), *sum_b.far_z(), (sums, 2))
-    sums += other
-    sums += swap(sums, 4, PARTS)
-    sums += swap(sums, 8, PARTS)
+    right_a, up_a = phase([], *to_xy)
+    (far_b,) = phase([], (sum_b.far_z()[0][0], 16))
     sum_a.add_xy(right_a, up_a)
-
-    *parts, near_b = phase([right_a, up_a, far_b, sums], *sum_a.along_z(), *sum_b.near_z(far_b))
-    sums += swap(*after([near_b], sums), 16, PARTS)
+    to_z = sum_a.along_z()
+    parts = phase([], *to_z)
+    sums.add(2, to_z[0][0])
+    sums.add(4)
+    (near_b,) = phase([], *sum_b.near_z(far_b))
     both = sum_b.end(near_b)
     in_grads = [sum_a.result(*parts), both[:, 2 * WIDTH :]]
     out_grads = [jnp.concatenate([both[:, :WIDTH], both[:, WIDTH : 2 * WIDTH]]), sum_c.end(near_c)]
-    return mixed, grad, in_grads, out_grads, sums, sums[:, 0, 2 * LANES : 2 * LANES + WIDTH]
+    return mixed, grad, in_grads, out_grads, sums.values
 
 
 def body(
@@ -706,11 +748,13 @@
     padded = jnp.pad(in_weight, ((0, 0), (0, 0), (0, PADDED - PROJ)))
     segs = (segments.reshape(rows, 1), segments.reshape(1, rows))
 
+    held = head_arrays(log_decay, skip_gain, step_bias)
+
     def small_of(packed):
-        return small_arrays(packed, count, (in_rows, chans, gates), log_decay, skip_gain, step_bias)
+        return small_arrays(packed, count, (in_rows, chans, gates), held)
 
     run = run_staged if count == PARTS and layers == 2 else partial(run_plain, count)
-    mixed, grad, in_grads, out_grads, sums, norms = run(
+    mixed, grad, in_grads, out_grads, sums = run(
         me, tokens.reshape(rows, WIDTH).astype(F32), segs, cotangent.reshape(rows, WIDTH),
         [padded[layer] for layer in range(layers)], [out_weight[layer] for layer in range(layers)], packed, small_of,
     )
@@ -723,7 +767,7 @@
     return (
         mixed.reshape(tokens.shape),
         grad.reshape(tokens.shape),
-        own(norms, in_rows),
+        jnp.stack([item[:, PROJ] for item in in_grads]),
         jnp.stack([item[:, :PROJ] for item in in_grads]),
         own(total[:, 1 : 1 + CONV], chans),
         own(total[:, 5], chans),

time: 333 us -> 320 us (0.961)
  local copies, waits for them, and re-layouts: 43.6 us -> 22.6 us
  starting transfers between devices: 52.3 us -> 61.7 us
  waiting for transfers between devices: 108 us -> 100 us
  between operations: 1.35 us -> 7.17 us
    unnamed x92 -> x73, local copies, waits for them, and re-layouts: 12.9 us -> 2.48 us
    ppermute x54 -> x51, starting transfers between devices: 52.3 us -> 61.7 us  [swap(): lax.ppermute(values, 'fsdp', [(index, index ^ bit) for index in range(cou...]
    squeeze x7 -> x1, local copies, waits for them, and re-layouts: 9.39 us -> 0.59 us  [small_arrays(): item[layer]]
    ppermute x54 -> x51, waiting for transfers between devices: 108 us -> 100 us  [swap(): lax.ppermute(values, 'fsdp', [(index, index ^ bit) for index in range(cou...]
    convert_element_type x1 -> x9, other arithmetic: 0.11 us -> 7.48 us  [the longest x3 3.78 us: along_xy(): return [(right.astype(LOW), 2), (up.astype(LOW), 4)]]
    slice x10 -> x12, local copies, waits for them, and re-layouts: 1.74 us -> 8.76 us  [the longest x9 7.36 us: nothing(): return values[(slice(0, 1),) * values.ndim].reshape(()) * 0]
    slice x6 -> x1, local copies, waits for them, and re-layouts: 6.94 us -> 0.01 us  [small_arrays(): item[layer]]
    concatenate x5 -> x2, other arithmetic: 4.58 us -> 0.3 us  [join(): return jnp.concatenate([own, *others], axis=0)]
  transfers between devices with their start and end apart: 54 -> 51, of which waited for: 27 -> 25; matrix products, arithmetic and copies ran while one was open for 18% -> 13% of each run, Pallas kernels for 21% -> 17%
where the time goes in v3:
time: 320 us; the launch traced here: 319 us
  waiting for transfers between devices  100 us (31%)
  Pallas kernels  94 us (29%)
  starting transfers between devices  61.7 us (19%)
  other arithmetic  29 us (9%)
  local copies, waits for them, and re-layouts  22.6 us (7%)
  between operations  7.17 us (2%)
  matrix products  4.06 us (1%)
    ppermute x51, waiting for transfers between devices, swap(): lax.ppermute(values, 'fsdp', [(index, index ^ bit) for index in range(cou...  100 us
    pallas_call x10, Pallas kernels, call(): pl.pallas_call(partial(skip_first, kernel, len(awaited)), out_shape=outs,...  94 us
    ppermute x51, starting transfers between devices, swap(): lax.ppermute(values, 'fsdp', [(index, index ^ bit) for index in range(cou...  61.7 us
    slice x9, local copies, waits for them, and re-layouts, nothing(): return values[(slice(0, 1),) * values.ndim].reshape(()) * 0  7.36 us
  transfers between devices with their start and end apart: 51, of which 25 were waited for; matrix products, arithmetic and copies ran while one was open for 13% of the time, Pallas kernels for 17%

profile of v3, /device:TPU:0, one launch (start us, length us, event | category | flops | bytes accessed | tf_op | source)
XLA Modules:
  0.0 318.7 jit_solution(11334952522937835094)
XLA Ops:
  5.1 5.1 %collective-permute-start.3 = (bf16[1,24,3456]{2,1,0:T(8,128)(2,1)S(1)}, bf16[1,24,3456]{2,1,0:T(8,128)(2,1)S(1)}, u32[]{:S(2)}, u32[]{:S(2)}) collective-permute-start(bf16[1,24,3456]{2,1,0:T(8,128)(2,1)S(1)} %bitcast.185), channel_id=1, source_target_pairs={{0,24},{1,25},{2,26},{3,27},{4,28},{5,29},{6,30},{7,31},{8,16},{9,... | collective-permute-start | bytes 497672 | tf_op jit(solution)/shard_map/ppermute | solution.py:431
  12.3 3.0 collective-permute-done.3
  15.3 8.9 %collective-permute-done.2 = bf16[1,24,3456]{2,1,0:T(8,128)(2,1)S(1)} collective-permute-done((bf16[1,24,3456]{2,1,0:T(8,128)(2,1)S(1)}, bf16[1,24,3456]{2,1,0:T(8,128)(2,1)S(1)}, u32[]{:S(2)}, u32[]{:S(2)}) %collective-permute-start.2) | collective-permute-done | bytes 165920 | tf_op jit(solution)/shard_map/ppermute | solution.py:431
  24.3 1.6 collective-permute-start.4
  27.2 3.0 collective-permute-start.1
  30.2 1.3 collective-permute-start.6
  31.5 1.5 collective-permute-start.7
  33.1 11.7 %collective-permute-done.5 = bf16[1,24,6528]{2,1,0:T(8,128)(2,1)S(1)} collective-permute-done((bf16[1,24,6528]{2,1,0:T(8,128)(2,1)S(1)}, bf16[1,24,6528]{2,1,0:T(8,128)(2,1)S(1)}, u32[]{:S(2)}, u32[]{:S(2)}) %collective-permute-start.5) | collective-permute-done | bytes 313376 | tf_op jit(solution)/shard_map/ppermute | solution.py:431
  45.3 4.3 %collective-permute-done.1 = bf16[1,24,6528]{2,1,0:T(8,128)(2,1)S(1)} collective-permute-done((bf16[1,24,6528]{2,1,0:T(8,128)(2,1)S(1)}, bf16[1,24,6528]{2,1,0:T(8,128)(2,1)S(1)}, u32[]{:S(2)}, u32[]{:S(2)}) %collective-permute-start.1) | collective-permute-done | bytes 313376 | tf_op jit(solution)/shard_map/ppermute | solution.py:431
  54.7 1.6 collective-permute-start.8
  56.8 5.1 %collective-permute-done.8.refs_4_ = bf16[2,24,3456]{2,1,0:T(8,128)(2,1)S(1)} collective-permute-done((bf16[2,24,3456]{2,1,0:T(8,128)(2,1)S(1)}, bf16[2,24,3456]{2,1,0:T(8,128)(2,1)S(1)}, u32[]{:S(2)}, u32[]{:S(2)}) %collective-permute-start.8) | collective-permute-done | bytes 331808 | tf_op jit(solution)/shard_map/ppermute | solution.py:431
  63.5 1.2 slice.451
  71.3 1.7 bitcast_convert_fusion.refs_2_.refs_4_
  73.9 5.2 %place.2 = bf16[32,1,24,3456]{3,2,1,0:T(8,128)(2,1)} custom-call(s32[1]{0:T(128)} %bitcast.6.refs_0_.refs_2_, bf16[4,24,3456]{2,1,0:T(8,128)(2,1)} %copy-done.5, bf16[4,24,3456]{2,1,0:T(8,128)(2,1)} %collective-permute-done.4.refs_2_, bf16[4,24,3456]{2,1,0:T(8,128)(2,1)} %collective-permute-done.7.refs_3_, bf16[2,24,3456]{2,1,0:T(8,128)(2,1)} %copy-done.23, ...), custom_call_target="tpu_custom_call" | custom-call | bytes 21233664 | tf_op jit(solution)/shard_map/place/pallas_call | solution.py:362
  81.0 4.3 %unpack.1 = (f32[1,768]{1,0:T(1,128)}, f32[5,1792]{1,0:T(8,128)}, f32[1,1536]{1,0:T(1,128)}, f32[1,768]{1,0:T(1,128)}, f32[5,1792]{1,0:T(8,128)}, /*index=5*/f32[1,1536]{1,0:T(1,128)}) custom-call(bf16[64,384]{1,0:T(8,128)(2,1)} %pad.54.refs_0_), custom_call_target="tpu_custom_call" | custom-call | bytes 200000 | tf_op jit(solution)/shard_map/unpack/pallas_call | solution.py:362
  85.3 1.2 slice.353
  87.1 3.4 %collective-permute-done.10.refs_2_ = bf16[4,24,6528]{2,1,0:T(8,128)(2,1)S(1)} collective-permute-done((bf16[4,24,6528]{2,1,0:T(8,128)(2,1)S(1)}, bf16[4,24,6528]{2,1,0:T(8,128)(2,1)S(1)}, u32[]{:S(2)}, u32[]{:S(2)}) %collective-permute-start.10) | collective-permute-done | bytes 1253408 | tf_op jit(solution)/shard_map/ppermute | solution.py:431
  91.3 12.5 %collective-permute-done.16.refs_3_ = bf16[4,24,6528]{2,1,0:T(8,128)(2,1)} collective-permute-done((bf16[4,24,6528]{2,1,0:T(8,128)(2,1)S(1)}, bf16[4,24,6528]{2,1,0:T(8,128)(2,1)}, u32[]{:S(2)}, u32[]{:S(2)}) %collective-permute-start.16) | collective-permute-done | bytes 1253408 | tf_op jit(solution)/shard_map/ppermute | solution.py:431
  105.0 1.6 collective-permute-start.18
  106.6 11.4 %mix_forward.2 = (f32[128,3456]{1,0:T(8,128)}, f32[128,1536]{1,0:T(8,128)}, bf16[128,768]{1,0:T(8,128)(2,1)}, bf16[128,1536]{1,0:T(8,128)(2,1)}) custom-call(bf16[2,24,6528]{2,1,0:T(8,128)(2,1)} %copy-done.18, bf16[2,24,6528]{2,1,0:T(8,128)(2,1)} %copy-done.17, f32[128,768]{1,0:T(8,128)} %bitcast_convert_fusion.refs_2_.refs_4_, bf16[768,3456]{1,0:T(8,128)(2,1)} %bitcast.178, ...), custom_call_target="tpu_custom_call" | custom-call | flops 10000000000 | bytes 10000000 | tf_op jit(solution)/shard_map/mix_forward/pallas_call | solution.py:362
  118.0 1.2 slice.358
  124.0 1.8 collective-permute-done.21.refs_8_
  126.8 8.4 %place.3 = (bf16[32,2,24,768]{3,2,1,0:T(8,128)(2,1)}, bf16[32,1,24,3456]{3,2,1,0:T(8,128)(2,1)}, bf16[32,2,24,768]{3,2,1,0:T(8,128)(2,1)}) custom-call(s32[1]{0:T(128)} %bitcast.6.refs_0_.refs_2_, bf16[4,24,6528]{2,1,0:T(8,128)(2,1)} %copy-done, bf16[4,24,6528]{2,1,0:T(8,128)(2,1)} %copy-done.2, bf16[4,24,6528]{2,1,0:T(8,128)(2,1)} %collective-permute-done.16.refs_3_, ...), custom_call_target="tpu_custom_call" | custom-call | bytes 40108032 | tf_op jit(solution)/shard_map/place/pallas_call | solution.py:362
  135.2 2.9 convolution_add_fusion.1.refs_0_.refs_4_
  138.1 11.3 %mix_forward.3 = (f32[128,3456]{1,0:T(8,128)}, f32[128,1536]{1,0:T(8,128)}, bf16[128,768]{1,0:T(8,128)(2,1)}, bf16[128,1536]{1,0:T(8,128)(2,1)}) custom-call(f32[128,768]{1,0:T(8,128)} %convolution_add_fusion.1.refs_0_.refs_4_, bf16[768,3456]{1,0:T(8,128)(2,1)} %bitcast.200, f32[1,768]{1,0:T(1,128)} %get-tuple-element.75.refs_2_.refs_8_, ...), custom_call_target="tpu_custom_call" | custom-call | flops 10000000000 | bytes 10000000 | tf_op jit(solution)/shard_map/mix_forward/pallas_call | solution.py:362
  149.3 5.4 %out_backward.1 = (f32[128,1536]{1,0:T(8,128)}, bf16[4,4,48,768]{3,2,1,0:T(8,128)(2,1)}, bf16[4,4,48,768]{3,2,1,0:T(8,128)(2,1)}) custom-call(s32[1]{0:T(128)} %bitcast.6.refs_0_.refs_2_, f32[128,768]{1,0:T(8,128)} %convert_multiply_fusion.refs_1_.refs_3_, bf16[128,1536]{1,0:T(8,128)(2,1)} %get-tuple-element.78.refs_2_, bf16[1536,768]{1,0:T(8,128)(2,1)} %bitcast.180), custom_call_target="tpu_custom_call" | custom-call | flops 2000000000 | bytes 8000000 | tf_op jit(solution)/shard_map/out_backward/pallas_call | solution.py:362
  154.9 11.8 %mix_backward.2 = (bf16[128,3456]{1,0:T(8,128)(2,1)}, f32[8,1792]{1,0:T(8,128)}) custom-call(f32[128,1536]{1,0:T(8,128)} %get-tuple-element.83.refs_0_, f32[128,3456]{1,0:T(8,128)} %get-tuple-element.84.refs_1_, f32[128,1536]{1,0:T(8,128)} %get-tuple-element.85.refs_2_, f32[5,1792]{1,0:T(8,128)} %get-tuple-element.76.refs_3_, ...), custom_call_target="tpu_custom_call" | custom-call | flops 12000000000 | bytes 5000000 | tf_op jit(solution)/shard_map/mix_backward/pallas_call | solution.py:362
  166.7 2.1 fusion.37
  168.8 14.0 %both_backward.1 = (f32[128,768]{1,0:T(8,128)}, bf16[4,4,24,4992]{3,2,1,0:T(8,128)(2,1)}, bf16[4,4,24,4992]{3,2,1,0:T(8,128)(2,1)}, f32[128,1536]{1,0:T(8,128)}) custom-call(bf16[2,48,768]{2,1,0:T(8,128)(2,1)} %get-tuple-element.91.refs_0_, bf16[2,48,768]{2,1,0:T(8,128)(2,1)} %get-tuple-element.92.refs_1_, s32[1]{0:T(128)} %bitcast.6.refs_0_.refs_2_, ...), custom_call_target="tpu_custom_call" | custom-call | flops 8000000000 | bytes 22000000 | tf_op jit(solution)/shard_map/both_backward/pallas_call | solution.py:362
  184.5 1.2 fusion.5
  185.7 3.7 %collective-permute-done.26 = bf16[2,48,768]{2,1,0:T(8,128)(2,1)S(1)} collective-permute-done((bf16[2,48,768]{2,1,0:T(8,128)(2,1)}, bf16[2,48,768]{2,1,0:T(8,128)(2,1)S(1)}, u32[]{:S(2)}, u32[]{:S(2)}) %collective-permute-start.26) | collective-permute-done | bytes 147488 | tf_op jit(solution)/shard_map/ppermute | solution.py:431
  189.6 1.2 fusion.8
  191.7 1.5 collective-permute-start.48
  193.2 1.4 fusion.11
  195.2 1.3 collective-permute-start.37
  196.5 11.9 %mix_backward.3 = (bf16[128,3456]{1,0:T(8,128)(2,1)}, f32[8,1792]{1,0:T(8,128)}) custom-call(bf16[4,48,768]{2,1,0:T(8,128)(2,1)} %copy-done.26, bf16[4,48,768]{2,1,0:T(8,128)(2,1)} %copy-done.25, f32[128,1536]{1,0:T(8,128)} %get-tuple-element.93.refs_2_, f32[128,3456]{1,0:T(8,128)} %get-tuple-element.94.refs_3_, f32[128,1536]{1,0:T(8,128)} %get-tuple-element.95.refs_4_, ...), custom_call_target="tpu_custom_call" | custom-call | flops 12000000000 | bytes 5000000 | tf_op jit(solution)/shard_map/mix_backward/pallas_call | solution.py:362
  209.7 2.1 fusion
  211.8 1.3 collective-permute-start.38
  213.1 1.4 collective-permute-start.39
  214.6 1.2 fusion.33
  215.7 7.7 %collective-permute-start.49 = (bf16[2,48,768]{2,1,0:T(8,128)(2,1)S(1)}, bf16[2,48,768]{2,1,0:T(8,128)(2,1)S(1)}, u32[]{:S(2)}, u32[]{:S(2)}) collective-permute-start(bf16[2,48,768]{2,1,0:T(8,128)(2,1)S(1)} %fusion.33), channel_id=1, source_target_pairs={{0,16},{1,17},{2,18},{3,19},{4,20},{5,21},{6,22},{7,23},{8,24},{9,... | collective-permute-start | bytes 442376 | tf_op jit(solution)/shard_map/ppermute | solution.py:431
  223.5 7.5 %collective-permute-done.49 = bf16[2,48,768]{2,1,0:T(8,128)(2,1)S(1)} collective-permute-done((bf16[2,48,768]{2,1,0:T(8,128)(2,1)S(1)}, bf16[2,48,768]{2,1,0:T(8,128)(2,1)S(1)}, u32[]{:S(2)}, u32[]{:S(2)}) %collective-permute-start.49) | collective-permute-done | bytes 147488 | tf_op jit(solution)/shard_map/ppermute | solution.py:431
  233.8 1.6 fusion.7
  235.5 7.7 %collective-permute-start.40 = (bf16[2,24,4992]{2,1,0:T(8,128)(2,1)S(1)}, bf16[2,24,4992]{2,1,0:T(8,128)(2,1)S(1)}, u32[]{:S(2)}, u32[]{:S(2)}) collective-permute-start(bf16[2,24,4992]{2,1,0:T(8,128)(2,1)S(1)} %fusion.7), channel_id=1, source_target_pairs={{0,16},{1,17},{2,18},{3,19},{4,20},{5,21},{6,22},{7,23},{8,24},{9,... | collective-permute-start | bytes 1437704 | tf_op jit(solution)/shard_map/ppermute | solution.py:431
  243.1 10.5 %in_backward.1 = (f32[128,768]{1,0:T(8,128)}, bf16[4,4,24,3456]{3,2,1,0:T(8,128)(2,1)}, bf16[4,4,24,3456]{3,2,1,0:T(8,128)(2,1)}) custom-call(bf16[2,24,4992]{2,1,0:T(8,128)(2,1)} %copy-done.20, bf16[2,24,4992]{2,1,0:T(8,128)(2,1)} %copy-done.19, s32[1]{0:T(128)} %bitcast.6.refs_0_.refs_2_, f32[128,768]{1,0:T(8,128)} %get-tuple-element.89.refs_3_, ...), custom_call_target="tpu_custom_call" | custom-call | flops 6000000000 | bytes 14000000 | tf_op jit(solution)/shard_map/in_backward/pallas_call | solution.py:362
  253.7 7.6 %collective-permute-done.40 = bf16[2,24,4992]{2,1,0:T(8,128)(2,1)S(1)} collective-permute-done((bf16[2,24,4992]{2,1,0:T(8,128)(2,1)S(1)}, bf16[2,24,4992]{2,1,0:T(8,128)(2,1)S(1)}, u32[]{:S(2)}, u32[]{:S(2)}) %collective-permute-start.40) | collective-permute-done | bytes 479264 | tf_op jit(solution)/shard_map/ppermute | solution.py:431
  261.3 1.3 fusion.14
  262.8 2.9 collective-permute-start.44
  266.8 2.8 collective-permute-done.41
  269.6 1.3 fusion.18
  271.1 1.4 collective-permute-start.29
  272.6 1.3 collective-permute-start.30
  273.9 4.4 %collective-permute-done.29 = bf16[2,24,3456]{2,1,0:T(8,128)(2,1)S(1)} collective-permute-done((bf16[2,24,3456]{2,1,0:T(8,128)(2,1)S(1)}, bf16[2,24,3456]{2,1,0:T(8,128)(2,1)S(1)}, u32[]{:S(2)}, u32[]{:S(2)}) %collective-permute-start.29) | collective-permute-done | bytes 331808 | tf_op jit(solution)/shard_map/ppermute | solution.py:431
  278.3 2.3 collective-permute-done.30
  281.1 1.3 collective-permute-start.31
  283.4 10.5 %collective-permute-done.31 = bf16[4,24,3456]{2,1,0:T(8,128)(2,1)S(1)} collective-permute-done((bf16[4,24,3456]{2,1,0:T(8,128)(2,1)S(1)}, bf16[4,24,3456]{2,1,0:T(8,128)(2,1)S(1)}, u32[]{:S(2)}, u32[]{:S(2)}) %collective-permute-start.31) | collective-permute-done | bytes 663584 | tf_op jit(solution)/shard_map/ppermute | solution.py:431
  293.9 1.2 fusion.22
  295.1 1.2 slice.497
  297.0 1.3 collective-permute-start.45
  299.1 2.2 collective-permute-done.45
  302.2 5.7 %collective-permute-start.34 = (bf16[1,24,3456]{2,1,0:T(8,128)(2,1)}, bf16[1,24,3456]{2,1,0:T(8,128)(2,1)S(1)}, u32[]{:S(2)}, u32[]{:S(2)}) collective-permute-start(bf16[1,24,3456]{2,1,0:T(8,128)(2,1)} %get-tuple-element.105), channel_id=1, source_target_pairs={{0,16},{1,17},{2,18},{3,19},{4,20},{5,21},{6,22},{7,23},{8,24},{9,... | collective-permute-start | bytes 497672 | tf_op jit(solution)/shard_map/ppermute | solution.py:431
  311.3 1.4 constant_dynamic-slice_fusion.2
  312.6 3.2 collective-permute-done.34
  315.8 1.2 fusion.31
  (209 shorter events, 45.5 us)
Async XLA Ops:
  5.1 10.3 %collective-permute-start.3 = (bf16[1,24,3456]{2,1,0:T(8,128)(2,1)S(1)}, bf16[1,24,3456]{2,1,0:T(8,128)(2,1)S(1)}, u32[]{:S(2)}, u32[]{:S(2)}) collective-permute-start(bf16[1,24,3456]{2,1,0:T(8,128)(2,1)S(1)} %bitcast.185), channel_id=1, source_target_pairs={{0,24},{1,25},{2,26},{3,27},{4,28},{5,29},{6,30},{7,31},{8,16},{9,... | collective-permute-start | bytes 497672 | tf_op jit(solution)/shard_map/ppermute | solution.py:431
  10.2 14.1 %collective-permute-start.2 = (bf16[1,24,3456]{2,1,0:T(8,128)(2,1)S(1)}, bf16[1,24,3456]{2,1,0:T(8,128)(2,1)S(1)}, u32[]{:S(2)}, u32[]{:S(2)}) collective-permute-start(bf16[1,24,3456]{2,1,0:T(8,128)(2,1)S(1)} %bitcast.186), channel_id=1, source_target_pairs={{0,16},{1,17},{2,18},{3,19},{4,20},{5,21},{6,22},{7,23},{8,24},{9,... | collective-permute-start | bytes 497672 | tf_op jit(solution)/shard_map/ppermute | solution.py:431
  10.2 14.1 %collective-permute-start = (bf16[1,24,3456]{2,1,0:T(8,128)(2,1)S(1)}, bf16[1,24,3456]{2,1,0:T(8,128)(2,1)S(1)}, u32[]{:S(2)}, u32[]{:S(2)}) collective-permute-start(bf16[1,24,3456]{2,1,0:T(8,128)(2,1)S(1)} %bitcast.187), channel_id=1, source_target_pairs={{0,8},{1,9},{2,10},{3,11},{4,12},{5,13},{6,14},{7,15},{8,0},{9,1},... | collective-permute-start | bytes 497672 | tf_op jit(solution)/shard_map/ppermute | solution.py:431
  24.3 42.6 %copy-start.5 = (bf16[4,24,3456]{2,1,0:T(8,128)(2,1)}, bf16[4,24,3456]{2,1,0:T(8,128)(2,1)S(1)}, u32[]{:S(2)}) copy-start(bf16[4,24,3456]{2,1,0:T(8,128)(2,1)S(1)} %pad_maximum_fusion.1.refs_1_) | copy-start | bytes 1990660
  24.3 28.3 %collective-permute-start.4 = (bf16[4,24,3456]{2,1,0:T(8,128)(2,1)S(1)}, bf16[4,24,3456]{2,1,0:T(8,128)(2,1)}, u32[]{:S(2)}, u32[]{:S(2)}) collective-permute-start(bf16[4,24,3456]{2,1,0:T(8,128)(2,1)S(1)} %pad_maximum_fusion.1.refs_1_), channel_id=1, source_target_pairs={{0,2},{1,3},{2,0},{3,1},{4,6},{5,7},{6,4},{7,5},{8,10},{9,11},{10,... | collective-permute-start | bytes 1990664 | tf_op jit(solution)/shard_map/ppermute | solution.py:431
  27.1 17.7 %collective-permute-start.5 = (bf16[1,24,6528]{2,1,0:T(8,128)(2,1)S(1)}, bf16[1,24,6528]{2,1,0:T(8,128)(2,1)S(1)}, u32[]{:S(2)}, u32[]{:S(2)}) collective-permute-start(bf16[1,24,6528]{2,1,0:T(8,128)(2,1)S(1)} %broadcast_add_fusion.5), channel_id=1, source_target_pairs={{0,16},{1,17},{2,18},{3,19},{4,20},{5,21},{6,22},{7,23},{8,24},{9,... | collective-permute-start | bytes 940040 | tf_op jit(solution)/shard_map/ppermute | solution.py:431
  27.2 22.4 %collective-permute-start.1 = (bf16[1,24,6528]{2,1,0:T(8,128)(2,1)S(1)}, bf16[1,24,6528]{2,1,0:T(8,128)(2,1)S(1)}, u32[]{:S(2)}, u32[]{:S(2)}) collective-permute-start(bf16[1,24,6528]{2,1,0:T(8,128)(2,1)S(1)} %broadcast_add_fusion.5), channel_id=1, source_target_pairs={{0,8},{1,9},{2,10},{3,11},{4,12},{5,13},{6,14},{7,15},{8,0},{9,1},... | collective-permute-start | bytes 940040 | tf_op jit(solution)/shard_map/ppermute | solution.py:431
  30.2 21.2 %collective-permute-start.6 = (bf16[1,24,6528]{2,1,0:T(8,128)(2,1)S(1)}, bf16[1,24,6528]{2,1,0:T(8,128)(2,1)S(1)}, u32[]{:S(2)}, u32[]{:S(2)}) collective-permute-start(bf16[1,24,6528]{2,1,0:T(8,128)(2,1)S(1)} %broadcast_add_fusion.5), channel_id=1, source_target_pairs={{0,24},{1,25},{2,26},{3,27},{4,28},{5,29},{6,30},{7,31},{8,16},{9,... | collective-permute-start | bytes 940040 | tf_op jit(solution)/shard_map/ppermute | solution.py:431
  31.5 22.1 %collective-permute-start.7 = (bf16[4,24,3456]{2,1,0:T(8,128)(2,1)S(1)}, bf16[4,24,3456]{2,1,0:T(8,128)(2,1)}, u32[]{:S(2)}, u32[]{:S(2)}) collective-permute-start(bf16[4,24,3456]{2,1,0:T(8,128)(2,1)S(1)} %pad_maximum_fusion.1.refs_1_), channel_id=1, source_target_pairs={{0,4},{1,5},{2,6},{3,7},{4,0},{5,1},{6,2},{7,3},{8,12},{9,13},{10,... | collective-permute-start | bytes 1990664 | tf_op jit(solution)/shard_map/ppermute | solution.py:431
  54.7 7.2 %collective-permute-start.8 = (bf16[2,24,3456]{2,1,0:T(8,128)(2,1)S(1)}, bf16[2,24,3456]{2,1,0:T(8,128)(2,1)S(1)}, u32[]{:S(2)}, u32[]{:S(2)}) collective-permute-start(bf16[2,24,3456]{2,1,0:T(8,128)(2,1)S(1)} %slice_add_fusion.3), channel_id=1, source_target_pairs={{0,4},{1,5},{2,6},{3,7},{4,0},{5,1},{6,2},{7,3},{8,12},{9,13},{10,... | collective-permute-start | bytes 995336 | tf_op jit(solution)/shard_map/ppermute | solution.py:431
  56.2 7.2 %collective-permute-start.9 = (bf16[2,24,3456]{2,1,0:T(8,128)(2,1)S(1)}, bf16[2,24,3456]{2,1,0:T(8,128)(2,1)}, u32[]{:S(2)}, u32[]{:S(2)}) collective-permute-start(bf16[2,24,3456]{2,1,0:T(8,128)(2,1)S(1)} %slice_add_fusion.2), channel_id=1, source_target_pairs={{0,2},{1,3},{2,0},{3,1},{4,6},{5,7},{6,4},{7,5},{8,10},{9,11},{10,... | collective-permute-start | bytes 995336 | tf_op jit(solution)/shard_map/ppermute | solution.py:431
  66.3 24.1 %collective-permute-start.10 = (bf16[4,24,6528]{2,1,0:T(8,128)(2,1)S(1)}, bf16[4,24,6528]{2,1,0:T(8,128)(2,1)S(1)}, u32[]{:S(2)}, u32[]{:S(2)}) collective-permute-start(bf16[4,24,6528]{2,1,0:T(8,128)(2,1)S(1)} %pad_maximum_fusion.refs_1_), channel_id=1, source_target_pairs={{0,2},{1,3},{2,0},{3,1},{4,6},{5,7},{6,4},{7,5},{8,10},{9,11},{10,... | collective-permute-start | bytes 3760136 | tf_op jit(solution)/shard_map/ppermute | solution.py:431
  66.9 2.1 collective-permute-start.11
  67.0 6.0 %collective-permute-start.12 = (bf16[4,24,3456]{2,1,0:T(8,128)(2,1)}, bf16[4,24,3456]{2,1,0:T(8,128)(2,1)}, u32[]{:S(2)}, u32[]{:S(2)}) collective-permute-start(bf16[4,24,3456]{2,1,0:T(8,128)(2,1)} %collective-permute-done.4.refs_2_), channel_id=1, source_target_pairs={{0,1},{1,0},{2,3},{3,2},{4,5},{5,4},{6,7},{7,6},{8,9},{9,8},{10,11... | collective-permute-start | bytes 1990664 | tf_op jit(solution)/shard_map/ppermute | solution.py:431
  67.5 6.3 %collective-permute-start.13 = (bf16[4,24,3456]{2,1,0:T(8,128)(2,1)}, bf16[4,24,3456]{2,1,0:T(8,128)(2,1)}, u32[]{:S(2)}, u32[]{:S(2)}) collective-permute-start(bf16[4,24,3456]{2,1,0:T(8,128)(2,1)} %collective-permute-done.7.refs_3_), channel_id=1, source_target_pairs={{0,1},{1,0},{2,3},{3,2},{4,5},{5,4},{6,7},{7,6},{8,9},{9,8},{10,11... | collective-permute-start | bytes 1990664 | tf_op jit(solution)/shard_map/ppermute | solution.py:431
  68.2 5.2 %collective-permute-start.14 = (bf16[2,24,3456]{2,1,0:T(8,128)(2,1)S(1)}, bf16[2,24,3456]{2,1,0:T(8,128)(2,1)}, u32[]{:S(2)}, u32[]{:S(2)}) collective-permute-start(bf16[2,24,3456]{2,1,0:T(8,128)(2,1)S(1)} %collective-permute-done.8.refs_4_), channel_id=1, source_target_pairs={{0,1},{1,0},{2,3},{3,2},{4,5},{5,4},{6,7},{7,6},{8,9},{9,8},{10,11... | collective-permute-start | bytes 995336 | tf_op jit(solution)/shard_map/ppermute | solution.py:431
  69.0 4.8 %collective-permute-start.15 = (bf16[2,24,3456]{2,1,0:T(8,128)(2,1)}, bf16[2,24,3456]{2,1,0:T(8,128)(2,1)}, u32[]{:S(2)}, u32[]{:S(2)}) collective-permute-start(bf16[2,24,3456]{2,1,0:T(8,128)(2,1)} %collective-permute-done.9.refs_5_), channel_id=1, source_target_pairs={{0,1},{1,0},{2,3},{3,2},{4,5},{5,4},{6,7},{7,6},{8,9},{9,8},{10,11... | collective-permute-start | bytes 995336 | tf_op jit(solution)/shard_map/ppermute | solution.py:431
  73.0 50.7 %collective-permute-start.19 = (bf16[4,24,6528]{2,1,0:T(8,128)(2,1)S(1)}, bf16[4,24,6528]{2,1,0:T(8,128)(2,1)}, u32[]{:S(2)}, u32[]{:S(2)}) collective-permute-start(bf16[4,24,6528]{2,1,0:T(8,128)(2,1)S(1)} %pad_maximum_fusion.refs_1_), channel_id=1, source_target_pairs={{0,1},{1,0},{2,3},{3,2},{4,5},{5,4},{6,7},{7,6},{8,9},{9,8},{10,11... | collective-permute-start | bytes 3760136 | tf_op jit(solution)/shard_map/ppermute | solution.py:431
  73.3 30.5 %collective-permute-start.16 = (bf16[4,24,6528]{2,1,0:T(8,128)(2,1)S(1)}, bf16[4,24,6528]{2,1,0:T(8,128)(2,1)}, u32[]{:S(2)}, u32[]{:S(2)}) collective-permute-start(bf16[4,24,6528]{2,1,0:T(8,128)(2,1)S(1)} %pad_maximum_fusion.refs_1_), channel_id=1, source_target_pairs={{0,4},{1,5},{2,6},{3,7},{4,0},{5,1},{6,2},{7,3},{8,12},{9,13},{10,... | collective-permute-start | bytes 3760136 | tf_op jit(solution)/shard_map/ppermute | solution.py:431
  90.4 29.4 %copy-start.2 = (bf16[4,24,6528]{2,1,0:T(8,128)(2,1)}, bf16[4,24,6528]{2,1,0:T(8,128)(2,1)S(1)}, u32[]{:S(2)}) copy-start(bf16[4,24,6528]{2,1,0:T(8,128)(2,1)S(1)} %collective-permute-done.10.refs_2_) | copy-start | bytes 3760132
  90.5 16.0 %copy-start.18 = (bf16[2,24,6528]{2,1,0:T(8,128)(2,1)}, bf16[2,24,6528]{2,1,0:T(8,128)(2,1)S(1)}, u32[]{:S(2)}) copy-start(bf16[2,24,6528]{2,1,0:T(8,128)(2,1)S(1)} %slice_add_fusion.1.refs_0_) | copy-start | bytes 1880068
  90.5 29.9 %collective-permute-start.17 = (bf16[2,24,6528]{2,1,0:T(8,128)(2,1)S(1)}, bf16[2,24,6528]{2,1,0:T(8,128)(2,1)S(1)}, u32[]{:S(2)}, u32[]{:S(2)}) collective-permute-start(bf16[2,24,6528]{2,1,0:T(8,128)(2,1)S(1)} %slice_add_fusion.1.refs_0_), channel_id=1, source_target_pairs={{0,4},{1,5},{2,6},{3,7},{4,0},{5,1},{6,2},{7,3},{8,12},{9,13},{10,... | collective-permute-start | bytes 1880072 | tf_op jit(solution)/shard_map/ppermute | solution.py:431
  105.0 15.7 %collective-permute-start.18 = (bf16[2,24,6528]{2,1,0:T(8,128)(2,1)S(1)}, bf16[2,24,6528]{2,1,0:T(8,128)(2,1)S(1)}, u32[]{:S(2)}, u32[]{:S(2)}) collective-permute-start(bf16[2,24,6528]{2,1,0:T(8,128)(2,1)S(1)} %slice_add_fusion.refs_1_), channel_id=1, source_target_pairs={{0,2},{1,3},{2,0},{3,1},{4,6},{5,7},{6,4},{7,5},{8,10},{9,11},{10,... | collective-permute-start | bytes 1880072 | tf_op jit(solution)/shard_map/ppermute | solution.py:431
  119.9 4.1 %collective-permute-start.20 = (bf16[4,24,6528]{2,1,0:T(8,128)(2,1)S(1)}, bf16[4,24,6528]{2,1,0:T(8,128)(2,1)}, u32[]{:S(2)}, u32[]{:S(2)}) collective-permute-start(bf16[4,24,6528]{2,1,0:T(8,128)(2,1)S(1)} %collective-permute-done.10.refs_2_), channel_id=1, source_target_pairs={{0,1},{1,0},{2,3},{3,2},{4,5},{5,4},{6,7},{7,6},{8,9},{9,8},{10,11... | collective-permute-start | bytes 3760136 | tf_op jit(solution)/shard_map/ppermute | solution.py:431
  119.9 5.9 %collective-permute-start.21 = (bf16[4,24,6528]{2,1,0:T(8,128)(2,1)}, bf16[4,24,6528]{2,1,0:T(8,128)(2,1)}, u32[]{:S(2)}, u32[]{:S(2)}) collective-permute-start(bf16[4,24,6528]{2,1,0:T(8,128)(2,1)} %collective-permute-done.16.refs_3_), channel_id=1, source_target_pairs={{0,1},{1,0},{2,3},{3,2},{4,5},{5,4},{6,7},{7,6},{8,9},{9,8},{10,11... | collective-permute-start | bytes 3760136 | tf_op jit(solution)/shard_map/ppermute | solution.py:431
  120.5 5.3 %collective-permute-start.22 = (bf16[2,24,6528]{2,1,0:T(8,128)(2,1)S(1)}, bf16[2,24,6528]{2,1,0:T(8,128)(2,1)}, u32[]{:S(2)}, u32[]{:S(2)}) collective-permute-start(bf16[2,24,6528]{2,1,0:T(8,128)(2,1)S(1)} %broadcast_add_fusion.1.refs_4_), channel_id=1, source_target_pairs={{0,1},{1,0},{2,3},{3,2},{4,5},{5,4},{6,7},{7,6},{8,9},{9,8},{10,11... | collective-permute-start | bytes 1880072 | tf_op jit(solution)/shard_map/ppermute | solution.py:431
  121.6 5.2 %collective-permute-start.23 = (bf16[2,24,6528]{2,1,0:T(8,128)(2,1)}, bf16[2,24,6528]{2,1,0:T(8,128)(2,1)}, u32[]{:S(2)}, u32[]{:S(2)}) collective-permute-start(bf16[2,24,6528]{2,1,0:T(8,128)(2,1)} %broadcast_add_fusion.refs_5_), channel_id=1, source_target_pairs={{0,1},{1,0},{2,3},{3,2},{4,5},{5,4},{6,7},{7,6},{8,9},{9,8},{10,11... | collective-permute-start | bytes 1880072 | tf_op jit(solution)/shard_map/ppermute | solution.py:431
  154.8 11.9 %collective-permute-start.24 = (bf16[4,4,48,768]{3,2,1,0:T(8,128)(2,1)}, bf16[4,4,48,768]{3,2,1,0:T(8,128)(2,1)S(1)}, u32[]{:S(2)}, u32[]{:S(2)}) collective-permute-start(bf16[4,4,48,768]{3,2,1,0:T(8,128)(2,1)} %get-tuple-element.81), channel_id=1, source_target_pairs={{0,1},{1,0},{2,3},{3,2},{4,5},{5,4},{6,7},{7,6},{8,9},{9,8},{10,11... | collective-permute-start | bytes 3538952 | tf_op jit(solution)/shard_map/ppermute | solution.py:431
  166.7 16.1 %copy-start.11 = (bf16[4,4,48,768]{3,2,1,0:T(8,128)(2,1)}, bf16[4,4,48,768]{3,2,1,0:T(8,128)(2,1)S(1)}, u32[]{:S(2)}) copy-start(bf16[4,4,48,768]{3,2,1,0:T(8,128)(2,1)S(1)} %collective-permute-done.24) | copy-start | bytes 3538948
  168.8 15.7 %copy-start.7 = (bf16[32,2,24,768]{3,2,1,0:T(8,128)(2,1)S(1)}, bf16[32,2,24,768]{3,2,1,0:T(8,128)(2,1)}, u32[]{:S(2)}) copy-start(bf16[32,2,24,768]{3,2,1,0:T(8,128)(2,1)} %get-tuple-element.79) | copy-start | bytes 7077892
  168.8 15.7 %copy-start.9 = (f32[128,768]{1,0:T(8,128)S(1)}, f32[128,768]{1,0:T(8,128)}, u32[]{:S(2)}) copy-start(f32[128,768]{1,0:T(8,128)} %convolution_add_fusion.1.refs_0_.refs_4_) | copy-start | bytes 1179652
  168.8 15.7 %copy-start.22 = (bf16[128,1536]{1,0:T(8,128)(2,1)S(1)}, bf16[128,1536]{1,0:T(8,128)(2,1)}, u32[]{:S(2)}) copy-start(bf16[128,1536]{1,0:T(8,128)(2,1)} %get-tuple-element.78.refs_2_) | copy-start | bytes 1179652
  168.8 15.7 %copy-start.32 = (f32[128]{0:T(128)S(1)}, f32[128]{0:T(128)}, u32[]{:S(2)}) copy-start(f32[128]{0:T(128)} %copy-done.31) | copy-start | bytes 1540
  182.8 10.4 %collective-permute-start.25 = (bf16[4,4,24,4992]{3,2,1,0:T(8,128)(2,1)}, bf16[4,4,24,4992]{3,2,1,0:T(8,128)(2,1)}, u32[]{:S(2)}, u32[]{:S(2)}) collective-permute-start(bf16[4,4,24,4992]{3,2,1,0:T(8,128)(2,1)} %get-tuple-element.88), channel_id=1, source_target_pairs={{0,1},{1,0},{2,3},{3,2},{4,5},{5,4},{6,7},{7,6},{8,9},{9,8},{10,11... | collective-permute-start | bytes 11501576 | tf_op jit(solution)/shard_map/ppermute | solution.py:431
  183.2 6.2 %collective-permute-start.26 = (bf16[2,48,768]{2,1,0:T(8,128)(2,1)}, bf16[2,48,768]{2,1,0:T(8,128)(2,1)S(1)}, u32[]{:S(2)}, u32[]{:S(2)}) collective-permute-start(bf16[2,48,768]{2,1,0:T(8,128)(2,1)} %get-tuple-element.91.refs_0_), channel_id=1, source_target_pairs={{0,4},{1,5},{2,6},{3,7},{4,0},{5,1},{6,2},{7,3},{8,12},{9,13},{10,... | collective-permute-start | bytes 442376 | tf_op jit(solution)/shard_map/ppermute | solution.py:431
  183.8 5.8 %collective-permute-start.27 = (bf16[2,48,768]{2,1,0:T(8,128)(2,1)}, bf16[2,48,768]{2,1,0:T(8,128)(2,1)S(1)}, u32[]{:S(2)}, u32[]{:S(2)}) collective-permute-start(bf16[2,48,768]{2,1,0:T(8,128)(2,1)} %get-tuple-element.92.refs_1_), channel_id=1, source_target_pairs={{0,2},{1,3},{2,0},{3,1},{4,6},{5,7},{6,4},{7,5},{8,10},{9,11},{10,... | collective-permute-start | bytes 442376 | tf_op jit(solution)/shard_map/ppermute | solution.py:431
  190.9 23.7 %collective-permute-start.47 = (bf16[4,48,768]{2,1,0:T(8,128)(2,1)S(1)}, bf16[4,48,768]{2,1,0:T(8,128)(2,1)S(1)}, u32[]{:S(2)}, u32[]{:S(2)}) collective-permute-start(bf16[4,48,768]{2,1,0:T(8,128)(2,1)S(1)} %get-tuple-element.113.refs_0_), channel_id=1, source_target_pairs={{0,2},{1,3},{2,0},{3,1},{4,6},{5,7},{6,4},{7,5},{8,10},{9,11},{10,... | collective-permute-start | bytes 884744 | tf_op jit(solution)/shard_map/ppermute | solution.py:431
  191.7 22.9 %collective-permute-start.48 = (bf16[4,48,768]{2,1,0:T(8,128)(2,1)S(1)}, bf16[4,48,768]{2,1,0:T(8,128)(2,1)S(1)}, u32[]{:S(2)}, u32[]{:S(2)}) collective-permute-start(bf16[4,48,768]{2,1,0:T(8,128)(2,1)S(1)} %get-tuple-element.114.refs_1_), channel_id=1, source_target_pairs={{0,4},{1,5},{2,6},{3,7},{4,0},{5,1},{6,2},{7,3},{8,12},{9,13},{10,... | collective-permute-start | bytes 884744 | tf_op jit(solution)/shard_map/ppermute | solution.py:431
  194.6 15.0 %collective-permute-start.36 = (bf16[2,24,4992]{2,1,0:T(8,128)(2,1)S(1)}, bf16[2,24,4992]{2,1,0:T(8,128)(2,1)S(1)}, u32[]{:S(2)}, u32[]{:S(2)}) collective-permute-start(bf16[2,24,4992]{2,1,0:T(8,128)(2,1)S(1)} %get-tuple-element.107.refs_0_), channel_id=1, source_target_pairs={{0,4},{1,5},{2,6},{3,7},{4,0},{5,1},{6,2},{7,3},{8,12},{9,13},{10,... | collective-permute-start | bytes 1437704 | tf_op jit(solution)/shard_map/ppermute | solution.py:431
  195.2 14.5 %collective-permute-start.37 = (bf16[2,24,4992]{2,1,0:T(8,128)(2,1)S(1)}, bf16[2,24,4992]{2,1,0:T(8,128)(2,1)S(1)}, u32[]{:S(2)}, u32[]{:S(2)}) collective-permute-start(bf16[2,24,4992]{2,1,0:T(8,128)(2,1)S(1)} %get-tuple-element.108.refs_1_), channel_id=1, source_target_pairs={{0,2},{1,3},{2,0},{3,1},{4,6},{5,7},{6,4},{7,5},{8,10},{9,11},{10,... | collective-permute-start | bytes 1437704 | tf_op jit(solution)/shard_map/ppermute | solution.py:431
  211.8 21.1 %collective-permute-start.38 = (bf16[4,24,4992]{2,1,0:T(8,128)(2,1)S(1)}, bf16[4,24,4992]{2,1,0:T(8,128)(2,1)S(1)}, u32[]{:S(2)}, u32[]{:S(2)}) collective-permute-start(bf16[4,24,4992]{2,1,0:T(8,128)(2,1)S(1)} %get-tuple-element.109), channel_id=1, source_target_pairs={{0,2},{1,3},{2,0},{3,1},{4,6},{5,7},{6,4},{7,5},{8,10},{9,11},{10,... | collective-permute-start | bytes 2875400 | tf_op jit(solution)/shard_map/ppermute | solution.py:431
  213.1 20.7 %collective-permute-start.39 = (bf16[4,24,4992]{2,1,0:T(8,128)(2,1)S(1)}, bf16[4,24,4992]{2,1,0:T(8,128)(2,1)S(1)}, u32[]{:S(2)}, u32[]{:S(2)}) collective-permute-start(bf16[4,24,4992]{2,1,0:T(8,128)(2,1)S(1)} %get-tuple-element.110), channel_id=1, source_target_pairs={{0,4},{1,5},{2,6},{3,7},{4,0},{5,1},{6,2},{7,3},{8,12},{9,13},{10,... | collective-permute-start | bytes 2875400 | tf_op jit(solution)/shard_map/ppermute | solution.py:431
  214.5 8.9 %collective-permute-start.42 = (bf16[2,8,1792]{2,1,0:T(8,128)(2,1)S(1)}, bf16[2,8,1792]{2,1,0:T(8,128)(2,1)S(1)}, u32[]{:S(2)}, u32[]{:S(2)}) collective-permute-start(bf16[2,8,1792]{2,1,0:T(8,128)(2,1)S(1)} %pad_maximum_fusion.4), channel_id=1, source_target_pairs={{0,1},{1,0},{2,3},{3,2},{4,5},{5,4},{6,7},{7,6},{8,9},{9,8},{10,11... | collective-permute-start | bytes 172040 | tf_op jit(solution)/shard_map/ppermute | solution.py:431
  214.6 39.1 %copy-start.24 = (bf16[4,48,768]{2,1,0:T(8,128)(2,1)}, bf16[4,48,768]{2,1,0:T(8,128)(2,1)S(1)}, u32[]{:S(2)}) copy-start(bf16[4,48,768]{2,1,0:T(8,128)(2,1)S(1)} %collective-permute-done.48) | copy-start | bytes 884740
  215.7 15.3 %collective-permute-start.49 = (bf16[2,48,768]{2,1,0:T(8,128)(2,1)S(1)}, bf16[2,48,768]{2,1,0:T(8,128)(2,1)S(1)}, u32[]{:S(2)}, u32[]{:S(2)}) collective-permute-start(bf16[2,48,768]{2,1,0:T(8,128)(2,1)S(1)} %fusion.33), channel_id=1, source_target_pairs={{0,16},{1,17},{2,18},{3,19},{4,20},{5,21},{6,22},{7,23},{8,24},{9,... | collective-permute-start | bytes 442376 | tf_op jit(solution)/shard_map/ppermute | solution.py:431
  223.4 39.3 %collective-permute-start.43 = (bf16[2,8,1792]{2,1,0:T(8,128)(2,1)S(1)}, bf16[2,8,1792]{2,1,0:T(8,128)(2,1)S(1)}, u32[]{:S(2)}, u32[]{:S(2)}) collective-permute-start(bf16[2,8,1792]{2,1,0:T(8,128)(2,1)S(1)} %add_convert_fusion.9), channel_id=1, source_target_pairs={{0,8},{1,9},{2,10},{3,11},{4,12},{5,13},{6,14},{7,15},{8,0},{9,1},... | collective-permute-start | bytes 172040 | tf_op jit(solution)/shard_map/ppermute | solution.py:431
  232.0 33.7 %collective-permute-start.50 = (bf16[1,48,768]{2,1,0:T(8,128)(2,1)S(1)}, bf16[1,48,768]{2,1,0:T(8,128)(2,1)S(1)}, u32[]{:S(2)}, u32[]{:S(2)}) collective-permute-start(bf16[1,48,768]{2,1,0:T(8,128)(2,1)S(1)} %fusion.40), channel_id=1, source_target_pairs={{0,8},{1,9},{2,10},{3,11},{4,12},{5,13},{6,14},{7,15},{8,0},{9,1},... | collective-permute-start | bytes 221192 | tf_op jit(solution)/shard_map/ppermute | solution.py:431
  235.5 25.9 %collective-permute-start.40 = (bf16[2,24,4992]{2,1,0:T(8,128)(2,1)S(1)}, bf16[2,24,4992]{2,1,0:T(8,128)(2,1)S(1)}, u32[]{:S(2)}, u32[]{:S(2)}) collective-permute-start(bf16[2,24,4992]{2,1,0:T(8,128)(2,1)S(1)} %fusion.7), channel_id=1, source_target_pairs={{0,16},{1,17},{2,18},{3,19},{4,20},{5,21},{6,22},{7,23},{8,24},{9,... | collective-permute-start | bytes 1437704 | tf_op jit(solution)/shard_map/ppermute | solution.py:431
  253.7 17.3 %copy-start.3 = (bf16[4,4,24,3456]{3,2,1,0:T(8,128)(2,1)S(1)}, bf16[4,4,24,3456]{3,2,1,0:T(8,128)(2,1)}, u32[]{:S(2)}) copy-start(bf16[4,4,24,3456]{3,2,1,0:T(8,128)(2,1)} %get-tuple-element.98) | copy-start | bytes 7962628
  253.7 17.3 %collective-permute-start.28 = (bf16[4,4,24,3456]{3,2,1,0:T(8,128)(2,1)}, bf16[4,4,24,3456]{3,2,1,0:T(8,128)(2,1)S(1)}, u32[]{:S(2)}, u32[]{:S(2)}) collective-permute-start(bf16[4,4,24,3456]{3,2,1,0:T(8,128)(2,1)} %get-tuple-element.99), channel_id=1, source_target_pairs={{0,1},{1,0},{2,3},{3,2},{4,5},{5,4},{6,7},{7,6},{8,9},{9,8},{10,11... | collective-permute-start | bytes 7962632 | tf_op jit(solution)/shard_map/ppermute | solution.py:431
  262.7 6.9 %collective-permute-start.41 = (bf16[1,24,4992]{2,1,0:T(8,128)(2,1)S(1)}, bf16[1,24,4992]{2,1,0:T(8,128)(2,1)S(1)}, u32[]{:S(2)}, u32[]{:S(2)}) collective-permute-start(bf16[1,24,4992]{2,1,0:T(8,128)(2,1)S(1)} %fusion.14), channel_id=1, source_target_pairs={{0,8},{1,9},{2,10},{3,11},{4,12},{5,13},{6,14},{7,15},{8,0},{9,1},... | collective-permute-start | bytes 718856 | tf_op jit(solution)/shard_map/ppermute | solution.py:431
  262.8 34.2 %collective-permute-start.44 = (bf16[2,8,1792]{2,1,0:T(8,128)(2,1)S(1)}, bf16[2,8,1792]{2,1,0:T(8,128)(2,1)S(1)}, u32[]{:S(2)}, u32[]{:S(2)}) collective-permute-start(bf16[2,8,1792]{2,1,0:T(8,128)(2,1)S(1)} %add_convert_fusion.8), channel_id=1, source_target_pairs={{0,16},{1,17},{2,18},{3,19},{4,20},{5,21},{6,22},{7,23},{8,24},{9,... | collective-permute-start | bytes 172040 | tf_op jit(solution)/shard_map/ppermute | solution.py:431
  270.9 23.0 %copy-start.4 = (bf16[4,4,24,3456]{3,2,1,0:T(8,128)(2,1)}, bf16[4,4,24,3456]{3,2,1,0:T(8,128)(2,1)S(1)}, u32[]{:S(2)}) copy-start(bf16[4,4,24,3456]{3,2,1,0:T(8,128)(2,1)S(1)} %collective-permute-done.28) | copy-start | bytes 7962628
  271.1 7.2 %collective-permute-start.29 = (bf16[2,24,3456]{2,1,0:T(8,128)(2,1)S(1)}, bf16[2,24,3456]{2,1,0:T(8,128)(2,1)S(1)}, u32[]{:S(2)}, u32[]{:S(2)}) collective-permute-start(bf16[2,24,3456]{2,1,0:T(8,128)(2,1)S(1)} %get-tuple-element.100), channel_id=1, source_target_pairs={{0,4},{1,5},{2,6},{3,7},{4,0},{5,1},{6,2},{7,3},{8,12},{9,13},{10,... | collective-permute-start | bytes 995336 | tf_op jit(solution)/shard_map/ppermute | solution.py:431
  272.6 8.0 %collective-permute-start.30 = (bf16[2,24,3456]{2,1,0:T(8,128)(2,1)S(1)}, bf16[2,24,3456]{2,1,0:T(8,128)(2,1)S(1)}, u32[]{:S(2)}, u32[]{:S(2)}) collective-permute-start(bf16[2,24,3456]{2,1,0:T(8,128)(2,1)S(1)} %get-tuple-element.101), channel_id=1, source_target_pairs={{0,2},{1,3},{2,0},{3,1},{4,6},{5,7},{6,4},{7,5},{8,10},{9,11},{10,... | collective-permute-start | bytes 995336 | tf_op jit(solution)/shard_map/ppermute | solution.py:431
  281.1 12.8 %collective-permute-start.31 = (bf16[4,24,3456]{2,1,0:T(8,128)(2,1)S(1)}, bf16[4,24,3456]{2,1,0:T(8,128)(2,1)S(1)}, u32[]{:S(2)}, u32[]{:S(2)}) collective-permute-start(bf16[4,24,3456]{2,1,0:T(8,128)(2,1)S(1)} %get-tuple-element.102), channel_id=1, source_target_pairs={{0,2},{1,3},{2,0},{3,1},{4,6},{5,7},{6,4},{7,5},{8,10},{9,11},{10,... | collective-permute-start | bytes 1990664 | tf_op jit(solution)/shard_map/ppermute | solution.py:431
  282.4 11.5 %collective-permute-start.32 = (bf16[4,24,3456]{2,1,0:T(8,128)(2,1)S(1)}, bf16[4,24,3456]{2,1,0:T(8,128)(2,1)S(1)}, u32[]{:S(2)}, u32[]{:S(2)}) collective-permute-start(bf16[4,24,3456]{2,1,0:T(8,128)(2,1)S(1)} %get-tuple-element.103), channel_id=1, source_target_pairs={{0,4},{1,5},{2,6},{3,7},{4,0},{5,1},{6,2},{7,3},{8,12},{9,13},{10,... | collective-permute-start | bytes 1990664 | tf_op jit(solution)/shard_map/ppermute | solution.py:431
  293.9 16.6 %copy-start.14 = (bf16[4,24,3456]{2,1,0:T(8,128)(2,1)}, bf16[4,24,3456]{2,1,0:T(8,128)(2,1)S(1)}, u32[]{:S(2)}) copy-start(bf16[4,24,3456]{2,1,0:T(8,128)(2,1)S(1)} %collective-permute-done.31) | copy-start | bytes 1990660
  293.9 16.6 %copy-start.15 = (bf16[4,24,3456]{2,1,0:T(8,128)(2,1)}, bf16[4,24,3456]{2,1,0:T(8,128)(2,1)S(1)}, u32[]{:S(2)}) copy-start(bf16[4,24,3456]{2,1,0:T(8,128)(2,1)S(1)} %collective-permute-done.32) | copy-start | bytes 1990660
  297.0 4.2 %collective-permute-start.45 = (bf16[2,8,1792]{2,1,0:T(8,128)(2,1)S(1)}, bf16[2,8,1792]{2,1,0:T(8,128)(2,1)S(1)}, u32[]{:S(2)}, u32[]{:S(2)}) collective-permute-start(bf16[2,8,1792]{2,1,0:T(8,128)(2,1)S(1)} %fusion.44), channel_id=1, source_target_pairs={{0,2},{1,3},{2,0},{3,1},{4,6},{5,7},{6,4},{7,5},{8,10},{9,11},{10,... | collective-permute-start | bytes 172040 | tf_op jit(solution)/shard_map/ppermute | solution.py:431
  301.3 6.7 %collective-permute-start.46 = (bf16[2,8,1792]{2,1,0:T(8,128)(2,1)S(1)}, bf16[2,8,1792]{2,1,0:T(8,128)(2,1)S(1)}, u32[]{:S(2)}, u32[]{:S(2)}) collective-permute-start(bf16[2,8,1792]{2,1,0:T(8,128)(2,1)S(1)} %add_convert_fusion.6), channel_id=1, source_target_pairs={{0,4},{1,5},{2,6},{3,7},{4,0},{5,1},{6,2},{7,3},{8,12},{9,13},{10,... | collective-permute-start | bytes 172040 | tf_op jit(solution)/shard_map/ppermute | solution.py:431
  302.2 10.5 %collective-permute-start.33 = (bf16[1,24,3456]{2,1,0:T(8,128)(2,1)}, bf16[1,24,3456]{2,1,0:T(8,128)(2,1)S(1)}, u32[]{:S(2)}, u32[]{:S(2)}) collective-permute-start(bf16[1,24,3456]{2,1,0:T(8,128)(2,1)} %get-tuple-element.104), channel_id=1, source_target_pairs={{0,8},{1,9},{2,10},{3,11},{4,12},{5,13},{6,14},{7,15},{8,0},{9,1},... | collective-permute-start | bytes 497672 | tf_op jit(solution)/shard_map/ppermute | solution.py:431
  302.2 13.6 %collective-permute-start.34 = (bf16[1,24,3456]{2,1,0:T(8,128)(2,1)}, bf16[1,24,3456]{2,1,0:T(8,128)(2,1)S(1)}, u32[]{:S(2)}, u32[]{:S(2)}) collective-permute-start(bf16[1,24,3456]{2,1,0:T(8,128)(2,1)} %get-tuple-element.105), channel_id=1, source_target_pairs={{0,16},{1,17},{2,18},{3,19},{4,20},{5,21},{6,22},{7,23},{8,24},{9,... | collective-permute-start | bytes 497672 | tf_op jit(solution)/shard_map/ppermute | solution.py:431
  307.9 7.9 %collective-permute-start.35 = (bf16[1,24,3456]{2,1,0:T(8,128)(2,1)}, bf16[1,24,3456]{2,1,0:T(8,128)(2,1)S(1)}, u32[]{:S(2)}, u32[]{:S(2)}) collective-permute-start(bf16[1,24,3456]{2,1,0:T(8,128)(2,1)} %get-tuple-element.106), channel_id=1, source_target_pairs={{0,24},{1,25},{2,26},{3,27},{4,28},{5,29},{6,30},{7,31},{8,16},{9,... | collective-permute-start | bytes 497672 | tf_op jit(solution)/shard_map/ppermute | solution.py:431
  (22 other events, 150.8 us)

commit v4 on v3

--- a/solution.py
+++ b/solution.py
@@ -523,14 +523,20 @@
 
 
 class Total:
-    def __init__(self, values):
-        self.values = values
+    def __init__(self, first, second, me):
+        self.even = me % 2 == 0
+        self.values = jnp.where(self.even, first, second)
+        self.values += swap(jnp.where(self.even, second, first), 1, PARTS)
 
     def add(self, bit, awaited=None):
-        low = self.values.astype(LOW)
+        values = self.values
         if awaited is not None:
-            low = low + nothing(awaited)
-        self.values = low.astype(F32) + swap(low, bit, PARTS).astype(F32)
+            values = values + nothing(awaited).astype(F32)
+        self.values = values + swap(values, bit, PARTS)
+
+    def both(self):
+        other = swap(self.values, 1, PARTS)
+        return jnp.stack([jnp.where(self.even, self.values, other), jnp.where(self.even, other, self.values)])
 
 
 def grow(values, other, me, bit):
@@ -699,14 +705,13 @@
     dhidden, small0 = backward_mixer(
         gated_grad, hidden, ssm, small[0], segs, *[item[0] for item in to_xy_c]
     )
-    sums = Total(jnp.stack([small0, small1]))
+    sums = Total(small0, small1, me)
     sum_b.add_core(core)
     sum_c.add_xy(*got)
 
     to_far_b = sum_b.across()
     far_b = phase([], *to_far_b)
     (far_c,) = phase([], *sum_c.far_z())
-    sums.add(1)
     grad, keep, send = backward_in(
         place, grad, resid, normed, dhidden, in0_full, small[0][0], *[item[0] for item in to_far_b]
     )
@@ -733,7 +738,7 @@
     both = sum_b.end(near_b)
     in_grads = [sum_a.result(*parts), both[:, 2 * WIDTH :]]
     out_grads = [jnp.concatenate([both[:, :WIDTH], both[:, WIDTH : 2 * WIDTH]]), sum_c.end(near_c)]
-    return mixed, grad, in_grads, out_grads, sums.values
+    return mixed, grad, in_grads, out_grads, sums.both()
 
 
 def body(

time: 320 us -> 322 us (level)
  starting transfers between devices: 61.7 us -> 49.1 us
  waiting for transfers between devices: 100 us -> 112 us
  other arithmetic: 29 us -> 35.1 us
  local copies, waits for them, and re-layouts: 22.6 us -> 18.7 us
    ppermute x51 -> x52, starting transfers between devices: 61.7 us -> 49.1 us  [swap(): lax.ppermute(values, 'fsdp', [(index, index ^ bit) for index in range(cou...]
    ppermute x51 -> x52, waiting for transfers between devices: 100 us -> 112 us  [swap(): lax.ppermute(values, 'fsdp', [(index, index ^ bit) for index in range(cou...]
  transfers between devices with their start and end apart: 51 -> 52, of which waited for: 25 -> 25; matrix products, arithmetic and copies ran while one was open for 13% -> 14% of each run, Pallas kernels for 17% -> 17%
where the time goes in v4:
time: 322 us; the launch traced here: 321 us
  waiting for transfers between devices  112 us (35%)
  Pallas kernels  94.3 us (29%)
  starting transfers between devices  49.1 us (15%)
  other arithmetic  35.1 us (11%)
  local copies, waits for them, and re-layouts  18.7 us (6%)
  between operations  7.16 us (2%)
  matrix products  5.07 us (2%)
    ppermute x52, waiting for transfers between devices, swap(): lax.ppermute(values, 'fsdp', [(index, index ^ bit) for index in range(cou...  112 us
    pallas_call x10, Pallas kernels, call(): pl.pallas_call(partial(skip_first, kernel, len(awaited)), out_shape=outs,...  94.3 us
    ppermute x52, starting transfers between devices, swap(): lax.ppermute(values, 'fsdp', [(index, index ^ bit) for index in range(cou...  49.1 us
    slice x9, local copies, waits for them, and re-layouts, nothing(): return values[(slice(0, 1),) * values.ndim].reshape(()) * 0  7.34 us
  transfers between devices with their start and end apart: 52, of which 25 were waited for; matrix products, arithmetic and copies ran while one was open for 14% of the time, Pallas kernels for 17%

profile of v4, /device:TPU:0, one launch (start us, length us, event | category | flops | bytes accessed | tf_op | source)
XLA Modules:
  0.0 321.1 jit_solution(16321209532129939394)
XLA Ops:
  5.1 3.1 collective-permute-start
  8.1 2.5 collective-permute-start.3
  12.8 6.6 %collective-permute-done.3 = bf16[1,24,3456]{2,1,0:T(8,128)(2,1)S(1)} collective-permute-done((bf16[1,24,3456]{2,1,0:T(8,128)(2,1)S(1)}, bf16[1,24,3456]{2,1,0:T(8,128)(2,1)S(1)}, u32[]{:S(2)}, u32[]{:S(2)}) %collective-permute-start.3) | collective-permute-done | bytes 165920 | tf_op jit(solution)/shard_map/ppermute | solution.py:431
  19.4 6.0 %collective-permute-done.2 = bf16[1,24,3456]{2,1,0:T(8,128)(2,1)S(1)} collective-permute-done((bf16[1,24,3456]{2,1,0:T(8,128)(2,1)S(1)}, bf16[1,24,3456]{2,1,0:T(8,128)(2,1)S(1)}, u32[]{:S(2)}, u32[]{:S(2)}) %collective-permute-start.2) | collective-permute-done | bytes 165920 | tf_op jit(solution)/shard_map/ppermute | solution.py:431
  25.5 1.6 collective-permute-start.4
  28.3 3.2 collective-permute-start.5
  31.5 1.2 collective-permute-start.6
  32.7 1.5 collective-permute-start.7
  34.2 7.5 %collective-permute-done.1 = bf16[1,24,6528]{2,1,0:T(8,128)(2,1)S(1)} collective-permute-done((bf16[1,24,6528]{2,1,0:T(8,128)(2,1)S(1)}, bf16[1,24,6528]{2,1,0:T(8,128)(2,1)S(1)}, u32[]{:S(2)}, u32[]{:S(2)}) %collective-permute-start.1) | collective-permute-done | bytes 313376 | tf_op jit(solution)/shard_map/ppermute | solution.py:431
  42.2 11.1 %collective-permute-done.5 = bf16[1,24,6528]{2,1,0:T(8,128)(2,1)S(1)} collective-permute-done((bf16[1,24,6528]{2,1,0:T(8,128)(2,1)S(1)}, bf16[1,24,6528]{2,1,0:T(8,128)(2,1)S(1)}, u32[]{:S(2)}, u32[]{:S(2)}) %collective-permute-start.5) | collective-permute-done | bytes 313376 | tf_op jit(solution)/shard_map/ppermute | solution.py:431
  58.3 1.6 collective-permute-start.8
  60.4 5.1 %collective-permute-done.8.refs_4_ = bf16[2,24,3456]{2,1,0:T(8,128)(2,1)S(1)} collective-permute-done((bf16[2,24,3456]{2,1,0:T(8,128)(2,1)S(1)}, bf16[2,24,3456]{2,1,0:T(8,128)(2,1)S(1)}, u32[]{:S(2)}, u32[]{:S(2)}) %collective-permute-start.8) | collective-permute-done | bytes 331808 | tf_op jit(solution)/shard_map/ppermute | solution.py:431
  66.0 3.5 %collective-permute-done.9.refs_5_ = bf16[2,24,3456]{2,1,0:T(8,128)(2,1)} collective-permute-done((bf16[2,24,3456]{2,1,0:T(8,128)(2,1)S(1)}, bf16[2,24,3456]{2,1,0:T(8,128)(2,1)}, u32[]{:S(2)}, u32[]{:S(2)}) %collective-permute-start.9) | collective-permute-done | bytes 331808 | tf_op jit(solution)/shard_map/ppermute | solution.py:431
  69.5 1.2 slice.451
  77.3 1.7 bitcast_convert_fusion.refs_2_.refs_4_
  79.7 5.2 %place.2 = bf16[32,1,24,3456]{3,2,1,0:T(8,128)(2,1)} custom-call(s32[1]{0:T(128)} %bitcast.6.refs_0_.refs_2_, bf16[4,24,3456]{2,1,0:T(8,128)(2,1)} %copy-done.5, bf16[4,24,3456]{2,1,0:T(8,128)(2,1)} %collective-permute-done.4.refs_2_, bf16[4,24,3456]{2,1,0:T(8,128)(2,1)} %collective-permute-done.7.refs_3_, bf16[2,24,3456]{2,1,0:T(8,128)(2,1)} %copy-done.21, ...), custom_call_target="tpu_custom_call" | custom-call | bytes 21233664 | tf_op jit(solution)/shard_map/place/pallas_call | solution.py:362
  86.8 4.3 %unpack.1 = (f32[1,768]{1,0:T(1,128)}, f32[5,1792]{1,0:T(8,128)}, f32[1,1536]{1,0:T(1,128)}, f32[1,768]{1,0:T(1,128)}, f32[5,1792]{1,0:T(8,128)}, /*index=5*/f32[1,1536]{1,0:T(1,128)}) custom-call(bf16[64,384]{1,0:T(8,128)(2,1)} %pad.54.refs_0_), custom_call_target="tpu_custom_call" | custom-call | bytes 200000 | tf_op jit(solution)/shard_map/unpack/pallas_call | solution.py:362
  91.1 1.2 slice.353
  94.8 15.1 %collective-permute-done.16.refs_3_ = bf16[4,24,6528]{2,1,0:T(8,128)(2,1)} collective-permute-done((bf16[4,24,6528]{2,1,0:T(8,128)(2,1)S(1)}, bf16[4,24,6528]{2,1,0:T(8,128)(2,1)}, u32[]{:S(2)}, u32[]{:S(2)}) %collective-permute-start.16) | collective-permute-done | bytes 1253408 | tf_op jit(solution)/shard_map/ppermute | solution.py:431
  109.9 1.1 slice_add_fusion.refs_1_
  111.0 1.6 collective-permute-start.18
  112.6 11.4 %mix_forward.2 = (f32[128,3456]{1,0:T(8,128)}, f32[128,1536]{1,0:T(8,128)}, bf16[128,768]{1,0:T(8,128)(2,1)}, bf16[128,1536]{1,0:T(8,128)(2,1)}) custom-call(bf16[2,24,6528]{2,1,0:T(8,128)(2,1)} %copy-done.18, bf16[2,24,6528]{2,1,0:T(8,128)(2,1)} %copy-done.17, f32[128,768]{1,0:T(8,128)} %bitcast_convert_fusion.refs_2_.refs_4_, bf16[768,3456]{1,0:T(8,128)(2,1)} %bitcast.179, ...), custom_call_target="tpu_custom_call" | custom-call | flops 10000000000 | bytes 10000000 | tf_op jit(solution)/shard_map/mix_forward/pallas_call | solution.py:362
  124.0 1.2 slice.358
  130.0 1.8 collective-permute-done.21.refs_8_
  132.9 8.4 %place.3 = (bf16[32,2,24,768]{3,2,1,0:T(8,128)(2,1)}, bf16[32,1,24,3456]{3,2,1,0:T(8,128)(2,1)}, bf16[32,2,24,768]{3,2,1,0:T(8,128)(2,1)}) custom-call(s32[1]{0:T(128)} %bitcast.6.refs_0_.refs_2_, bf16[4,24,6528]{2,1,0:T(8,128)(2,1)} %copy-done, bf16[4,24,6528]{2,1,0:T(8,128)(2,1)} %copy-done.2, bf16[4,24,6528]{2,1,0:T(8,128)(2,1)} %collective-permute-done.16.refs_3_, ...), custom_call_target="tpu_custom_call" | custom-call | bytes 40108032 | tf_op jit(solution)/shard_map/place/pallas_call | solution.py:362
  141.2 2.9 convolution_add_fusion.1.refs_0_.refs_4_
  144.1 11.2 %mix_forward.3 = (f32[128,3456]{1,0:T(8,128)}, f32[128,1536]{1,0:T(8,128)}, bf16[128,768]{1,0:T(8,128)(2,1)}, bf16[128,1536]{1,0:T(8,128)(2,1)}) custom-call(f32[128,768]{1,0:T(8,128)} %convolution_add_fusion.1.refs_0_.refs_4_, bf16[768,3456]{1,0:T(8,128)(2,1)} %bitcast.201, f32[1,768]{1,0:T(1,128)} %get-tuple-element.75.refs_2_.refs_8_, ...), custom_call_target="tpu_custom_call" | custom-call | flops 10000000000 | bytes 10000000 | tf_op jit(solution)/shard_map/mix_forward/pallas_call | solution.py:362
  155.4 5.4 %out_backward.1 = (f32[128,1536]{1,0:T(8,128)}, bf16[4,4,48,768]{3,2,1,0:T(8,128)(2,1)}, bf16[4,4,48,768]{3,2,1,0:T(8,128)(2,1)}) custom-call(s32[1]{0:T(128)} %bitcast.6.refs_0_.refs_2_, f32[128,768]{1,0:T(8,128)} %convert_multiply_fusion.refs_1_.refs_3_, bf16[128,1536]{1,0:T(8,128)(2,1)} %get-tuple-element.78.refs_2_, bf16[1536,768]{1,0:T(8,128)(2,1)} %bitcast.181), custom_call_target="tpu_custom_call" | custom-call | flops 2000000000 | bytes 8000000 | tf_op jit(solution)/shard_map/out_backward/pallas_call | solution.py:362
  160.9 11.9 %mix_backward.2 = (bf16[128,3456]{1,0:T(8,128)(2,1)}, f32[8,1792]{1,0:T(8,128)}) custom-call(f32[128,1536]{1,0:T(8,128)} %get-tuple-element.83.refs_0_, f32[128,3456]{1,0:T(8,128)} %get-tuple-element.84.refs_1_, f32[128,1536]{1,0:T(8,128)} %get-tuple-element.85.refs_2_, f32[5,1792]{1,0:T(8,128)} %get-tuple-element.76.refs_3_, ...), custom_call_target="tpu_custom_call" | custom-call | flops 12000000000 | bytes 5000000 | tf_op jit(solution)/shard_map/mix_backward/pallas_call | solution.py:362
  173.7 13.9 %both_backward.1 = (f32[128,768]{1,0:T(8,128)}, bf16[4,4,24,4992]{3,2,1,0:T(8,128)(2,1)}, bf16[4,4,24,4992]{3,2,1,0:T(8,128)(2,1)}, f32[128,1536]{1,0:T(8,128)}) custom-call(bf16[2,48,768]{2,1,0:T(8,128)(2,1)} %get-tuple-element.91.refs_0_, bf16[2,48,768]{2,1,0:T(8,128)(2,1)} %get-tuple-element.92.refs_1_, s32[1]{0:T(128)} %bitcast.6.refs_0_.refs_2_, ...), custom_call_target="tpu_custom_call" | custom-call | flops 8000000000 | bytes 22000000 | tf_op jit(solution)/shard_map/both_backward/pallas_call | solution.py:362
  189.0 4.9 %collective-permute-done.27 = bf16[2,48,768]{2,1,0:T(8,128)(2,1)S(1)} collective-permute-done((bf16[2,48,768]{2,1,0:T(8,128)(2,1)S(1)}, bf16[2,48,768]{2,1,0:T(8,128)(2,1)S(1)}, u32[]{:S(2)}, u32[]{:S(2)}) %collective-permute-start.27) | collective-permute-done | bytes 147488 | tf_op jit(solution)/shard_map/ppermute | solution.py:431
  195.6 1.3 collective-permute-start.48
  196.9 2.5 fusion.11
  200.1 1.7 collective-permute-start.36
  201.9 12.0 %mix_backward.3 = (bf16[128,3456]{1,0:T(8,128)(2,1)}, f32[8,1792]{1,0:T(8,128)}) custom-call(bf16[4,48,768]{2,1,0:T(8,128)(2,1)} %get-tuple-element.113.refs_0_, bf16[4,48,768]{2,1,0:T(8,128)(2,1)} %get-tuple-element.114.refs_1_, f32[128,1536]{1,0:T(8,128)} %get-tuple-element.93.refs_2_, f32[128,3456]{1,0:T(8,128)} %get-tuple-element.94.refs_3_, ...), custom_call_target="tpu_custom_call" | custom-call | flops 12000000000 | bytes 5000000 | tf_op jit(solution)/shard_map/mix_backward/pallas_call | solution.py:362
  213.9 2.1 fusion
  216.0 1.6 collective-permute-start.39
  217.6 1.3 collective-permute-start.38
  220.1 1.7 collective-permute-start.50
  221.8 2.5 collective-permute-start.43
  224.3 6.1 %collective-permute-done.50 = bf16[2,48,768]{2,1,0:T(8,128)(2,1)S(1)} collective-permute-done((bf16[2,48,768]{2,1,0:T(8,128)(2,1)S(1)}, bf16[2,48,768]{2,1,0:T(8,128)(2,1)S(1)}, u32[]{:S(2)}, u32[]{:S(2)}) %collective-permute-start.50) | collective-permute-done | bytes 147488 | tf_op jit(solution)/shard_map/ppermute | solution.py:431
  230.5 1.6 fusion.40
  232.1 5.0 %collective-permute-done.39 = bf16[4,24,4992]{2,1,0:T(8,128)(2,1)S(1)} collective-permute-done((bf16[4,24,4992]{2,1,0:T(8,128)(2,1)S(1)}, bf16[4,24,4992]{2,1,0:T(8,128)(2,1)S(1)}, u32[]{:S(2)}, u32[]{:S(2)}) %collective-permute-start.39) | collective-permute-done | bytes 958496 | tf_op jit(solution)/shard_map/ppermute | solution.py:431
  237.0 1.2 collective-permute-done.38
  238.2 1.6 fusion.7
  239.8 1.7 collective-permute-start.40
  241.5 10.6 %in_backward.1 = (f32[128,768]{1,0:T(8,128)}, bf16[4,4,24,3456]{3,2,1,0:T(8,128)(2,1)}, bf16[4,4,24,3456]{3,2,1,0:T(8,128)(2,1)}) custom-call(bf16[2,24,4992]{2,1,0:T(8,128)(2,1)} %get-tuple-element.107.refs_0_, bf16[2,24,4992]{2,1,0:T(8,128)(2,1)} %copy-done.19, s32[1]{0:T(128)} %bitcast.6.refs_0_.refs_2_, f32[128,768]{1,0:T(8,128)} %get-tuple-element.89.refs_3_, ...), custom_call_target="tpu_custom_call" | custom-call | flops 6000000000 | bytes 14000000 | tf_op jit(solution)/shard_map/in_backward/pallas_call | solution.py:362
  252.2 8.4 %collective-permute-done.40 = bf16[2,24,4992]{2,1,0:T(8,128)(2,1)} collective-permute-done((bf16[2,24,4992]{2,1,0:T(8,128)(2,1)S(1)}, bf16[2,24,4992]{2,1,0:T(8,128)(2,1)}, u32[]{:S(2)}, u32[]{:S(2)}) %collective-permute-start.40) | collective-permute-done | bytes 479264 | tf_op jit(solution)/shard_map/ppermute | solution.py:431
  260.6 1.3 fusion.14
  262.0 2.2 fusion.5
  265.2 3.1 collective-permute-start.44
  268.2 1.7 fusion.43
  269.9 1.5 fusion.18
  271.6 1.3 collective-permute-start.30
  274.4 6.4 %collective-permute-done.30 = bf16[2,24,3456]{2,1,0:T(8,128)(2,1)S(1)} collective-permute-done((bf16[2,24,3456]{2,1,0:T(8,128)(2,1)S(1)}, bf16[2,24,3456]{2,1,0:T(8,128)(2,1)S(1)}, u32[]{:S(2)}, u32[]{:S(2)}) %collective-permute-start.30) | collective-permute-done | bytes 331808 | tf_op jit(solution)/shard_map/ppermute | solution.py:431
  283.9 13.5 %collective-permute-done.32 = bf16[4,24,3456]{2,1,0:T(8,128)(2,1)S(1)} collective-permute-done((bf16[4,24,3456]{2,1,0:T(8,128)(2,1)S(1)}, bf16[4,24,3456]{2,1,0:T(8,128)(2,1)S(1)}, u32[]{:S(2)}, u32[]{:S(2)}) %collective-permute-start.32) | collective-permute-done | bytes 663584 | tf_op jit(solution)/shard_map/ppermute | solution.py:431
  298.9 1.2 slice.497
  300.1 1.8 collective-permute-start.35
  302.2 2.3 collective-permute-start.33
  306.8 1.7 pad_maximum_fusion.3
  308.5 1.7 collective-permute-done.45
  310.3 1.3 collective-permute-start.46
  311.8 2.7 collective-permute-done.46
  314.6 1.4 fusion.31
  (210 shorter events, 47.3 us)
Async XLA Ops:
  5.1 7.7 %collective-permute-start = (bf16[1,24,3456]{2,1,0:T(8,128)(2,1)S(1)}, bf16[1,24,3456]{2,1,0:T(8,128)(2,1)S(1)}, u32[]{:S(2)}, u32[]{:S(2)}) collective-permute-start(bf16[1,24,3456]{2,1,0:T(8,128)(2,1)S(1)} %bitcast.186), channel_id=1, source_target_pairs={{0,8},{1,9},{2,10},{3,11},{4,12},{5,13},{6,14},{7,15},{8,0},{9,1},... | collective-permute-start | bytes 497672 | tf_op jit(solution)/shard_map/ppermute | solution.py:431
  8.1 11.2 %collective-permute-start.3 = (bf16[1,24,3456]{2,1,0:T(8,128)(2,1)S(1)}, bf16[1,24,3456]{2,1,0:T(8,128)(2,1)S(1)}, u32[]{:S(2)}, u32[]{:S(2)}) collective-permute-start(bf16[1,24,3456]{2,1,0:T(8,128)(2,1)S(1)} %bitcast.187), channel_id=1, source_target_pairs={{0,24},{1,25},{2,26},{3,27},{4,28},{5,29},{6,30},{7,31},{8,16},{9,... | collective-permute-start | bytes 497672 | tf_op jit(solution)/shard_map/ppermute | solution.py:431
  10.6 14.7 %collective-permute-start.2 = (bf16[1,24,3456]{2,1,0:T(8,128)(2,1)S(1)}, bf16[1,24,3456]{2,1,0:T(8,128)(2,1)S(1)}, u32[]{:S(2)}, u32[]{:S(2)}) collective-permute-start(bf16[1,24,3456]{2,1,0:T(8,128)(2,1)S(1)} %bitcast.188), channel_id=1, source_target_pairs={{0,16},{1,17},{2,18},{3,19},{4,20},{5,21},{6,22},{7,23},{8,24},{9,... | collective-permute-start | bytes 497672 | tf_op jit(solution)/shard_map/ppermute | solution.py:431
  25.4 47.5 %copy-start.5 = (bf16[4,24,3456]{2,1,0:T(8,128)(2,1)}, bf16[4,24,3456]{2,1,0:T(8,128)(2,1)S(1)}, u32[]{:S(2)}) copy-start(bf16[4,24,3456]{2,1,0:T(8,128)(2,1)S(1)} %pad_maximum_fusion.1.refs_1_) | copy-start | bytes 1990660
  25.5 30.8 %collective-permute-start.4 = (bf16[4,24,3456]{2,1,0:T(8,128)(2,1)S(1)}, bf16[4,24,3456]{2,1,0:T(8,128)(2,1)}, u32[]{:S(2)}, u32[]{:S(2)}) collective-permute-start(bf16[4,24,3456]{2,1,0:T(8,128)(2,1)S(1)} %pad_maximum_fusion.1.refs_1_), channel_id=1, source_target_pairs={{0,2},{1,3},{2,0},{3,1},{4,6},{5,7},{6,4},{7,5},{8,10},{9,11},{10,... | collective-permute-start | bytes 1990664 | tf_op jit(solution)/shard_map/ppermute | solution.py:431
  28.2 13.4 %collective-permute-start.1 = (bf16[1,24,6528]{2,1,0:T(8,128)(2,1)S(1)}, bf16[1,24,6528]{2,1,0:T(8,128)(2,1)S(1)}, u32[]{:S(2)}, u32[]{:S(2)}) collective-permute-start(bf16[1,24,6528]{2,1,0:T(8,128)(2,1)S(1)} %broadcast_add_fusion.5), channel_id=1, source_target_pairs={{0,8},{1,9},{2,10},{3,11},{4,12},{5,13},{6,14},{7,15},{8,0},{9,1},... | collective-permute-start | bytes 940040 | tf_op jit(solution)/shard_map/ppermute | solution.py:431
  28.3 24.9 %collective-permute-start.5 = (bf16[1,24,6528]{2,1,0:T(8,128)(2,1)S(1)}, bf16[1,24,6528]{2,1,0:T(8,128)(2,1)S(1)}, u32[]{:S(2)}, u32[]{:S(2)}) collective-permute-start(bf16[1,24,6528]{2,1,0:T(8,128)(2,1)S(1)} %broadcast_add_fusion.5), channel_id=1, source_target_pairs={{0,16},{1,17},{2,18},{3,19},{4,20},{5,21},{6,22},{7,23},{8,24},{9,... | collective-permute-start | bytes 940040 | tf_op jit(solution)/shard_map/ppermute | solution.py:431
  31.5 23.6 %collective-permute-start.6 = (bf16[1,24,6528]{2,1,0:T(8,128)(2,1)S(1)}, bf16[1,24,6528]{2,1,0:T(8,128)(2,1)S(1)}, u32[]{:S(2)}, u32[]{:S(2)}) collective-permute-start(bf16[1,24,6528]{2,1,0:T(8,128)(2,1)S(1)} %broadcast_add_fusion.5), channel_id=1, source_target_pairs={{0,24},{1,25},{2,26},{3,27},{4,28},{5,29},{6,30},{7,31},{8,16},{9,... | collective-permute-start | bytes 940040 | tf_op jit(solution)/shard_map/ppermute | solution.py:431
  32.7 24.6 %collective-permute-start.7 = (bf16[4,24,3456]{2,1,0:T(8,128)(2,1)S(1)}, bf16[4,24,3456]{2,1,0:T(8,128)(2,1)}, u32[]{:S(2)}, u32[]{:S(2)}) collective-permute-start(bf16[4,24,3456]{2,1,0:T(8,128)(2,1)S(1)} %pad_maximum_fusion.1.refs_1_), channel_id=1, source_target_pairs={{0,4},{1,5},{2,6},{3,7},{4,0},{5,1},{6,2},{7,3},{8,12},{9,13},{10,... | collective-permute-start | bytes 1990664 | tf_op jit(solution)/shard_map/ppermute | solution.py:431
  58.3 7.2 %collective-permute-start.8 = (bf16[2,24,3456]{2,1,0:T(8,128)(2,1)S(1)}, bf16[2,24,3456]{2,1,0:T(8,128)(2,1)S(1)}, u32[]{:S(2)}, u32[]{:S(2)}) collective-permute-start(bf16[2,24,3456]{2,1,0:T(8,128)(2,1)S(1)} %slice_add_fusion.3), channel_id=1, source_target_pairs={{0,4},{1,5},{2,6},{3,7},{4,0},{5,1},{6,2},{7,3},{8,12},{9,13},{10,... | collective-permute-start | bytes 995336 | tf_op jit(solution)/shard_map/ppermute | solution.py:431
  59.9 9.6 %collective-permute-start.9 = (bf16[2,24,3456]{2,1,0:T(8,128)(2,1)S(1)}, bf16[2,24,3456]{2,1,0:T(8,128)(2,1)}, u32[]{:S(2)}, u32[]{:S(2)}) collective-permute-start(bf16[2,24,3456]{2,1,0:T(8,128)(2,1)S(1)} %slice_add_fusion.2), channel_id=1, source_target_pairs={{0,2},{1,3},{2,0},{3,1},{4,6},{5,7},{6,4},{7,5},{8,10},{9,11},{10,... | collective-permute-start | bytes 995336 | tf_op jit(solution)/shard_map/ppermute | solution.py:431
  72.4 21.5 %collective-permute-start.10 = (bf16[4,24,6528]{2,1,0:T(8,128)(2,1)S(1)}, bf16[4,24,6528]{2,1,0:T(8,128)(2,1)S(1)}, u32[]{:S(2)}, u32[]{:S(2)}) collective-permute-start(bf16[4,24,6528]{2,1,0:T(8,128)(2,1)S(1)} %pad_maximum_fusion.refs_1_), channel_id=1, source_target_pairs={{0,2},{1,3},{2,0},{3,1},{4,6},{5,7},{6,4},{7,5},{8,10},{9,11},{10,... | collective-permute-start | bytes 3760136 | tf_op jit(solution)/shard_map/ppermute | solution.py:431
  73.0 2.1 collective-permute-start.11
  73.0 6.0 %collective-permute-start.12 = (bf16[4,24,3456]{2,1,0:T(8,128)(2,1)}, bf16[4,24,3456]{2,1,0:T(8,128)(2,1)}, u32[]{:S(2)}, u32[]{:S(2)}) collective-permute-start(bf16[4,24,3456]{2,1,0:T(8,128)(2,1)} %collective-permute-done.4.refs_2_), channel_id=1, source_target_pairs={{0,1},{1,0},{2,3},{3,2},{4,5},{5,4},{6,7},{7,6},{8,9},{9,8},{10,11... | collective-permute-start | bytes 1990664 | tf_op jit(solution)/shard_map/ppermute | solution.py:431
  73.6 5.8 %collective-permute-start.13 = (bf16[4,24,3456]{2,1,0:T(8,128)(2,1)}, bf16[4,24,3456]{2,1,0:T(8,128)(2,1)}, u32[]{:S(2)}, u32[]{:S(2)}) collective-permute-start(bf16[4,24,3456]{2,1,0:T(8,128)(2,1)} %collective-permute-done.7.refs_3_), channel_id=1, source_target_pairs={{0,1},{1,0},{2,3},{3,2},{4,5},{5,4},{6,7},{7,6},{8,9},{9,8},{10,11... | collective-permute-start | bytes 1990664 | tf_op jit(solution)/shard_map/ppermute | solution.py:431
  74.2 5.4 %collective-permute-start.14 = (bf16[2,24,3456]{2,1,0:T(8,128)(2,1)S(1)}, bf16[2,24,3456]{2,1,0:T(8,128)(2,1)}, u32[]{:S(2)}, u32[]{:S(2)}) collective-permute-start(bf16[2,24,3456]{2,1,0:T(8,128)(2,1)S(1)} %collective-permute-done.8.refs_4_), channel_id=1, source_target_pairs={{0,1},{1,0},{2,3},{3,2},{4,5},{5,4},{6,7},{7,6},{8,9},{9,8},{10,11... | collective-permute-start | bytes 995336 | tf_op jit(solution)/shard_map/ppermute | solution.py:431
  75.1 4.6 %collective-permute-start.15 = (bf16[2,24,3456]{2,1,0:T(8,128)(2,1)}, bf16[2,24,3456]{2,1,0:T(8,128)(2,1)}, u32[]{:S(2)}, u32[]{:S(2)}) collective-permute-start(bf16[2,24,3456]{2,1,0:T(8,128)(2,1)} %collective-permute-done.9.refs_5_), channel_id=1, source_target_pairs={{0,1},{1,0},{2,3},{3,2},{4,5},{5,4},{6,7},{7,6},{8,9},{9,8},{10,11... | collective-permute-start | bytes 995336 | tf_op jit(solution)/shard_map/ppermute | solution.py:431
  79.0 50.7 %collective-permute-start.19 = (bf16[4,24,6528]{2,1,0:T(8,128)(2,1)S(1)}, bf16[4,24,6528]{2,1,0:T(8,128)(2,1)}, u32[]{:S(2)}, u32[]{:S(2)}) collective-permute-start(bf16[4,24,6528]{2,1,0:T(8,128)(2,1)S(1)} %pad_maximum_fusion.refs_1_), channel_id=1, source_target_pairs={{0,1},{1,0},{2,3},{3,2},{4,5},{5,4},{6,7},{7,6},{8,9},{9,8},{10,11... | collective-permute-start | bytes 3760136 | tf_op jit(solution)/shard_map/ppermute | solution.py:431
  79.4 30.5 %collective-permute-start.16 = (bf16[4,24,6528]{2,1,0:T(8,128)(2,1)S(1)}, bf16[4,24,6528]{2,1,0:T(8,128)(2,1)}, u32[]{:S(2)}, u32[]{:S(2)}) collective-permute-start(bf16[4,24,6528]{2,1,0:T(8,128)(2,1)S(1)} %pad_maximum_fusion.refs_1_), channel_id=1, source_target_pairs={{0,4},{1,5},{2,6},{3,7},{4,0},{5,1},{6,2},{7,3},{8,12},{9,13},{10,... | collective-permute-start | bytes 3760136 | tf_op jit(solution)/shard_map/ppermute | solution.py:431
  93.9 32.0 %copy-start.2 = (bf16[4,24,6528]{2,1,0:T(8,128)(2,1)}, bf16[4,24,6528]{2,1,0:T(8,128)(2,1)S(1)}, u32[]{:S(2)}) copy-start(bf16[4,24,6528]{2,1,0:T(8,128)(2,1)S(1)} %collective-permute-done.10.refs_2_) | copy-start | bytes 3760132
  93.9 18.7 %copy-start.18 = (bf16[2,24,6528]{2,1,0:T(8,128)(2,1)}, bf16[2,24,6528]{2,1,0:T(8,128)(2,1)S(1)}, u32[]{:S(2)}) copy-start(bf16[2,24,6528]{2,1,0:T(8,128)(2,1)S(1)} %slice_add_fusion.1.refs_0_) | copy-start | bytes 1880068
  93.9 32.5 %collective-permute-start.17 = (bf16[2,24,6528]{2,1,0:T(8,128)(2,1)S(1)}, bf16[2,24,6528]{2,1,0:T(8,128)(2,1)S(1)}, u32[]{:S(2)}, u32[]{:S(2)}) collective-permute-start(bf16[2,24,6528]{2,1,0:T(8,128)(2,1)S(1)} %slice_add_fusion.1.refs_0_), channel_id=1, source_target_pairs={{0,4},{1,5},{2,6},{3,7},{4,0},{5,1},{6,2},{7,3},{8,12},{9,13},{10,... | collective-permute-start | bytes 1880072 | tf_op jit(solution)/shard_map/ppermute | solution.py:431
  111.0 15.7 %collective-permute-start.18 = (bf16[2,24,6528]{2,1,0:T(8,128)(2,1)S(1)}, bf16[2,24,6528]{2,1,0:T(8,128)(2,1)S(1)}, u32[]{:S(2)}, u32[]{:S(2)}) collective-permute-start(bf16[2,24,6528]{2,1,0:T(8,128)(2,1)S(1)} %slice_add_fusion.refs_1_), channel_id=1, source_target_pairs={{0,2},{1,3},{2,0},{3,1},{4,6},{5,7},{6,4},{7,5},{8,10},{9,11},{10,... | collective-permute-start | bytes 1880072 | tf_op jit(solution)/shard_map/ppermute | solution.py:431
  125.9 4.1 %collective-permute-start.20 = (bf16[4,24,6528]{2,1,0:T(8,128)(2,1)S(1)}, bf16[4,24,6528]{2,1,0:T(8,128)(2,1)}, u32[]{:S(2)}, u32[]{:S(2)}) collective-permute-start(bf16[4,24,6528]{2,1,0:T(8,128)(2,1)S(1)} %collective-permute-done.10.refs_2_), channel_id=1, source_target_pairs={{0,1},{1,0},{2,3},{3,2},{4,5},{5,4},{6,7},{7,6},{8,9},{9,8},{10,11... | collective-permute-start | bytes 3760136 | tf_op jit(solution)/shard_map/ppermute | solution.py:431
  126.0 5.9 %collective-permute-start.21 = (bf16[4,24,6528]{2,1,0:T(8,128)(2,1)}, bf16[4,24,6528]{2,1,0:T(8,128)(2,1)}, u32[]{:S(2)}, u32[]{:S(2)}) collective-permute-start(bf16[4,24,6528]{2,1,0:T(8,128)(2,1)} %collective-permute-done.16.refs_3_), channel_id=1, source_target_pairs={{0,1},{1,0},{2,3},{3,2},{4,5},{5,4},{6,7},{7,6},{8,9},{9,8},{10,11... | collective-permute-start | bytes 3760136 | tf_op jit(solution)/shard_map/ppermute | solution.py:431
  126.6 5.3 %collective-permute-start.22 = (bf16[2,24,6528]{2,1,0:T(8,128)(2,1)S(1)}, bf16[2,24,6528]{2,1,0:T(8,128)(2,1)}, u32[]{:S(2)}, u32[]{:S(2)}) collective-permute-start(bf16[2,24,6528]{2,1,0:T(8,128)(2,1)S(1)} %broadcast_add_fusion.1.refs_4_), channel_id=1, source_target_pairs={{0,1},{1,0},{2,3},{3,2},{4,5},{5,4},{6,7},{7,6},{8,9},{9,8},{10,11... | collective-permute-start | bytes 1880072 | tf_op jit(solution)/shard_map/ppermute | solution.py:431
  127.6 5.2 %collective-permute-start.23 = (bf16[2,24,6528]{2,1,0:T(8,128)(2,1)}, bf16[2,24,6528]{2,1,0:T(8,128)(2,1)}, u32[]{:S(2)}, u32[]{:S(2)}) collective-permute-start(bf16[2,24,6528]{2,1,0:T(8,128)(2,1)} %broadcast_add_fusion.refs_5_), channel_id=1, source_target_pairs={{0,1},{1,0},{2,3},{3,2},{4,5},{5,4},{6,7},{7,6},{8,9},{9,8},{10,11... | collective-permute-start | bytes 1880072 | tf_op jit(solution)/shard_map/ppermute | solution.py:431
  160.8 12.0 %collective-permute-start.24 = (bf16[4,4,48,768]{3,2,1,0:T(8,128)(2,1)}, bf16[4,4,48,768]{3,2,1,0:T(8,128)(2,1)S(1)}, u32[]{:S(2)}, u32[]{:S(2)}) collective-permute-start(bf16[4,4,48,768]{3,2,1,0:T(8,128)(2,1)} %get-tuple-element.81), channel_id=1, source_target_pairs={{0,1},{1,0},{2,3},{3,2},{4,5},{5,4},{6,7},{7,6},{8,9},{9,8},{10,11... | collective-permute-start | bytes 3538952 | tf_op jit(solution)/shard_map/ppermute | solution.py:431
  172.8 57.6 %copy-start.11 = (bf16[4,4,48,768]{3,2,1,0:T(8,128)(2,1)}, bf16[4,4,48,768]{3,2,1,0:T(8,128)(2,1)S(1)}, u32[]{:S(2)}) copy-start(bf16[4,4,48,768]{3,2,1,0:T(8,128)(2,1)S(1)} %collective-permute-done.24) | copy-start | bytes 3538948
  173.7 14.3 %copy-start.29 = (bf16[2,48,768]{2,1,0:T(8,128)(2,1)S(1)}, bf16[2,48,768]{2,1,0:T(8,128)(2,1)}, u32[]{:S(2)}) copy-start(bf16[2,48,768]{2,1,0:T(8,128)(2,1)} %get-tuple-element.92.refs_1_) | copy-start | bytes 442372
  173.7 15.0 %copy-start.28 = (bf16[2,48,768]{2,1,0:T(8,128)(2,1)S(1)}, bf16[2,48,768]{2,1,0:T(8,128)(2,1)}, u32[]{:S(2)}) copy-start(bf16[2,48,768]{2,1,0:T(8,128)(2,1)} %get-tuple-element.91.refs_0_) | copy-start | bytes 442372
  187.6 9.3 %collective-permute-start.25 = (bf16[4,4,24,4992]{3,2,1,0:T(8,128)(2,1)}, bf16[4,4,24,4992]{3,2,1,0:T(8,128)(2,1)}, u32[]{:S(2)}, u32[]{:S(2)}) collective-permute-start(bf16[4,4,24,4992]{3,2,1,0:T(8,128)(2,1)} %get-tuple-element.88), channel_id=1, source_target_pairs={{0,1},{1,0},{2,3},{3,2},{4,5},{5,4},{6,7},{7,6},{8,9},{9,8},{10,11... | collective-permute-start | bytes 11501576 | tf_op jit(solution)/shard_map/ppermute | solution.py:431
  188.0 5.9 %collective-permute-start.27 = (bf16[2,48,768]{2,1,0:T(8,128)(2,1)S(1)}, bf16[2,48,768]{2,1,0:T(8,128)(2,1)S(1)}, u32[]{:S(2)}, u32[]{:S(2)}) collective-permute-start(bf16[2,48,768]{2,1,0:T(8,128)(2,1)S(1)} %copy-done.29), channel_id=1, source_target_pairs={{0,2},{1,3},{2,0},{3,1},{4,6},{5,7},{6,4},{7,5},{8,10},{9,11},{10,... | collective-permute-start | bytes 442376 | tf_op jit(solution)/shard_map/ppermute | solution.py:431
  188.8 5.6 %collective-permute-start.26 = (bf16[2,48,768]{2,1,0:T(8,128)(2,1)S(1)}, bf16[2,48,768]{2,1,0:T(8,128)(2,1)S(1)}, u32[]{:S(2)}, u32[]{:S(2)}) collective-permute-start(bf16[2,48,768]{2,1,0:T(8,128)(2,1)S(1)} %copy-done.28), channel_id=1, source_target_pairs={{0,4},{1,5},{2,6},{3,7},{4,0},{5,1},{6,2},{7,3},{8,12},{9,13},{10,... | collective-permute-start | bytes 442376 | tf_op jit(solution)/shard_map/ppermute | solution.py:431
  195.4 23.6 %collective-permute-start.49 = (bf16[4,48,768]{2,1,0:T(8,128)(2,1)}, bf16[4,48,768]{2,1,0:T(8,128)(2,1)S(1)}, u32[]{:S(2)}, u32[]{:S(2)}) collective-permute-start(bf16[4,48,768]{2,1,0:T(8,128)(2,1)} %get-tuple-element.114.refs_1_), channel_id=1, source_target_pairs={{0,4},{1,5},{2,6},{3,7},{4,0},{5,1},{6,2},{7,3},{8,12},{9,13},{10,... | collective-permute-start | bytes 884744 | tf_op jit(solution)/shard_map/ppermute | solution.py:431
  195.6 23.4 %collective-permute-start.48 = (bf16[4,48,768]{2,1,0:T(8,128)(2,1)}, bf16[4,48,768]{2,1,0:T(8,128)(2,1)}, u32[]{:S(2)}, u32[]{:S(2)}) collective-permute-start(bf16[4,48,768]{2,1,0:T(8,128)(2,1)} %get-tuple-element.113.refs_0_), channel_id=1, source_target_pairs={{0,2},{1,3},{2,0},{3,1},{4,6},{5,7},{6,4},{7,5},{8,10},{9,11},{10,... | collective-permute-start | bytes 884744 | tf_op jit(solution)/shard_map/ppermute | solution.py:431
  199.4 14.5 %copy-start.19 = (bf16[2,24,4992]{2,1,0:T(8,128)(2,1)}, bf16[2,24,4992]{2,1,0:T(8,128)(2,1)S(1)}, u32[]{:S(2)}) copy-start(bf16[2,24,4992]{2,1,0:T(8,128)(2,1)S(1)} %get-tuple-element.108.refs_1_) | copy-start | bytes 1437700
  199.4 14.5 %collective-permute-start.37 = (bf16[2,24,4992]{2,1,0:T(8,128)(2,1)S(1)}, bf16[2,24,4992]{2,1,0:T(8,128)(2,1)S(1)}, u32[]{:S(2)}, u32[]{:S(2)}) collective-permute-start(bf16[2,24,4992]{2,1,0:T(8,128)(2,1)S(1)} %get-tuple-element.108.refs_1_), channel_id=1, source_target_pairs={{0,2},{1,3},{2,0},{3,1},{4,6},{5,7},{6,4},{7,5},{8,10},{9,11},{10,... | collective-permute-start | bytes 1437704 | tf_op jit(solution)/shard_map/ppermute | solution.py:431
  200.1 13.8 %collective-permute-start.36 = (bf16[2,24,4992]{2,1,0:T(8,128)(2,1)}, bf16[2,24,4992]{2,1,0:T(8,128)(2,1)S(1)}, u32[]{:S(2)}, u32[]{:S(2)}) collective-permute-start(bf16[2,24,4992]{2,1,0:T(8,128)(2,1)} %get-tuple-element.107.refs_0_), channel_id=1, source_target_pairs={{0,4},{1,5},{2,6},{3,7},{4,0},{5,1},{6,2},{7,3},{8,12},{9,13},{10,... | collective-permute-start | bytes 1437704 | tf_op jit(solution)/shard_map/ppermute | solution.py:431
  216.0 21.1 %collective-permute-start.39 = (bf16[4,24,4992]{2,1,0:T(8,128)(2,1)S(1)}, bf16[4,24,4992]{2,1,0:T(8,128)(2,1)S(1)}, u32[]{:S(2)}, u32[]{:S(2)}) collective-permute-start(bf16[4,24,4992]{2,1,0:T(8,128)(2,1)S(1)} %get-tuple-element.110), channel_id=1, source_target_pairs={{0,4},{1,5},{2,6},{3,7},{4,0},{5,1},{6,2},{7,3},{8,12},{9,13},{10,... | collective-permute-start | bytes 2875400 | tf_op jit(solution)/shard_map/ppermute | solution.py:431
  217.6 20.6 %collective-permute-start.38 = (bf16[4,24,4992]{2,1,0:T(8,128)(2,1)S(1)}, bf16[4,24,4992]{2,1,0:T(8,128)(2,1)S(1)}, u32[]{:S(2)}, u32[]{:S(2)}) collective-permute-start(bf16[4,24,4992]{2,1,0:T(8,128)(2,1)S(1)} %get-tuple-element.109), channel_id=1, source_target_pairs={{0,2},{1,3},{2,0},{3,1},{4,6},{5,7},{6,4},{7,5},{8,10},{9,11},{10,... | collective-permute-start | bytes 2875400 | tf_op jit(solution)/shard_map/ppermute | solution.py:431
  218.9 2.9 collective-permute-start.42
  219.0 22.5 %copy-start.22 = (bf16[4,48,768]{2,1,0:T(8,128)(2,1)}, bf16[4,48,768]{2,1,0:T(8,128)(2,1)S(1)}, u32[]{:S(2)}) copy-start(bf16[4,48,768]{2,1,0:T(8,128)(2,1)S(1)} %collective-permute-done.49) | copy-start | bytes 884740
  220.1 10.4 %collective-permute-start.50 = (bf16[2,48,768]{2,1,0:T(8,128)(2,1)S(1)}, bf16[2,48,768]{2,1,0:T(8,128)(2,1)S(1)}, u32[]{:S(2)}, u32[]{:S(2)}) collective-permute-start(bf16[2,48,768]{2,1,0:T(8,128)(2,1)S(1)} %fusion.33), channel_id=1, source_target_pairs={{0,16},{1,17},{2,18},{3,19},{4,20},{5,21},{6,22},{7,23},{8,24},{9,... | collective-permute-start | bytes 442376 | tf_op jit(solution)/shard_map/ppermute | solution.py:431
  221.8 42.4 %collective-permute-start.43 = (f32[8,1792]{1,0:T(8,128)S(1)}, f32[8,1792]{1,0:T(8,128)}, u32[]{:S(2)}, u32[]{:S(2)}) collective-permute-start(f32[8,1792]{1,0:T(8,128)S(1)} %select_add_fusion), channel_id=1, source_target_pairs={{0,8},{1,9},{2,10},{3,11},{4,12},{5,13},{6,14},{7,15},{8,0},{9,1},... | collective-permute-start | bytes 172040 | tf_op jit(solution)/shard_map/ppermute | solution.py:431
  232.1 36.2 %collective-permute-start.51 = (bf16[1,48,768]{2,1,0:T(8,128)(2,1)}, bf16[1,48,768]{2,1,0:T(8,128)(2,1)S(1)}, u32[]{:S(2)}, u32[]{:S(2)}) collective-permute-start(bf16[1,48,768]{2,1,0:T(8,128)(2,1)} %fusion.40), channel_id=1, source_target_pairs={{0,8},{1,9},{2,10},{3,11},{4,12},{5,13},{6,14},{7,15},{8,0},{9,1},... | collective-permute-start | bytes 221192 | tf_op jit(solution)/shard_map/ppermute | solution.py:431
  237.0 23.6 %copy-start.12 = (bf16[4,24,4992]{2,1,0:T(8,128)(2,1)}, bf16[4,24,4992]{2,1,0:T(8,128)(2,1)S(1)}, u32[]{:S(2)}) copy-start(bf16[4,24,4992]{2,1,0:T(8,128)(2,1)S(1)} %collective-permute-done.39) | copy-start | bytes 2875396
  239.8 20.8 %collective-permute-start.40 = (bf16[2,24,4992]{2,1,0:T(8,128)(2,1)S(1)}, bf16[2,24,4992]{2,1,0:T(8,128)(2,1)}, u32[]{:S(2)}, u32[]{:S(2)}) collective-permute-start(bf16[2,24,4992]{2,1,0:T(8,128)(2,1)S(1)} %fusion.7), channel_id=1, source_target_pairs={{0,16},{1,17},{2,18},{3,19},{4,20},{5,21},{6,22},{7,23},{8,24},{9,... | collective-permute-start | bytes 1437704 | tf_op jit(solution)/shard_map/ppermute | solution.py:431
  241.5 20.5 %copy-start.7 = (bf16[32,2,24,768]{3,2,1,0:T(8,128)(2,1)S(1)}, bf16[32,2,24,768]{3,2,1,0:T(8,128)(2,1)}, u32[]{:S(2)}) copy-start(bf16[32,2,24,768]{3,2,1,0:T(8,128)(2,1)} %get-tuple-element.79) | copy-start | bytes 7077892
  241.5 20.5 %copy-start.9 = (f32[128,768]{1,0:T(8,128)S(1)}, f32[128,768]{1,0:T(8,128)}, u32[]{:S(2)}) copy-start(f32[128,768]{1,0:T(8,128)} %convolution_add_fusion.1.refs_0_.refs_4_) | copy-start | bytes 1179652
  252.2 19.3 %collective-permute-start.28 = (bf16[4,4,24,3456]{3,2,1,0:T(8,128)(2,1)}, bf16[4,4,24,3456]{3,2,1,0:T(8,128)(2,1)S(1)}, u32[]{:S(2)}, u32[]{:S(2)}) collective-permute-start(bf16[4,4,24,3456]{3,2,1,0:T(8,128)(2,1)} %get-tuple-element.99), channel_id=1, source_target_pairs={{0,1},{1,0},{2,3},{3,2},{4,5},{5,4},{6,7},{7,6},{8,9},{9,8},{10,11... | collective-permute-start | bytes 7962632 | tf_op jit(solution)/shard_map/ppermute | solution.py:431
  261.9 8.0 %collective-permute-start.41 = (bf16[1,24,4992]{2,1,0:T(8,128)(2,1)S(1)}, bf16[1,24,4992]{2,1,0:T(8,128)(2,1)S(1)}, u32[]{:S(2)}, u32[]{:S(2)}) collective-permute-start(bf16[1,24,4992]{2,1,0:T(8,128)(2,1)S(1)} %fusion.14), channel_id=1, source_target_pairs={{0,8},{1,9},{2,10},{3,11},{4,12},{5,13},{6,14},{7,15},{8,0},{9,1},... | collective-permute-start | bytes 718856 | tf_op jit(solution)/shard_map/ppermute | solution.py:431
  265.2 40.0 %collective-permute-start.44 = (f32[8,1792]{1,0:T(8,128)S(1)}, f32[8,1792]{1,0:T(8,128)}, u32[]{:S(2)}, u32[]{:S(2)}) collective-permute-start(f32[8,1792]{1,0:T(8,128)S(1)} %add.503), channel_id=1, source_target_pairs={{0,16},{1,17},{2,18},{3,19},{4,20},{5,21},{6,22},{7,23},{8,24},{9,... | collective-permute-start | bytes 172040 | tf_op jit(solution)/shard_map/ppermute | solution.py:431
  271.4 26.5 %copy-start.4 = (bf16[4,4,24,3456]{3,2,1,0:T(8,128)(2,1)}, bf16[4,4,24,3456]{3,2,1,0:T(8,128)(2,1)S(1)}, u32[]{:S(2)}) copy-start(bf16[4,4,24,3456]{3,2,1,0:T(8,128)(2,1)S(1)} %collective-permute-done.28) | copy-start | bytes 7962628
  271.6 9.2 %collective-permute-start.30 = (bf16[2,24,3456]{2,1,0:T(8,128)(2,1)S(1)}, bf16[2,24,3456]{2,1,0:T(8,128)(2,1)S(1)}, u32[]{:S(2)}, u32[]{:S(2)}) collective-permute-start(bf16[2,24,3456]{2,1,0:T(8,128)(2,1)S(1)} %get-tuple-element.101), channel_id=1, source_target_pairs={{0,2},{1,3},{2,0},{3,1},{4,6},{5,7},{6,4},{7,5},{8,10},{9,11},{10,... | collective-permute-start | bytes 995336 | tf_op jit(solution)/shard_map/ppermute | solution.py:431
  273.0 8.9 %collective-permute-start.29 = (bf16[2,24,3456]{2,1,0:T(8,128)(2,1)S(1)}, bf16[2,24,3456]{2,1,0:T(8,128)(2,1)S(1)}, u32[]{:S(2)}, u32[]{:S(2)}) collective-permute-start(bf16[2,24,3456]{2,1,0:T(8,128)(2,1)S(1)} %get-tuple-element.100), channel_id=1, source_target_pairs={{0,4},{1,5},{2,6},{3,7},{4,0},{5,1},{6,2},{7,3},{8,12},{9,13},{10,... | collective-permute-start | bytes 995336 | tf_op jit(solution)/shard_map/ppermute | solution.py:431
  282.3 15.1 %collective-permute-start.32 = (bf16[4,24,3456]{2,1,0:T(8,128)(2,1)S(1)}, bf16[4,24,3456]{2,1,0:T(8,128)(2,1)S(1)}, u32[]{:S(2)}, u32[]{:S(2)}) collective-permute-start(bf16[4,24,3456]{2,1,0:T(8,128)(2,1)S(1)} %get-tuple-element.103), channel_id=1, source_target_pairs={{0,4},{1,5},{2,6},{3,7},{4,0},{5,1},{6,2},{7,3},{8,12},{9,13},{10,... | collective-permute-start | bytes 1990664 | tf_op jit(solution)/shard_map/ppermute | solution.py:431
  283.1 14.8 %collective-permute-start.31 = (bf16[4,24,3456]{2,1,0:T(8,128)(2,1)S(1)}, bf16[4,24,3456]{2,1,0:T(8,128)(2,1)S(1)}, u32[]{:S(2)}, u32[]{:S(2)}) collective-permute-start(bf16[4,24,3456]{2,1,0:T(8,128)(2,1)S(1)} %get-tuple-element.102), channel_id=1, source_target_pairs={{0,2},{1,3},{2,0},{3,1},{4,6},{5,7},{6,4},{7,5},{8,10},{9,11},{10,... | collective-permute-start | bytes 1990664 | tf_op jit(solution)/shard_map/ppermute | solution.py:431
  300.1 14.5 %collective-permute-start.35 = (bf16[1,24,3456]{2,1,0:T(8,128)(2,1)}, bf16[1,24,3456]{2,1,0:T(8,128)(2,1)}, u32[]{:S(2)}, u32[]{:S(2)}) collective-permute-start(bf16[1,24,3456]{2,1,0:T(8,128)(2,1)} %get-tuple-element.106), channel_id=1, source_target_pairs={{0,24},{1,25},{2,26},{3,27},{4,28},{5,29},{6,30},{7,31},{8,16},{9,... | collective-permute-start | bytes 497672 | tf_op jit(solution)/shard_map/ppermute | solution.py:431
  301.9 12.7 %collective-permute-start.34 = (bf16[1,24,3456]{2,1,0:T(8,128)(2,1)}, bf16[1,24,3456]{2,1,0:T(8,128)(2,1)}, u32[]{:S(2)}, u32[]{:S(2)}) collective-permute-start(bf16[1,24,3456]{2,1,0:T(8,128)(2,1)} %get-tuple-element.105), channel_id=1, source_target_pairs={{0,16},{1,17},{2,18},{3,19},{4,20},{5,21},{6,22},{7,23},{8,24},{9,... | collective-permute-start | bytes 497672 | tf_op jit(solution)/shard_map/ppermute | solution.py:431
  302.2 12.5 %collective-permute-start.33 = (bf16[1,24,3456]{2,1,0:T(8,128)(2,1)}, bf16[1,24,3456]{2,1,0:T(8,128)(2,1)}, u32[]{:S(2)}, u32[]{:S(2)}) collective-permute-start(bf16[1,24,3456]{2,1,0:T(8,128)(2,1)} %get-tuple-element.104), channel_id=1, source_target_pairs={{0,8},{1,9},{2,10},{3,11},{4,12},{5,13},{6,14},{7,15},{8,0},{9,1},... | collective-permute-start | bytes 497672 | tf_op jit(solution)/shard_map/ppermute | solution.py:431
  306.0 4.2 %collective-permute-start.45 = (f32[8,1792]{1,0:T(8,128)S(1)}, f32[8,1792]{1,0:T(8,128)S(1)}, u32[]{:S(2)}, u32[]{:S(2)}) collective-permute-start(f32[8,1792]{1,0:T(8,128)S(1)} %add_add_fusion), channel_id=1, source_target_pairs={{0,2},{1,3},{2,0},{3,1},{4,6},{5,7},{6,4},{7,5},{8,10},{9,11},{10,... | collective-permute-start | bytes 172040 | tf_op jit(solution)/shard_map/ppermute | solution.py:431
  310.3 4.2 %collective-permute-start.46 = (f32[8,1792]{1,0:T(8,128)S(1)}, f32[8,1792]{1,0:T(8,128)S(1)}, u32[]{:S(2)}, u32[]{:S(2)}) collective-permute-start(f32[8,1792]{1,0:T(8,128)S(1)} %add.507), channel_id=1, source_target_pairs={{0,4},{1,5},{2,6},{3,7},{4,0},{5,1},{6,2},{7,3},{8,12},{9,13},{10,... | collective-permute-start | bytes 172040 | tf_op jit(solution)/shard_map/ppermute | solution.py:431
  314.5 3.2 %collective-permute-start.47 = (f32[8,1792]{1,0:T(8,128)S(1)}, f32[8,1792]{1,0:T(8,128)S(1)}, u32[]{:S(2)}, u32[]{:S(2)}) collective-permute-start(f32[8,1792]{1,0:T(8,128)S(1)} %add.508), channel_id=1, source_target_pairs={{0,1},{1,0},{2,3},{3,2},{4,5},{5,4},{6,7},{7,6},{8,9},{9,8},{10,11... | collective-permute-start | bytes 172040 | tf_op jit(solution)/shard_map/ppermute | solution.py:431
  (22 other events, 132.0 us)
